TPU v7x, 32 devices: a whole 2x2x4 slice. The times are simulated.
32 devices in a mesh: dp: 4 (over y, core), expert: 2 (over x), narrow: 4 (over z).
Axes of the slice: x: 2, y: 2, z: 4, core: 2. Of those that a mesh axis runs over, the one named last changes fastest.
Arguments:
- inputs: float32 [16384, 512], P('dp'), may hold values from -6 to 6
- seg_ids: int32 [16, 1024], P('dp'), may hold values from 0 to 7, never falling along the last dimension, each value on 1 to 256 neighbouring positions
- chosen: int32 [16384, 2], P('dp'), may hold values from 0 to 7, all different within a row
- gain_one: float32 [512], replicated, may hold values from 0.5 to 1.5
- shift_one: float32 [512], replicated, may hold values from -1.2 to 1.2
- query_w: bfloat16 [8, 512, 64], P('expert', None, 'narrow'), may hold values from -0.25 to 0.25
- query_b: float32 [8, 64], P('expert', 'narrow'), may hold values from -1.2 to 1.2
- key_w: bfloat16 [512, 64], P(None, 'narrow'), may hold values from -0.25 to 0.25
- value_w: bfloat16 [512, 64], P(None, 'narrow'), may hold values from -0.25 to 0.25
- value_b: float32 [64], P('narrow'), may hold values from -1.2 to 1.2
- out_w: bfloat16 [8, 64, 512], P('expert', 'narrow'), may hold values from -2 to 2
- out_b: float32 [512], replicated, may hold values from -1.2 to 1.2
- router_w: bfloat16 [512, 8], replicated, may hold values from -0.25 to 0.25
- router_b: float32 [8], replicated, may hold values from -0.6 to 0.6
- gain_two: float32 [512], replicated, may hold values from 0.5 to 1.5
- shift_two: float32 [512], replicated, may hold values from -1.2 to 1.2
- up_w: bfloat16 [512, 2048], P(None, 'narrow'), may hold values from -0.25 to 0.25
- up_b: float32 [2048], P('narrow'), may hold values from -1.2 to 1.2
- down_w: bfloat16 [2048, 512], P('narrow'), may hold values from -0.125 to 0.125
- down_b: float32 [512], replicated, may hold values from -1.2 to 1.2
- cotangent: bfloat16 [16384, 512], P(('dp', 'expert'), 'narrow'), may hold values from -6 to 6
Outputs:
- output: float32 [16384, 512], P(('dp', 'expert'), 'narrow')
- input_grad: float32 [16384, 512], P(('dp', 'expert', 'narrow'))
- gain_one_grad: float32 [512], replicated
- shift_one_grad: float32 [512], replicated
- query_w_grad: float32 [8, 512, 64], P('expert', None, 'narrow')
- query_b_grad: float32 [8, 64], P('expert', 'narrow')
- key_w_grad: float32 [512, 64], P(None, 'narrow')
- value_w_grad: float32 [512, 64], P(None, 'narrow')
- value_b_grad: float32 [64], P('narrow')
- out_w_grad: float32 [8, 64, 512], P('expert', 'narrow')
- out_b_grad: float32 [512], replicated
- router_w_grad: float32 [512, 8], replicated
- router_b_grad: float32 [8], replicated
- gain_two_grad: float32 [512], replicated
- shift_two_grad: float32 [512], replicated
- up_w_grad: float32 [512, 2048], P(None, 'narrow')
- up_b_grad: float32 [2048], P('narrow')
- down_w_grad: float32 [2048, 512], P('narrow')
- down_b_grad: float32 [512], replicated
Inputs may be any that keep to these rules, and one draw needn't show every extreme that they name: `chosen`: each token names two different experts. `seg_ids`: sentence numbers never fall along a row; a sentence has 1 to 256 tokens.
All inputs are finite; a program needn't handle non-finite values.
Results may differ from a plain program's by a relative error of at most 0.02.
Values may be sent and summed in bfloat16 or wider, within the bound.
A program may use at most 320 MiB of HBM per device.

v0:
```python
import math

import jax
import jax.numpy as jnp
from jax import lax
from jax.sharding import PartitionSpec as P

HEAD = 64


epsilon = 1e-05
masked_fill = -1000000000.0
precise = lax.Precision.HIGHEST


def norm_forward(values, scales, shifts):
    average = jnp.mean(values, axis=1, keepdims=True)
    centred = values - average
    inverse = lax.rsqrt(jnp.mean(centred * centred, axis=1, keepdims=True) + epsilon)
    unit = centred * inverse
    return (unit * scales + shifts, unit, inverse)


def norm_backward(grads, unit, inverse, scales):
    scaled = grads * scales
    inner = (
        scaled
        - jnp.mean(scaled, axis=1, keepdims=True)
        - unit * jnp.mean(scaled * unit, axis=1, keepdims=True)
    )
    return (inner * inverse, jnp.sum(grads * unit, axis=0), jnp.sum(grads, axis=0))


def full_scores(query_row, key_row):
    return jnp.einsum("esh,kh->esk", query_row, key_row, preferred_element_type=jnp.float32) * (
        1.0 / math.sqrt(HEAD)
    )


def per_device(
    inputs,
    seg_ids,
    chosen,
    gain_one,
    shift_one,
    query_w,
    query_b,
    key_w,
    value_w,
    value_b,
    out_w,
    out_b,
    router_w,
    router_b,
    gain_two,
    shift_two,
    up_w,
    up_b,
    down_w,
    down_b,
    cotangent,
):
    expert_count = lax.axis_size("expert")
    narrow_count = lax.axis_size("narrow")
    expert_at = lax.axis_index("expert")
    narrow_at = lax.axis_index("narrow")
    local_experts = query_w.shape[0]
    total_experts = router_w.shape[1]
    row_count = seg_ids.shape[0]
    row_len = seg_ids.shape[1]
    tokens_here = inputs.shape[0]
    model_width = inputs.shape[1]
    block_rows = tokens_here // expert_count
    block_start = expert_at * block_rows
    grad_rows = block_rows // narrow_count
    grad_start = block_start + narrow_at * grad_rows
    col_width = model_width // narrow_count
    col_start = narrow_at * col_width
    score_scale = 1.0 / math.sqrt(HEAD)
    normed, unit_one, inverse_one = norm_forward(inputs, gain_one, shift_one)
    rounded = normed.astype(jnp.bfloat16)
    queries = (
        jnp.einsum("td,edh->eth", rounded, query_w, preferred_element_type=jnp.float32)
        + query_b[:, None, :]
    ).astype(jnp.bfloat16)
    key_all = jnp.dot(rounded, key_w, preferred_element_type=jnp.float32).astype(jnp.bfloat16)
    value_all = (jnp.dot(rounded, value_w, preferred_element_type=jnp.float32) + value_b).astype(
        jnp.bfloat16
    )
    logits = jnp.dot(rounded, router_w, preferred_element_type=jnp.float32) + router_b
    onehot = (
        chosen[:, :, None] == jnp.arange(total_experts, dtype=jnp.int32)[None, None, :]
    ).astype(jnp.float32)
    picked = jnp.sum(logits[:, None, :] * onehot, axis=2)
    weights = jax.nn.softmax(picked, axis=1)
    gate_dense = jnp.sum(weights[:, :, None] * onehot, axis=1)
    local_gates = lax.dynamic_slice_in_dim(gate_dense, expert_at * local_experts, local_experts, 1)
    query_full, key_full = (
        lax.all_gather(queries, "narrow", axis=2, tiled=True),
        lax.all_gather(key_all, "narrow", axis=1, tiled=True),
    )
    same_docs = []
    log_totals = []
    mixed_rows = []
    for row_index in range(row_count):
        row_lower = row_index * row_len
        value_row = value_all[row_lower : row_lower + row_len]
        seg_row = seg_ids[row_index]
        same_doc = (seg_row[:, None] == seg_row[None, :])[None]
        scores = full_scores(
            query_full[:, row_lower : row_lower + row_len],
            key_full[row_lower : row_lower + row_len],
        )
        scores = jnp.where(same_doc, scores, masked_fill)
        row_top = jnp.max(scores, axis=2, keepdims=True)
        row_total = jnp.sum(jnp.exp(scores - row_top), axis=2, keepdims=True)
        log_total = row_top + jnp.log(row_total)
        probability = jnp.exp(scores - log_total)
        same_docs.append(same_doc)
        log_totals.append(log_total)
        mixed_rows.append(
            jnp.einsum(
                "esk,kh->esh",
                probability.astype(jnp.bfloat16),
                value_row,
                preferred_element_type=jnp.float32,
            ).astype(jnp.bfloat16)
        )
    mixed = jnp.concatenate(mixed_rows, axis=1)
    projected = jnp.einsum("eth,ehd->etd", mixed, out_w, preferred_element_type=jnp.float32)
    gated = jnp.sum(jnp.transpose(local_gates)[:, :, None] * projected, axis=0)
    attention = (
        lax.psum(gated.astype(jnp.bfloat16), ("expert", "narrow")).astype(jnp.float32) + out_b
    )
    hidden = inputs + attention
    hidden_rows = lax.dynamic_slice_in_dim(hidden, block_start, block_rows, 0)
    second, unit_two, inverse_two = norm_forward(hidden_rows, gain_two, shift_two)
    second_low = second.astype(jnp.bfloat16)
    upper = jnp.dot(second_low, up_w, preferred_element_type=jnp.float32) + up_b
    active_low = jax.nn.gelu(upper).astype(jnp.bfloat16)
    ffn_part = jnp.dot(active_low, down_w, preferred_element_type=jnp.float32)
    ffn_cols = lax.psum_scatter(
        ffn_part.astype(jnp.bfloat16), "narrow", scatter_dimension=1, tiled=True
    ).astype(jnp.float32)
    output = (
        lax.dynamic_slice_in_dim(hidden_rows, col_start, col_width, 1)
        + ffn_cols
        + lax.dynamic_slice_in_dim(down_b, col_start, col_width, 0)
    )
    cot_full = lax.all_gather(cotangent, "narrow", axis=1, tiled=True)
    down_w_grad = jnp.einsum("tf,td->fd", active_low, cot_full, preferred_element_type=jnp.float32)
    down_b_grad = jnp.sum(cot_full.astype(jnp.float32), axis=0)
    act_grad = jnp.einsum("td,fd->tf", cot_full, down_w, preferred_element_type=jnp.float32)
    upper_grad = jax.vjp(jax.nn.gelu, upper)[1](act_grad)[0].astype(jnp.bfloat16)
    up_w_grad = jnp.einsum("td,tf->df", second_low, upper_grad, preferred_element_type=jnp.float32)
    up_b_grad = jnp.sum(upper_grad.astype(jnp.float32), axis=0)
    second_grad = lax.psum(
        jnp.einsum("tf,df->td", upper_grad, up_w, preferred_element_type=jnp.float32).astype(
            jnp.bfloat16
        ),
        "narrow",
    ).astype(jnp.float32)
    back_two, gain_two_part, shift_two_part = norm_backward(
        second_grad, unit_two, inverse_two, gain_two
    )
    hidden_rows_grad = cot_full.astype(jnp.float32) + back_two
    up_w_grad, up_b_grad, down_w_grad, down_b_grad, gain_two_grad, shift_two_grad = lax.psum(
        (up_w_grad, up_b_grad, down_w_grad, down_b_grad, gain_two_part, shift_two_part),
        ("dp", "expert"),
    )
    hidden_grad = lax.all_gather(
        hidden_rows_grad.astype(jnp.bfloat16), "expert", axis=0, tiled=True
    ).astype(hidden_rows_grad.dtype)
    scaled_grad = (jnp.transpose(local_gates)[:, :, None] * hidden_grad[None]).astype(jnp.bfloat16)
    gate_local = jnp.transpose(jnp.sum(hidden_grad[None] * projected, axis=2))
    gate_part = lax.dynamic_update_slice_in_dim(
        jnp.zeros((tokens_here, total_experts), jnp.float32),
        gate_local,
        expert_at * local_experts,
        1,
    )
    gate_grad = lax.psum(gate_part.astype(jnp.bfloat16), ("expert", "narrow")).astype(jnp.float32)
    out_b_grad = jnp.sum(hidden_grad, axis=0)
    out_w_grad = jnp.einsum("eth,etd->ehd", mixed, scaled_grad, preferred_element_type=jnp.float32)
    mixed_grad = jnp.einsum(
        "etd,ehd->eth", scaled_grad, out_w, preferred_element_type=jnp.float32
    ).astype(jnp.bfloat16)
    weight_grad = jnp.sum(gate_grad[:, None, :] * onehot, axis=2)
    picked_grad = weights * (weight_grad - jnp.sum(weights * weight_grad, axis=1, keepdims=True))
    logit_grad = jnp.sum(picked_grad[:, :, None] * onehot, axis=1)
    router_w_grad = jnp.einsum(
        "td,te->de", rounded, logit_grad, precision=precise, preferred_element_type=jnp.float32
    )
    router_b_grad = jnp.sum(logit_grad, axis=0)
    grad_full, value_full = (
        lax.all_gather(mixed_grad, "narrow", axis=2, tiled=True),
        lax.all_gather(value_all, "narrow", axis=1, tiled=True),
    )
    query_grads = []
    key_grads = []
    value_grads = []
    for row_index in range(row_count):
        row_lower = row_index * row_len
        query_row = queries[:, row_lower : row_lower + row_len]
        key_row = key_all[row_lower : row_lower + row_len]
        grad_row = mixed_grad[:, row_lower : row_lower + row_len]
        scores = full_scores(
            query_full[:, row_lower : row_lower + row_len],
            key_full[row_lower : row_lower + row_len],
        )
        probability = jnp.exp(
            jnp.where(same_docs[row_index], scores, masked_fill) - log_totals[row_index]
        )
        prob_low = probability.astype(jnp.bfloat16)
        prob_grad = jnp.einsum(
            "esh,kh->esk",
            grad_full[:, row_lower : row_lower + row_len],
            value_full[row_lower : row_lower + row_len],
            preferred_element_type=jnp.float32,
        )
        row_delta = jnp.sum(probability * prob_grad, axis=2, keepdims=True)
        score_grad = (probability * (prob_grad - row_delta)).astype(jnp.bfloat16)
        query_grads.append(
            (
                jnp.einsum("esk,kh->esh", score_grad, key_row, preferred_element_type=jnp.float32)
                * score_scale
            ).astype(jnp.bfloat16)
        )
        key_grads.append(
            jnp.einsum("esk,esh->kh", score_grad, query_row, preferred_element_type=jnp.float32)
            * score_scale
        )
        value_grads.append(
            jnp.einsum("esk,esh->kh", prob_low, grad_row, preferred_element_type=jnp.float32)
        )
    query_grad = jnp.concatenate(query_grads, axis=1)
    key_grad = jnp.concatenate(key_grads, axis=0)
    value_grad = jnp.concatenate(value_grads, axis=0)
    query_w_grad = jnp.einsum(
        "td,eth->edh", rounded, query_grad, preferred_element_type=jnp.float32
    )
    query_b_grad = jnp.sum(query_grad.astype(jnp.float32), axis=1)
    key_w_grad = jnp.einsum(
        "td,th->dh", rounded, key_grad, precision=precise, preferred_element_type=jnp.float32
    )
    value_w_grad = jnp.einsum(
        "td,th->dh", rounded, value_grad, precision=precise, preferred_element_type=jnp.float32
    )
    value_b_grad = jnp.sum(value_grad, axis=0)
    normed_part = jnp.einsum("eth,edh->td", query_grad, query_w, preferred_element_type=jnp.float32)
    normed_part = normed_part + jnp.einsum(
        "th,dh->td", key_grad, key_w, precision=precise, preferred_element_type=jnp.float32
    )
    normed_part = normed_part + jnp.einsum(
        "th,dh->td", value_grad, value_w, precision=precise, preferred_element_type=jnp.float32
    )
    normed_rows = lax.psum_scatter(
        normed_part.astype(jnp.bfloat16), ("expert", "narrow"), scatter_dimension=0, tiled=True
    ).astype(jnp.float32)
    logit_rows = lax.dynamic_slice_in_dim(logit_grad, grad_start, grad_rows, 0)
    normed_rows = normed_rows + jnp.einsum(
        "te,de->td", logit_rows, router_w, precision=precise, preferred_element_type=jnp.float32
    )
    unit_rows = lax.dynamic_slice_in_dim(unit_one, grad_start, grad_rows, 0)
    inverse_rows = lax.dynamic_slice_in_dim(inverse_one, grad_start, grad_rows, 0)
    back_one, gain_one_part, shift_one_part = norm_backward(
        normed_rows, unit_rows, inverse_rows, gain_one
    )
    input_grad = lax.dynamic_slice_in_dim(hidden_grad, grad_start, grad_rows, 0) + back_one
    key_w_grad, value_w_grad, value_b_grad = lax.psum(
        (key_w_grad, value_w_grad, value_b_grad), ("dp", "expert")
    )
    query_w_grad, query_b_grad, out_w_grad, out_b_grad, router_w_grad, router_b_grad = (
        lax.psum(query_w_grad.astype(jnp.bfloat16), "dp").astype(jnp.float32),
        lax.psum(query_b_grad.astype(jnp.bfloat16), "dp").astype(jnp.float32),
        lax.psum(out_w_grad.astype(jnp.bfloat16), "dp").astype(jnp.float32),
        lax.psum(out_b_grad.astype(jnp.bfloat16), "dp").astype(jnp.float32),
        lax.psum(router_w_grad.astype(jnp.bfloat16), "dp").astype(jnp.float32),
        lax.psum(router_b_grad.astype(jnp.bfloat16), "dp").astype(jnp.float32),
    )
    gain_one_grad, shift_one_grad = lax.psum(
        (gain_one_part, shift_one_part), ("dp", "expert", "narrow")
    )
    return (
        output,
        input_grad,
        gain_one_grad,
        shift_one_grad,
        query_w_grad,
        query_b_grad,
        key_w_grad,
        value_w_grad,
        value_b_grad,
        out_w_grad,
        out_b_grad,
        router_w_grad,
        router_b_grad,
        gain_two_grad,
        shift_two_grad,
        up_w_grad,
        up_b_grad,
        down_w_grad,
        down_b_grad,
    )


def solution(mesh):
    return jax.shard_map(
        per_device,
        mesh=mesh,
        in_specs=(
            P("dp", None),
            P("dp", None),
            P("dp", None),
            P(),
            P(),
            P("expert", None, "narrow"),
            P("expert", "narrow"),
            P(None, "narrow"),
            P(None, "narrow"),
            P("narrow"),
            P("expert", "narrow", None),
            P(),
            P(),
            P(),
            P(),
            P(),
            P(None, "narrow"),
            P("narrow"),
            P("narrow", None),
            P(),
            P(("dp", "expert"), "narrow"),
        ),
        out_specs=(
            P(("dp", "expert"), "narrow"),
            P(("dp", "expert", "narrow"), None),
            P(),
            P(),
            P("expert", None, "narrow"),
            P("expert", "narrow"),
            P(None, "narrow"),
            P(None, "narrow"),
            P("narrow"),
            P("expert", "narrow", None),
            P(),
            P(),
            P(),
            P(),
            P(),
            P(None, "narrow"),
            P("narrow"),
            P("narrow", None),
            P(),
        ),
        check_vma=False,
    )
```

profile of v0, /device:TPU:0, one launch (start us, length us, event | category | flops | bytes accessed | tf_op | source)
XLA Modules:
  0.0 1010.4 jit_solution(2829049117726960064)
XLA Ops:
  7.3 4.0 reduce_sum.360
  11.3 4.2 multiply_reduce_fusion.6
  15.6 6.3 add_convert_fusion
  34.2 24.7 %all_gather.19 = bf16[4096,64]{0,1:T(8,128)(2,1)} all-gather(bf16[4096,16]{0,1:T(8,128)(2,1)S(1)} %convolution_convert_fusion), channel_id=1, replica_groups=mesh['dp'=4,'expert'=2,'narrow'=4] {'narrow'}, dimensions={1}, use_global_device_ids=true | all-gather | bytes 655360 | tf_op jit(solution)/shard_map/all_gather | solution.py:100
  64.8 18.7 %all-gather.5.cloned.1.call-done = bf16[4,4096,64]{1,2,0:T(8,128)(2,1)} async-done(((bf16[4,4096,16]{1,2,0:T(8,128)(2,1)}), bf16[4,4096,64]{1,2,0:T(8,128)(2,1)}) %all-gather.5.cloned.1.call-update) | async-done | bytes 2097168 | tf_op jit(solution)/shard_map/all_gather | solution.py:99
  83.5 4.5 fusion.9
  101.4 9.9 convolution_convert_fusion.3
  111.3 4.6 convolution_convert_fusion.4
  124.4 4.2 convolution_convert_fusion.5
  137.1 4.2 convolution_convert_fusion.6
  141.3 16.8 %multiply_reduce_fusion.1 = (bf16[4096,512]{0,1:T(8,128)(2,1)}, f32[4,4096,512]{1,2,0:T(8,128)}) fusion(f32[4,4096]{1,0:T(4,128)S(1)} %dynamic-slice_bitcast_fusion, bf16[4,16,512]{2,1,0:T(8,128)(2,1)S(1)} %copy-done.46, bf16[4,1024,16]{1,2,0:T(8,128)(2,1)S(1)} %convolution_convert_fusion.3, bf16[4,1024,16]{1,2,0:T(8,128)(2,1)S(1)} %convolution_convert_fusion.4, ...), kind=kOutput, calls=%fused_computation.2 | convolution fusion | flops 285212672 | bytes 38404096 | tf_op jit(solution)/shard_map/eth,ehd->etd/dot_general | solution.py:130
  158.1 6.5 copy.88
  165.4 154.2 %all-reduce.12.cloned.1.call-done = bf16[4096,512]{1,0:T(8,128)(2,1)} async-done(((bf16[4096,512]{1,0:T(8,128)(2,1)}), bf16[4096,512]{1,0:T(8,128)(2,1)}) %all-reduce.12.cloned.1.call-update) | async-done | bytes 4194320 | tf_op jit(solution)/shard_map/psum | solution.py:133
  319.6 5.9 add_add_fusion
  331.8 34.7 %all-gather.7.cloned.1.call-done = bf16[2048,512]{1,0:T(8,128)(2,1)} async-done(((bf16[2048,128]{1,0:T(8,128)(2,1)}), bf16[2048,512]{1,0:T(8,128)(2,1)}) %all-gather.7.cloned.1.call-update) | async-done | bytes 2097168 | tf_op jit(solution)/shard_map/all_gather | solution.py:150
  366.5 7.6 convert_reduce_fusion.2
  378.1 84.9 %all-reduce.14.cloned.1.call-done = bf16[2048,512]{1,0:T(8,128)(2,1)} async-done(((bf16[2048,512]{1,0:T(8,128)(2,1)}), bf16[2048,512]{1,0:T(8,128)(2,1)}) %all-reduce.14.cloned.1.call-update) | async-done | bytes 2097168 | tf_op jit(solution)/shard_map/psum | solution.py:157
  463.0 4.7 fusion.32
  467.7 5.9 convert_reduce_fusion.1
  474.1 55.4 %all-gather.9.cloned.1.call-done = bf16[4096,512]{1,0:T(8,128)(2,1)} async-done(((bf16[2048,512]{1,0:T(8,128)(2,1)}), bf16[4096,512]{1,0:T(8,128)(2,1)}) %all-gather.9.cloned.1.call-update) | async-done | bytes 4194320 | tf_op jit(solution)/shard_map/all_gather | solution.py:171
  529.5 7.1 copy.89
  536.6 6.5 fusion.19
  543.1 20.1 %all_gather.23 = bf16[4096,64]{0,1:T(8,128)(2,1)S(1)} all-gather(bf16[4096,16]{0,1:T(8,128)(2,1)S(1)} %fusion.20), channel_id=1, replica_groups=mesh['dp'=4,'expert'=2,'narrow'=4] {'narrow'}, dimensions={1}, use_global_device_ids=true | all-gather | bytes 655360 | tf_op jit(solution)/shard_map/all_gather | solution.py:197
  563.2 4.4 convolution_convert_fusion.2
  571.6 8.8 fusion.109
  580.4 14.9 %multiply_reduce_fusion = bf16[4,4096]{1,0:T(4,128)(2,1)S(1)} fusion(f32[4,4096,512]{1,2,0:T(8,128)} %get-tuple-element.68, f32[4096,512]{0,1:T(8,128)} %copy.89), kind=kLoop, calls=%fused_computation | loop fusion | flops 16760832 | bytes 41975808 | tf_op jit(solution)/shard_map/reduce_sum | solution.py:175
  595.4 8.7 fusion.42
  604.1 9.0 fusion.110
  613.1 8.9 fusion.112
  622.1 4.7 fusion.111
  626.8 5.7 fusion.70
  632.6 15.3 %multiply_reduce_fusion.2 = (f32[4,1024]{1,0:T(4,128)S(1)}, f32[4,1024,1024]{1,2,0:T(8,128)}) fusion(f32[4,1024,1024]{1,2,0:T(8,128)} %copy-done.8, f32[4,1024]{1,0:T(4,128)S(1)} %log_add_fusion, pred[1024,1024]{0,1:T(8,128)(4,1)} %broadcast_compare_fusion, bf16[4096,64]{0,1:T(8,128)(2,1)S(1)} %all_gather.23, ...), kind=kOutput, calls=%fused_computation.6 | convolution fusion | flops 557838336 | bytes 35291136 | tf_op jit(solution)/shard_map/esh,kh->esk/dot_general | solution.py:215
  647.9 12.9 %multiply_convert_fusion.3 = bf16[4,1024,1024]{1,2,0:T(8,128)(2,1)S(1)} fusion(f32[4,1024,1024]{1,2,0:T(8,128)} %get-tuple-element.70, f32[4,1024,1024]{1,2,0:T(8,128)} %copy-done.8, f32[4,1024]{1,0:T(4,128)S(1)} %get-tuple-element.69, f32[4,1024]{1,0:T(4,128)S(1)} %log_add_fusion, pred[1024,1024]{0,1:T(8,128)(4,1)S(1)} %copy-done.13), kind=kLoop, calls=%fused_computation.5 | loop fusion | flops 25165824 | bytes 43024384 | tf_op jit(solution)/shard_map/convert_element_type | solution.py:222
  666.4 10.2 %multiply_reduce_fusion.3 = (f32[4,1024]{1,0:T(4,128)}, f32[4,1024,1024]{1,2,0:T(8,128)}) fusion(f32[4,1024,1024]{1,2,0:T(8,128)S(1)} %bitcast.170, f32[4,1024]{1,0:T(4,128)} %copy-done.45, pred[1024,1024]{0,1:T(8,128)(4,1)} %broadcast_compare_fusion.1, bf16[4096,64]{0,1:T(8,128)(2,1)} %copy-done.15, bf16[4,4096,64]{1,2,0:T(8,128)(2,1)} %all-gather.11.cloned.1.call-done), kind=kOutput, calls=%fused_computation.8 | convolution fusion | flops 557838336 | bytes 35291136 | tf_op jit(solution)/shard_map/esh,kh->esk/dot_general | solution.py:215
  676.6 13.4 %multiply_convert_fusion.4 = bf16[4,1024,1024]{1,2,0:T(8,128)(2,1)S(1)} fusion(f32[4,1024,1024]{1,2,0:T(8,128)} %get-tuple-element.72, f32[4,1024,1024]{1,2,0:T(8,128)} %copy-done.7, f32[4,1024]{1,0:T(4,128)} %get-tuple-element.71, f32[4,1024]{1,0:T(4,128)} %copy-done.45, pred[1024,1024]{0,1:T(8,128)(4,1)} %broadcast_compare_fusion.1), kind=kLoop, calls=%fused_computation.7 | loop fusion | flops 25165824 | bytes 43024384 | tf_op jit(solution)/shard_map/convert_element_type | solution.py:222
  695.6 10.0 multiply_reduce_fusion.4
  705.6 12.8 %multiply_convert_fusion.5 = bf16[4,1024,1024]{1,2,0:T(8,128)(2,1)S(1)} fusion(f32[4,1024,1024]{1,2,0:T(8,128)} %get-tuple-element.74, f32[4,1024,1024]{1,2,0:T(8,128)} %copy-done.6, f32[4,1024]{1,0:T(4,128)} %get-tuple-element.73, f32[4,1024]{1,0:T(4,128)} %copy-done.44, pred[1024,1024]{0,1:T(8,128)(4,1)S(1)} %broadcast_compare_fusion.2), kind=kLoop, calls=%fused_computation.9 | loop fusion | flops 25165824 | bytes 43024384 | tf_op jit(solution)/shard_map/convert_element_type | solution.py:222
  722.0 9.6 multiply_reduce_fusion.5
  731.6 8.3 multiply_convert_fusion.6
  748.6 6.8 fusion.15
  761.2 5.9 fusion.50
  771.7 4.6 fusion.69
  786.0 10.9 %all-reduce.3 = (bf16[4,16]{1,0:T(4,128)(2,1)S(1)}, bf16[512]{0:T(512)(128)(2,1)S(1)}, bf16[512,8]{0,1:T(8,128)(2,1)S(1)}, bf16[8]{0:T(256)(128)(2,1)S(1)}) all-reduce(bf16[4,16]{1,0:T(4,128)(2,1)S(1)} %add_add_fusion.2, bf16[512]{0:T(512)(128)(2,1)S(1)} %get-tuple-element.51, ...), channel_id=1, replica_groups=mesh['dp'=4,'expert'=2,'narrow'=4] {'dp'}, use_global_device_ids=true, to_apply=%region_43.44 | all-reduce | flops 4680 | bytes 18720 | tf_op jit(solution)/shard_map/psum | solution.py:275
  799.2 4.6 fusion.71
  806.9 60.5 %reduce-scatter.5.cloned.1.call-done = bf16[512,512]{1,0:T(8,128)(2,1)} async-done(((bf16[4096,512]{1,0:T(8,128)(2,1)}), bf16[512,512]{1,0:T(8,128)(2,1)}) %reduce-scatter.5.cloned.1.call-update) | async-done | bytes 524304 | tf_op jit(solution)/shard_map/reduce_scatter | solution.py:257
  872.6 40.4 %all-reduce = (f32[512]{0:T(512)}, f32[512]{0:T(512)}) all-reduce(f32[512]{0:T(512)S(1)} %get-tuple-element.21, f32[512]{0:T(512)S(1)} %get-tuple-element.26), channel_id=1, replica_groups=mesh['dp'=4,'expert'=2,'narrow'=4] {'dp','expert','narrow'}, use_global_device_ids=true, to_apply=%region_35.36 | all-reduce | flops 1024 | bytes 8192 | tf_op jit(solution)/shard_map/psum | solution.py:281
  913.0 20.5 %all-reduce.20.cloned.1.call-done = (f32[512,512]{1,0:T(8,128)}, f32[512,512]{1,0:T(8,128)}) async-done(((f32[512,512]{1,0:T(8,128)}, f32[512,512]{1,0:T(8,128)}), (f32[512,512]{1,0:T(8,128)}, f32[512,512]{1,0:T(8,128)})) %all-reduce.20.cloned.1.call-update) | async-done | bytes 2097168 | tf_op jit(solution)/shard_map/psum | solution.py:167
  933.5 56.3 %all-reduce.18.cloned.1.call-done = (f32[512,16]{0,1:T(8,128)}, f32[512,16]{0,1:T(8,128)}, f32[16]{0:T(128)}, f32[512]{0:T(512)}, f32[512]{0:T(512)}, /*index=5*/f32[512]{0:T(512)}, f32[512]{0:T(512)}) async-done(((f32[512,16]{0,1:T(8,128)}, f32[512,16]{0,1:T(8,128)}, f32[16]{0:T(128)}, f32[512]{0:T(512)}, f32[512]{0:T(512)}, /*index=5*/f32[512]{0:T(512)}, f32[512]{0:T(512)}), (f32[512,16]{0,1:T(8,128)}, ...) | async-done | bytes 73808 | tf_op jit(solution)/shard_map/psum | solution.py:270
  (312 shorter events, 131.2 us)
Async XLA Ops:
  7.2 359.3 %copy-start = (bf16[512,512]{1,0:T(8,128)(2,1)S(1)}, bf16[512,512]{1,0:T(8,128)(2,1)}, u32[]{:S(2)}) copy-start(bf16[512,512]{1,0:T(8,128)(2,1)} %param.39) | copy-start | bytes 1572868
  7.2 76.3 %all-gather.5.cloned.1.call-start = ((), (), s32[]{:S(2)}) async-start(), calls=%async_computation.2 | async-start | bytes 2621440 | tf_op jit(solution)/shard_map/all_gather | solution.py:99
  25.3 33.7 %copy-start.65 = (s32[4,1024]{1,0:T(4,128)S(1)}, s32[4,1024]{1,0:T(4,128)}, u32[]{:S(2)}) copy-start(s32[4,1024]{1,0:T(4,128)} %param.22) | copy-start | bytes 49156
  26.2 37.3 %copy-start.57 = (bf16[512,16]{0,1:T(8,128)(2,1)S(1)}, bf16[512,16]{0,1:T(8,128)(2,1)}, u32[]{:S(2)}) copy-start(bf16[512,16]{0,1:T(8,128)(2,1)} %param.29) | copy-start | bytes 49156
  26.3 37.3 %copy-start.71 = (f32[16]{0:T(128)S(1)}, f32[16]{0:T(128)}, u32[]{:S(2)}) copy-start(f32[16]{0:T(128)} %param.30) | copy-start | bytes 196
  26.3 293.3 %all-reduce.12.cloned.1.call-start = ((), (), s32[]{:S(2)}) async-start(), calls=%async_computation.3 | async-start | bytes 8388608 | tf_op jit(solution)/shard_map/psum | solution.py:133
  29.8 34.9 %copy-start.19 = (f32[4096,2]{0,1:T(2,128)}, f32[4096,2]{0,1:T(2,128)S(1)}, u32[]{:S(2)}) copy-start(f32[4096,2]{0,1:T(2,128)S(1)} %select_reduce_fusion.4) | copy-start | bytes 98308
  29.9 34.8 %copy-start.29 = (f32[4096]{0:T(1024)}, f32[4096]{0:T(1024)S(1)}, u32[]{:S(2)}) copy-start(f32[4096]{0:T(1024)S(1)} %reduce_max.45) | copy-start | bytes 49156
  30.6 32.9 %copy-start.3 = (bf16[4096,512]{1,0:T(8,128)(2,1)S(1)}, bf16[4096,512]{1,0:T(8,128)(2,1)}, u32[]{:S(2)}) copy-start(bf16[4096,512]{1,0:T(8,128)(2,1)} %copy-done.2) | copy-start | bytes 12582916
  34.2 24.7 %copy-start.17 = (bf16[4096,16]{0,1:T(8,128)(2,1)}, bf16[4096,16]{0,1:T(8,128)(2,1)S(1)}, u32[]{:S(2)}) copy-start(bf16[4096,16]{0,1:T(8,128)(2,1)S(1)} %convolution_convert_fusion) | copy-start | bytes 393220
  101.4 502.7 %copy-start.45 = (f32[4,1024]{1,0:T(4,128)}, f32[4,1024]{1,0:T(4,128)S(1)}, u32[]{:S(2)}) copy-start(f32[4,1024]{1,0:T(4,128)S(1)} %log_add_fusion.1) | copy-start | bytes 49156
  111.3 30.0 %copy-start.47 = (bf16[4,1024,16]{1,2,0:T(8,128)(2,1)}, bf16[4,1024,16]{1,2,0:T(8,128)(2,1)S(1)}, u32[]{:S(2)}) copy-start(bf16[4,1024,16]{1,2,0:T(8,128)(2,1)S(1)} %convolution_convert_fusion.3) | copy-start | bytes 393220
  115.9 25.4 %copy-start.49 = (bf16[4,1024,16]{1,2,0:T(8,128)(2,1)}, bf16[4,1024,16]{1,2,0:T(8,128)(2,1)S(1)}, u32[]{:S(2)}) copy-start(bf16[4,1024,16]{1,2,0:T(8,128)(2,1)S(1)} %convolution_convert_fusion.4) | copy-start | bytes 393220
  124.4 488.7 %copy-start.44 = (f32[4,1024]{1,0:T(4,128)}, f32[4,1024]{1,0:T(4,128)S(1)}, u32[]{:S(2)}) copy-start(f32[4,1024]{1,0:T(4,128)S(1)} %log_add_fusion.2) | copy-start | bytes 49156
  141.3 16.8 %copy-start.51 = (bf16[4,1024,16]{1,2,0:T(8,128)(2,1)}, bf16[4,1024,16]{1,2,0:T(8,128)(2,1)S(1)}, u32[]{:S(2)}) copy-start(bf16[4,1024,16]{1,2,0:T(8,128)(2,1)S(1)} %convolution_convert_fusion.6) | copy-start | bytes 393220
  158.1 161.5 %copy-start.72 = (f32[512]{0:T(512)S(1)}, f32[512]{0:T(512)}, u32[]{:S(2)}) copy-start(f32[512]{0:T(512)} %param.32) | copy-start | bytes 6148
  164.6 201.9 %all-gather.7.cloned.1.call-start = ((), (), s32[]{:S(2)}) async-start(), calls=%async_computation.4 | async-start | bytes 2621440 | tf_op jit(solution)/shard_map/all_gather | solution.py:150
  165.3 297.6 %all-reduce.14.cloned.1.call-start = ((), (), s32[]{:S(2)}) async-start(), calls=%async_computation.5 | async-start | bytes 4194304 | tf_op jit(solution)/shard_map/psum | solution.py:157
  325.6 40.9 %copy-start.79 = (f32[512]{0:T(512)S(1)}, f32[512]{0:T(512)}, u32[]{:S(2)}) copy-start(f32[512]{0:T(512)} %param.38) | copy-start | bytes 6148
  326.0 141.7 %copy-start.52 = (f32[2048]{0:T(1024)}, f32[2048]{0:T(1024)S(1)}, u32[]{:S(2)}) copy-start(f32[2048]{0:T(1024)S(1)} %broadcast_multiply_fusion.3) | copy-start | bytes 24580
  328.9 138.8 %copy-start.55 = (f32[2048]{0:T(1024)}, f32[2048]{0:T(1024)S(1)}, u32[]{:S(2)}) copy-start(f32[2048]{0:T(1024)S(1)} %add_rsqrt_fusion.1) | copy-start | bytes 24580
  378.0 151.4 %all-gather.9.cloned.1.call-start = ((), (), s32[]{:S(2)}) async-start(), calls=%async_computation.6 | async-start | bytes 6291456 | tf_op jit(solution)/shard_map/all_gather | solution.py:171
  473.6 158.9 %all-gather.11.cloned.1.call-start = ((), (), s32[]{:S(2)}) async-start(), calls=%async_computation.7 | async-start | bytes 2621440 | tf_op jit(solution)/shard_map/all_gather | solution.py:196
  543.1 224.1 %reduce-scatter.7.cloned.1.call-start = ((), (), s32[]{:S(2)}) async-start(), calls=%async_computation.10 | async-start | bytes 2621440
  563.2 69.4 %copy-start.15 = (bf16[4096,64]{0,1:T(8,128)(2,1)}, bf16[4096,64]{0,1:T(8,128)(2,1)S(1)}, u32[]{:S(2)}) copy-start(bf16[4096,64]{0,1:T(8,128)(2,1)S(1)} %all_gather.23) | copy-start | bytes 1572868
  571.5 209.2 %all-reduce.16.cloned.1.call-start = ((), (), s32[]{:S(2)}) async-start(), calls=%async_computation.9 | async-start | bytes 131072 | tf_op jit(solution)/shard_map/psum | solution.py:182
  580.4 46.4 %copy-start.33 = (f32[1024,16]{0,1:T(8,128)}, f32[1024,16]{0,1:T(8,128)S(1)}, u32[]{:S(2)}) copy-start(f32[1024,16]{0,1:T(8,128)S(1)} %get-tuple-element.87) | copy-start | bytes 196612
  595.4 17.7 %copy-start.41 = (bf16[4096,8]{0,1:T(8,128)(2,1)}, bf16[4096,8]{0,1:T(8,128)(2,1)S(1)}, u32[]{:S(2)}) copy-start(bf16[4096,8]{0,1:T(8,128)(2,1)S(1)} %bitcast_dynamic-update-slice_fusion) | copy-start | bytes 196612
  604.1 17.9 %slice-start = ((s8[16777216]{0:T(1024)(128)(4,1)}), s8[4194304]{0:T(1024)(128)(4,1)S(1)}, s32[]{:S(2)}) async-start(s8[16777216]{0:T(1024)(128)(4,1)} %bitcast.163), calls=%async_computation.14 | async-start | bytes 8388608
  604.1 17.9 %slice-start.1 = ((s8[16777216]{0:T(1024)(128)(4,1)}), s8[4194304]{0:T(1024)(128)(4,1)S(1)}, s32[]{:S(2)}) async-start(s8[16777216]{0:T(1024)(128)(4,1)} %bitcast.163), calls=%async_computation.15 | async-start | bytes 8388608
  626.7 21.1 %copy-start.39 = (f32[1024,16]{0,1:T(8,128)}, f32[1024,16]{0,1:T(8,128)S(1)}, u32[]{:S(2)}) copy-start(f32[1024,16]{0,1:T(8,128)S(1)} %get-tuple-element.91) | copy-start | bytes 196612
  626.8 177.1 %all-reduce.22.cloned.1.call-start = ((), (), s32[]{:S(2)}) async-start(), calls=%async_computation.13 | async-start | bytes 262144 | tf_op jit(solution)/shard_map/psum | solution.py:274
  632.6 15.3 %copy-start.13 = (pred[1024,1024]{0,1:T(8,128)(4,1)S(1)}, pred[1024,1024]{0,1:T(8,128)(4,1)}, u32[]{:S(2)}) copy-start(pred[1024,1024]{0,1:T(8,128)(4,1)} %broadcast_compare_fusion) | copy-start | bytes 3145732
  647.9 18.5 %slice-start.12 = ((s8[16777216]{0:T(1024)(128)(4,1)}), s8[4194304]{0:T(1024)(128)(4,1)S(1)}, s32[]{:S(2)}) async-start(s8[16777216]{0:T(1024)(128)(4,1)} %bitcast.169), calls=%async_computation.26 | async-start | bytes 8388608
  647.9 18.5 %slice-start.13 = ((s8[16777216]{0:T(1024)(128)(4,1)}), s8[4194304]{0:T(1024)(128)(4,1)S(1)}, s32[]{:S(2)}) async-start(s8[16777216]{0:T(1024)(128)(4,1)} %bitcast.169), calls=%async_computation.27 | async-start | bytes 8388608
  647.9 18.4 %slice-start.14 = ((s8[16777216]{0:T(1024)(128)(4,1)}), s8[4194304]{0:T(1024)(128)(4,1)S(1)}, s32[]{:S(2)}) async-start(s8[16777216]{0:T(1024)(128)(4,1)} %bitcast.169), calls=%async_computation.28 | async-start | bytes 8388608
  676.6 19.0 %slice-start.8 = ((s8[16777216]{0:T(1024)(128)(4,1)}), s8[4194304]{0:T(1024)(128)(4,1)S(1)}, s32[]{:S(2)}) async-start(s8[16777216]{0:T(1024)(128)(4,1)} %bitcast.167), calls=%async_computation.22 | async-start | bytes 8388608
  676.6 19.0 %slice-start.9 = ((s8[16777216]{0:T(1024)(128)(4,1)}), s8[4194304]{0:T(1024)(128)(4,1)S(1)}, s32[]{:S(2)}) async-start(s8[16777216]{0:T(1024)(128)(4,1)} %bitcast.167), calls=%async_computation.23 | async-start | bytes 8388608
  676.6 19.0 %slice-start.10 = ((s8[16777216]{0:T(1024)(128)(4,1)}), s8[4194304]{0:T(1024)(128)(4,1)S(1)}, s32[]{:S(2)}) async-start(s8[16777216]{0:T(1024)(128)(4,1)} %bitcast.167), calls=%async_computation.24 | async-start | bytes 8388608
  705.6 16.4 %slice-start.4 = ((s8[16777216]{0:T(1024)(128)(4,1)}), s8[4194304]{0:T(1024)(128)(4,1)S(1)}, s32[]{:S(2)}) async-start(s8[16777216]{0:T(1024)(128)(4,1)} %bitcast.165), calls=%async_computation.18 | async-start | bytes 8388608
  705.6 16.4 %slice-start.5 = ((s8[16777216]{0:T(1024)(128)(4,1)}), s8[4194304]{0:T(1024)(128)(4,1)S(1)}, s32[]{:S(2)}) async-start(s8[16777216]{0:T(1024)(128)(4,1)} %bitcast.165), calls=%async_computation.19 | async-start | bytes 8388608
  705.6 16.4 %slice-start.6 = ((s8[16777216]{0:T(1024)(128)(4,1)}), s8[4194304]{0:T(1024)(128)(4,1)S(1)}, s32[]{:S(2)}) async-start(s8[16777216]{0:T(1024)(128)(4,1)} %bitcast.165), calls=%async_computation.20 | async-start | bytes 8388608
  745.0 122.4 %reduce-scatter.5.cloned.1.call-start = ((), (), s32[]{:S(2)}) async-start(), calls=%async_computation.8 | async-start | bytes 4718592 | tf_op jit(solution)/shard_map/reduce_scatter | solution.py:257
  755.4 178.1 %all-reduce.20.cloned.1.call-start = ((), (), s32[]{:S(2)}) async-start(), calls=%async_computation.12 | async-start | bytes 4194304 | tf_op jit(solution)/shard_map/psum | solution.py:167
  767.1 222.7 %all-reduce.18.cloned.1.call-start = ((), (), s32[]{:S(2)}) async-start(), calls=%async_computation.11 | async-start | bytes 148480 | tf_op jit(solution)/shard_map/psum | solution.py:270
  776.8 90.6 %copy-start.62 = (bf16[512,8]{0,1:T(8,128)(2,1)S(1)}, bf16[512,8]{0,1:T(8,128)(2,1)}, u32[]{:S(2)}) copy-start(bf16[512,8]{0,1:T(8,128)(2,1)} %param.33) | copy-start | bytes 24580
  776.8 90.6 %copy-start.64 = (f32[512]{0:T(512)S(1)}, f32[512]{0:T(512)}, u32[]{:S(2)}) copy-start(f32[512]{0:T(512)} %param.24) | copy-start | bytes 6148
  782.0 221.3 %copy-start.1 = (bf16[512,512]{1,0:T(8,128)(2,1)S(1)}, bf16[512,512]{1,0:T(8,128)(2,1)}, u32[]{:S(2)}) copy-start(bf16[512,512]{1,0:T(8,128)(2,1)} %param.39) | copy-start | bytes 1572868
  (63 other events, 457.6 us)
Sparse Core Ops, SparseCore 0:
  26.4 57.0 all-gather.4
  164.7 154.8 all-reduce.11
  321.2 45.2 all-gather.6
  378.2 84.7 all-reduce.13
  473.7 55.6 all-gather.8
  543.2 49.0 all-gather.10
  594.7 42.2 reduce-scatter.6
  640.4 67.8 all-reduce.15
  745.1 30.2 all-reduce.21
  779.3 87.9 reduce-scatter.4
  871.8 61.6 all-reduce.19
  939.1 50.7 all-reduce.17
where the time goes:
time: 1020 us; the launch traced here: 1010 us
  waiting for transfers between devices  486 us (48%)
  matrix products  232 us (23%)
  other arithmetic  132 us (13%)
  blocking collectives  96.1 us (9%)
  local copies, waits for them, and re-layouts  47.6 us (5%)
  between operations  15.8 us (2%)
    psum x1, waiting for transfers between devices, per_device(): lax.psum(gated.astype(jnp.bfloat16), ('expert', 'narrow'))  154 us
    psum x1, waiting for transfers between devices, per_device(): lax.psum(jnp.einsum('tf,df->td', upper_grad, up_w, preferred_element_type...  84.9 us
    reduce_scatter x1, waiting for transfers between devices, per_device(): lax.psum_scatter(normed_part.astype(jnp.bfloat16), ('expert', 'narrow'),...  60.5 us
    psum x1, waiting for transfers between devices, per_device(): lax.psum((key_w_grad, value_w_grad, value_b_grad), ('dp', 'expert'))  56.3 us
    all_gather x1, waiting for transfers between devices, per_device(): lax.all_gather(hidden_rows_grad.astype(jnp.bfloat16), 'expert', axis=0, t...  55.4 us
    convert_element_type x4, other arithmetic, per_device(): score_grad = (probability * (prob_grad - row_delta)).astype(jnp.bfloat16)  47.3 us
    dot_general x4, matrix products, per_device(): jnp.einsum('esh,kh->esk', grad_full[:, row_lower:row_lower + row_len], va...  45.1 us
    psum x1, blocking collectives, per_device(): lax.psum((gain_one_part, shift_one_part), ('dp', 'expert', 'narrow'))  40.4 us
  transfers between devices with their start and end apart: 12, of which 8 were waited for; matrix products, arithmetic and copies ran while one was open for 26% of the time, Pallas kernels for 0%

commit v1 on v0

v1 whole, which is shorter than its diff:
```python
import functools
import math

import jax
import jax.numpy as jnp
from jax import lax
from jax.experimental import pallas as pl
from jax.experimental.pallas import tpu as pltpu
from jax.sharding import PartitionSpec as P

HEAD = 64
LONGEST = 256
EPSILON = 1e-05
MASKED = -1000000000.0
GELU_A = math.sqrt(2.0 / math.pi)
GELU_B = 0.044715
F32 = jnp.float32
BF16 = jnp.bfloat16
MESH = pl.DeviceIdType.MESH


def dot(a, b):
    return lax.dot_general(a, b, (((1,), (0,)), ((), ())), preferred_element_type=F32)


def dot_nt(a, b):
    return lax.dot_general(a, b, (((1,), (1,)), ((), ())), preferred_element_type=F32)


def dot_tn(a, b):
    return lax.dot_general(a, b, (((0,), (0,)), ((), ())), preferred_element_type=F32)


def norm_stats(x):
    centred = x - jnp.mean(x, axis=1, keepdims=True)
    inverse = lax.rsqrt(jnp.mean(centred * centred, axis=1, keepdims=True) + EPSILON)
    return centred * inverse, inverse


def rem(a, b):
    return lax.rem(a, b)


class Sizes:
    def __init__(self, dp, expert, narrow, tokens, width, row_len, local_experts, ff_local):
        self.dp, self.expert, self.narrow = dp, expert, narrow
        self.tokens, self.width, self.row_len = tokens, width, row_len
        self.local_experts = local_experts
        self.experts = local_experts * expert
        self.group = expert * narrow
        self.block = tokens // self.group
        self.rows_y = dp // 2
        self.plane = self.rows_y * expert
        self.ff_local = ff_local
        self.head_part = HEAD // narrow
        self.shard = local_experts * self.head_part
        self.per_row = row_len // self.block
        spans = [
            min(row_len, (j + 1) * self.block + LONGEST) - max(0, j * self.block - LONGEST)
            for j in range(self.per_row)
        ]
        self.window = max(spans)
        self.reach = max(1, LONGEST // self.block) if self.per_row > 1 else 0
        self.piece = min(self.block, LONGEST)
        self.tile = min(256, self.block)
        self.up_rows = narrow * ff_local // width
        self.small_rows = 24


def kernel(
    z,
    x_any,
    seg_ref,
    chosen_ref,
    vec_ref,
    q_ref,
    k_ref,
    v_ref,
    o_ref,
    r_ref,
    up_any,
    down_any,
    cot_ref,
    out_ref,
    ig_ref,
    gq_ref,
    go_ref,
    gk_ref,
    gv_ref,
    gup_ref,
    gdown_ref,
    small_ref,
    xw,
    xcols,
    rw,
    wq,
    wo,
    wk,
    wv,
    bias,
    ffw,
    cot,
    segs,
    segc,
    kn,
    vn,
    kt,
    vt,
    qt,
    qk,
    prob,
    mix,
    mixg,
    hid,
    acc,
    second,
    active,
    ugrad,
    sgrad,
    hgrad,
    hgb,
    mgk,
    dk,
    dv,
    dq,
    dqt,
    halo_out,
    halo_in,
    delta,
    outd,
    gsend,
    crecv,
    psend,
    precv,
    zsend,
    zrecv,
    fin,
    gqo,
    cqo,
    pqo,
    rqo,
    zqo,
    yqo,
    fqo,
    gkv,
    ckv,
    pkv,
    rkv,
    zkv,
    ykv,
    fkv,
    sp,
    csp,
    psp,
    rsp,
    zsp,
    ysp,
    loc_sem,
    q_s,
    q_r,
    o_s,
    o_r,
    w_s,
    w_r,
    b_s,
    b_r,
    m_s,
    m_r,
    fz_s,
    fz_r,
    fp_s,
    fp_r,
    fm_s,
    fm_r,
    ct_s,
    ct_r,
    od_s,
    od_r,
    hl_s,
    hl_r,
    gc_s,
    gc_r,
    gp_s,
    gp_r,
    gz_s,
    gz_r,
    ga_s,
    ga_r,
    qc_s,
    qc_r,
    qp_s,
    qp_r,
    qz_s,
    qz_r,
    qa_s,
    qa_r,
):
    d, e, n = lax.axis_index("dp"), lax.axis_index("expert"), lax.axis_index("narrow")
    c, y = rem(d, 2), lax.div(d, 2)
    N, G, NP, NE, NY = z.narrow, z.group, z.plane, z.expert, z.rows_y
    T, W, D, R, HP, LE = z.block, z.window, z.width, z.shard, z.head_part, z.local_experts
    FL = z.ff_local
    half = D // 2
    here = e * N + n
    spot = y * NE + e
    mate = (d + 1 - 2 * c, e, n)

    def in_group(j):
        at = rem(here + j + G, G)
        return at, (d, lax.div(at, N), rem(at, N))

    def in_plane(j):
        at = rem(spot + j + NP, NP)
        return at, (2 * lax.div(at, NE) + c, rem(at, NE), n)

    def in_line(j):
        at = rem(n + j + N, N)
        return at, (d, e, at)

    def in_rows(j):
        at = rem(y + j + NY, NY)
        return at, (2 * at + c, e, n)

    started = []

    def push(src, dst, send, recv, device):
        copy = pltpu.make_async_remote_copy(
            src_ref=src,
            dst_ref=dst,
            send_sem=send,
            recv_sem=recv,
            device_id=device,
            device_id_type=MESH,
        )
        copy.start()
        started.append(copy)

    def landed(dst, send, recv):
        pltpu.make_async_remote_copy(
            src_ref=dst,
            dst_ref=dst,
            send_sem=send,
            recv_sem=recv,
            device_id=mate,
            device_id_type=MESH,
        ).wait_recv()

    def rows(start, size, step=16):
        return pl.ds(pl.multiple_of(start, step), size)

    start = here * T
    row = lax.div(start, z.row_len)
    spot_in_row = rem(here, z.per_row)
    base = row * z.row_len
    ws = jnp.minimum(jnp.maximum(spot_in_row * T - LONGEST, 0), z.row_len - W)
    off = spot_in_row * T - ws
    own = rows(off, T, 128)

    x_copy = pltpu.make_async_copy(x_any.at[rows(base + ws, W, 128)], xw, loc_sem.at[0])
    x_copy.start()
    up_copy = pltpu.make_async_copy(up_any, ffw.at[n, pl.ds(0, D)], loc_sem.at[1])
    up_copy.start()
    down_copy = pltpu.make_async_copy(down_any, ffw.at[n, pl.ds(D, FL)], loc_sem.at[2])
    down_copy.start()
    cols_copy = pltpu.make_async_copy(
        x_any.at[rows(e * N * T, N * T, 128), rows(n * (D // N), D // N, 128)], xcols, loc_sem.at[3]
    )
    cols_copy.start()

    wq[rows(here * R, R)] = q_ref[...]
    wo[rows(here * R, R)] = o_ref[...]
    wk[rows(n * HP, HP)] = k_ref[...]
    wv[rows(n * HP, HP)] = v_ref[...]
    bias[here] = vec_ref[8:16, :]

    barrier = pltpu.get_barrier_semaphore()
    pl.semaphore_signal(barrier, inc=1, device_id=mate, device_id_type=MESH)
    for j in range(1, NP):
        pl.semaphore_signal(barrier, inc=1, device_id=in_plane(j)[1], device_id_type=MESH)
    for j in range(1, G):
        pl.semaphore_signal(barrier, inc=1, device_id=in_group(j)[1], device_id_type=MESH)
    pl.semaphore_wait(barrier, NP + G - 1)

    mine_cols = rows(c * half, half, 128)
    for j in range(1, N):
        _, to = in_line(j)
        at = rows(n * HP, HP)
        push(wk.at[at], wk.at[at], w_s.at[0, j], w_r.at[0, j], to)
        push(wv.at[at], wv.at[at], w_s.at[1, j], w_r.at[1, j], to)
    for j in range(1, G):
        _, to = in_group(j)
        push(bias.at[here], bias.at[here], b_s.at[j], b_r.at[j], to)
    for j in range(1, G):
        _, to = in_group(j)
        at = wq.at[rows(here * R, R), mine_cols]
        push(at, at, q_s.at[j], q_r.at[j], to)
    for j in range(1, G):
        _, to = in_group(j)
        at = wo.at[rows(here * R, R), mine_cols]
        push(at, at, o_s.at[j], o_r.at[j], to)
    up_copy.wait()
    down_copy.wait()
    FR = D + FL
    SR = FR // (2 * NP)
    slot_rows = rows((c * NP + spot) * SR, SR)
    for j in range(1, N):
        _, to = in_line(j)
        at = ffw.at[n, slot_rows]
        push(at, at, fz_s.at[j], fz_r.at[j], to)
    CW = D // N
    cot[:, rows(n * CW, CW, 128)] = cot_ref[rows(n * T, T, 128), :]
    for j in range(1, N):
        there, to = in_line(j)
        push(
            cot_ref.at[rows(there * T, T, 128)],
            cot.at[:, rows(n * CW, CW, 128)],
            ct_s.at[j],
            ct_r.at[j],
            to,
        )

    x_copy.wait()
    gain_one, shift_one = vec_ref[0:1, :], vec_ref[1:2, :]

    def norm_one(i, carry):
        at = rows(i * 128, 128, 128)
        unit, _ = norm_stats(xw[at, :])
        rw[at, :] = (unit * gain_one + shift_one).astype(BF16)
        return carry

    lax.fori_loop(0, W // 128, norm_one, 0)

    seg_all = seg_ref[...].astype(F32)
    row_id = lax.broadcasted_iota(jnp.int32, seg_all.shape, 0)
    seg_here = jnp.sum(jnp.where(row_id == row, seg_all, 0.0), axis=0, keepdims=True)
    segs[...] = jnp.broadcast_to(seg_here, segs.shape)
    segc[...] = jnp.transpose(segs[:, rows(ws, W, 128)])
    seg_own = segs[0:1, rows(spot_in_row * T, T, 128)]
    logits = dot_nt(r_ref[...], rw[own, :]) + vec_ref[16:24, 0:1]
    expert_id = lax.broadcasted_iota(jnp.int32, (z.experts, T), 0)
    hot, picked = [], []
    for k in range(2):
        chosen = chosen_ref[k : k + 1, rows(start, T, 128)]
        hot.append((expert_id == chosen).astype(F32))
        picked.append(jnp.sum(logits * hot[k], axis=0, keepdims=True))
    top = jnp.maximum(picked[0], picked[1])
    raised = [jnp.exp(p - top) for p in picked]
    total = raised[0] + raised[1]
    gate = [r / total for r in raised]

    for j in range(1, N):
        there, _ = in_line(-j)
        at = rows(there * HP, HP)
        landed(wk.at[at], w_s.at[0, j], w_r.at[0, j])
        landed(wv.at[at], w_s.at[1, j], w_r.at[1, j])
    for j in range(1, G):
        there, _ = in_group(-j)
        landed(bias.at[there], b_s.at[j], b_r.at[j])
    value_b = bias[0, 2:3, 0:HEAD]
    for j in range(1, N):
        value_b = value_b + bias[j, 2:3, 0:HEAD]
    value_col = jnp.transpose(jnp.broadcast_to(value_b, (8, HEAD)))[:, 0:1]
    kn[...] = dot_nt(rw[...], wk[...]).astype(BF16)
    kt[...] = dot_nt(wk[...], rw[...]).astype(BF16)
    vn[...] = (dot_nt(rw[...], wv[...]) + value_b).astype(BF16)
    vt[...] = (dot_nt(wv[...], rw[...]) + value_col).astype(BF16)

    other_cols = rows((1 - c) * half, half, 128)
    for j in range(1, G):
        there, _ = in_group(-j)
        at = wq.at[rows(there * R, R), mine_cols]
        landed(at, q_s.at[j], q_r.at[j])
        push(at, at, m_s.at[0, j], m_r.at[0, j], mate)
    for j in range(1, G):
        there, _ = in_group(-j)
        landed(wq.at[rows(there * R, R), other_cols], m_s.at[0, j], m_r.at[0, j])
    qt[...] = dot_nt(wq[...], rw[own, :])

    def expert_rows(at, i, part):
        return ((at * N + part) * LE + i) * HP

    for part in range(N):
        chosen_rows = [jnp.zeros((HP, T), F32), jnp.zeros((HP, T), F32)]
        for at in range(NE):
            g = at * N + part
            column = jnp.transpose(jnp.broadcast_to(bias[g, 1:2, 0:128], (8, 128)))
            for i in range(LE):
                lo = expert_rows(at, i, part)
                one = qt[lo : lo + HP, :] + column[i * HP : (i + 1) * HP, 0:1]
                for k in range(2):
                    chosen_rows[k] = chosen_rows[k] + one * hot[k][at * LE + i : at * LE + i + 1, :]
        for k in range(2):
            qk[k, part * HP : (part + 1) * HP, :] = chosen_rows[k].astype(BF16)

    for j in range(1, G):
        there, _ = in_group(-j)
        at = wo.at[rows(there * R, R), mine_cols]
        landed(at, o_s.at[j], o_r.at[j])
        push(at, at, m_s.at[1, j], m_r.at[1, j], mate)

    scale = 1.0 / math.sqrt(HEAD)
    TL = z.tile
    tiles = T // TL
    seg_tiles = [seg_own[:, i * TL : (i + 1) * TL] for i in range(tiles)]

    def attend(k):
        for i in range(tiles):
            at = pl.ds(i * TL, TL)
            scores = dot(kn[...], qk[k, :, at]) * scale
            scores = jnp.where(segc[:, 0:1] == seg_tiles[i], scores, MASKED)
            high = jnp.max(scores, axis=0, keepdims=True)
            raised_scores = jnp.exp(scores - high)
            low = (raised_scores * (1.0 / jnp.sum(raised_scores, axis=0, keepdims=True))).astype(BF16)
            prob[k, :, at] = low
            mix[k, :, at] = dot(vt[...], low)

    attend(0)
    for j in range(1, N):
        there, _ = in_line(-j)
        at = ffw.at[there, slot_rows]
        landed(at, fz_s.at[j], fz_r.at[j])
        for i in range(1, NP):
            _, to = in_plane(i)
            push(at, at, fp_s.at[j, i], fp_r.at[j, i], to)
    attend(1)

    for part in range(N):
        for at in range(NE):
            for i in range(LE):
                lo = expert_rows(at, i, part)
                x = at * LE + i
                gated = jnp.zeros((HP, T), F32)
                for k in range(2):
                    rounded_mix = mix[k, part * HP : (part + 1) * HP, :].astype(BF16).astype(F32)
                    gated = gated + rounded_mix * (hot[k][x : x + 1, :] * gate[k])
                mixg[lo : lo + HP, :] = gated.astype(BF16)
    for j in range(1, G):
        there, _ = in_group(-j)
        landed(wo.at[rows(there * R, R), other_cols], m_s.at[1, j], m_r.at[1, j])
    out_b, down_b = vec_ref[2:3, :], vec_ref[5:6, :]
    gain_two, shift_two = vec_ref[3:4, :], vec_ref[4:5, :]
    attention = dot_tn(mixg[...], wo[...]) + out_b
    acc[...] = attention + down_b
    hid[...] = xw[own, :] + attention

    def norm_two(i, carry):
        at = rows(i * 128, 128, 128)
        unit, _ = norm_stats(hid[at, :])
        second[at, :] = (unit * gain_two + shift_two).astype(BF16)
        return carry

    lax.fori_loop(0, T // 128, norm_two, 0)
    sgrad[...] = jnp.zeros_like(sgrad)

    for j in range(1, N):
        there, _ = in_line(-j)
        landed(cot.at[:, rows(there * CW, CW, 128)], ct_s.at[j], ct_r.at[j])

    HR = FR // 2
    HS = HR // NP

    def core_start(j):
        push(
            gsend.at[j, rows((1 - c) * HR, HR)], crecv.at[j], gc_s.at[j], gc_r.at[j], mate
        )

    def plane_start(j):
        landed(crecv.at[j], gc_s.at[j], gc_r.at[j])
        psend[j] = (
            gsend[j, rows(c * HR, HR), :].astype(F32) + crecv[j].astype(F32)
        ).astype(BF16)
        for i in range(1, NP):
            there, to = in_plane(i)
            push(psend.at[j, rows(there * HS, HS)], precv.at[j, i], gp_s.at[j, i], gp_r.at[j, i], to)

    def line_start(j):
        whole = psend[j, rows(spot * HS, HS), :].astype(F32)
        for i in range(1, NP):
            landed(precv.at[j, i], gp_s.at[j, i], gp_r.at[j, i])
            whole = whole + precv[j, i].astype(F32)
        zsend[j] = whole.astype(BF16)
        if j:
            _, to = in_line(-j)
            push(zsend.at[j], zrecv.at[j], gz_s.at[j], gz_r.at[j], to)

    for j in range(N):
        there, _ = in_line(-j)
        if j:
            for i in range(1, NP):
                near, _ = in_plane(-i)
                landed(ffw.at[there, rows((c * NP + near) * SR, SR)], fp_s.at[j, i], fp_r.at[j, i])
            at = ffw.at[there, rows(c * HR, HR)]
            push(at, at, fm_s.at[j], fm_r.at[j], mate)
            landed(ffw.at[there, rows((1 - c) * HR, HR)], fm_s.at[j], fm_r.at[j])
        up_b = bias[there, 0:1, :]

        def feed(i, carry):
            at = rows(i * TL, TL, 128)
            upper = dot(second[at, :], ffw[there, 0:D, :]) + up_b
            square = upper * upper
            t = jnp.tanh(upper * (GELU_A + (GELU_A * GELU_B) * square))
            one = 0.5 + 0.5 * t
            low = (upper * one).astype(BF16)
            active[at, :] = low
            slope_here = one + (0.5 * upper) * (1.0 - t * t) * (
                GELU_A + (3.0 * GELU_A * GELU_B) * square
            )
            acc[at, :] = acc[at, :] + dot(low, ffw[there, D : D + FL, :])
            back = (dot_nt(cot[at, :], ffw[there, D : D + FL, :]) * slope_here).astype(BF16)
            ugrad[at, :] = back
            sgrad[at, :] = sgrad[at, :] + dot_nt(back, ffw[there, 0:D, :])
            return carry

        lax.fori_loop(0, T // TL, feed, 0)
        sp[pl.ds(8 + there, 1), :] = jnp.sum(ugrad[...].astype(F32), axis=0, keepdims=True)
        gsend[j, 0:D, :] = dot_tn(second[...], ugrad[...]).astype(BF16)
        gsend[j, D : D + FL, :] = dot_tn(active[...], cot[...]).astype(BF16)
        core_start(j)
        if j:
            plane_start(j - 1)

    delta[...] = acc[...].astype(BF16)
    outd[n] = delta[:, rows(n * CW, CW, 128)]
    for j in range(1, N):
        there, to = in_line(j)
        push(delta.at[:, rows(there * CW, CW, 128)], outd.at[n], od_s.at[j], od_r.at[j], to)

    zero_row = jnp.zeros((1, D), F32)

    def norm_two_back(i, carry):
        at = rows(i * 128, 128, 128)
        unit, inverse = norm_stats(hid[at, :])
        grad = sgrad[at, :]
        scaled = grad * gain_two
        back = inverse * (
            scaled
            - jnp.mean(scaled, axis=1, keepdims=True)
            - unit * jnp.mean(scaled * unit, axis=1, keepdims=True)
        )
        top_grad = cot[at, :].astype(F32)
        whole = top_grad + back
        hgrad[at, :] = whole
        hgb[at, :] = whole.astype(BF16)
        parts = (grad * unit, grad, whole, top_grad)
        return tuple(a + jnp.sum(b, axis=0, keepdims=True) for a, b in zip(carry, parts))

    sums = lax.fori_loop(0, T // 128, norm_two_back, (zero_row,) * 4)
    sp[3:4, :] = sums[0]
    sp[4:5, :] = sums[1]
    sp[2:3, :] = sums[2]
    sp[5:6, :] = sums[3]

    plane_start(N - 1)

    gqo[1] = dot(mixg[...], hgb[...]).astype(BF16)
    qt[...] = dot_nt(wo[...], hgb[...])
    gate_grad = [jnp.zeros((1, T), F32), jnp.zeros((1, T), F32)]
    for part in range(N):
        picked_rows = [jnp.zeros((HP, T), F32), jnp.zeros((HP, T), F32)]
        for at in range(NE):
            for i in range(LE):
                lo = expert_rows(at, i, part)
                one = qt[lo : lo + HP, :]
                x = at * LE + i
                for k in range(2):
                    picked_rows[k] = picked_rows[k] + one * hot[k][x : x + 1, :]
        for k in range(2):
            span = slice(part * HP, (part + 1) * HP)
            rounded_mix = mix[k, span, :].astype(BF16).astype(F32)
            gate_grad[k] = gate_grad[k] + jnp.sum(picked_rows[k] * rounded_mix, axis=0, keepdims=True)
            mgk[k, span, :] = (picked_rows[k] * gate[k]).astype(BF16)
    middle = gate[0] * gate_grad[0] + gate[1] * gate_grad[1]
    logit_grad = sum(hot[k] * (gate[k] * (gate_grad[k] - middle)) for k in range(2))
    logit_low = logit_grad.astype(BF16)

    def attend_back(k):
        for i in range(tiles):
            at = pl.ds(i * TL, TL)
            low = prob[k, :, at]
            p = low.astype(F32)
            prob_grad = dot(vn[...], mgk[k, :, at])
            inner = jnp.sum(p * prob_grad, axis=0, keepdims=True)
            score = (p * (prob_grad - inner)).astype(BF16)
            dq[k, :, at] = (dot(kt[...], score) * scale).astype(BF16)
            key_part = dot_nt(score, qk[k, :, at])
            value_part = dot_nt(low, mgk[k, :, at])
            if k == 0 and i == 0:
                dk[...] = key_part
                dv[...] = value_part
            else:
                dk[...] = dk[...] + key_part
                dv[...] = dv[...] + value_part

    attend_back(0)
    for j in range(N):
        line_start(j)
    attend_back(1)

    H, PC = z.reach, z.piece
    offsets = [o for o in range(-H, H + 1) if o]
    inside = T >= LONGEST

    def halo_source(o):
        if inside:
            return (spot_in_row + 1) * T - ws if o > 0 else spot_in_row * T - LONGEST - ws
        return (spot_in_row + o) * T - ws

    def halo_copy(s, o):
        to = rem(here + o + G, G)
        return pltpu.make_async_remote_copy(
            src_ref=halo_out.at[s],
            dst_ref=halo_in.at[s],
            send_sem=hl_s.at[s],
            recv_sem=hl_r.at[s],
            device_id=(d, lax.div(to, N), rem(to, N)),
            device_id_type=MESH,
        )

    for s, o in enumerate(offsets):
        valid = jnp.logical_and(spot_in_row + o >= 0, spot_in_row + o < z.per_row)

        @pl.when(valid)
        def _(s=s, o=o):
            at = rows(halo_source(o), PC, 128)
            halo_out[s, 0] = (dk[at, :] * scale).astype(BF16)
            halo_out[s, 1] = dv[at, :].astype(BF16)
            halo_copy(s, o).start()

    for part in range(N):
        for at in range(NE):
            for i in range(LE):
                lo = expert_rows(at, i, part)
                x = at * LE + i
                span = slice(part * HP, (part + 1) * HP)
                one = dq[0, span, :].astype(F32) * hot[0][x : x + 1, :]
                one = one + dq[1, span, :].astype(F32) * hot[1][x : x + 1, :]
                dqt[lo : lo + HP, :] = one.astype(BF16)
    gqo[0] = dot(dqt[...], rw[own, :]).astype(BF16)
    push(gqo.at[1 - c], cqo, qc_s.at[0], qc_r.at[0], mate)
    ones = jnp.ones((8, T), BF16)
    sp[6:7, :] = dot_nt(ones, dqt[...])[0:1, :]
    sp[7:8, :] = jnp.zeros((1, D), F32)
    sp[7:8, 0 : z.experts] = jnp.transpose(
        jnp.broadcast_to(jnp.sum(logit_grad, axis=1, keepdims=True), (z.experts, 128))
    )[0:1, :]
    acc[...] = dot_tn(dqt[...], wq[...]) + dot_tn(logit_low, r_ref[...])
    sp[16:24, :] = dot(logit_low, rw[own, :])

    whole = zsend[0].astype(F32)
    for j in range(1, N):
        landed(zrecv.at[j], gz_s.at[j], gz_r.at[j])
        whole = whole + zrecv[j].astype(F32)
    fin_at = rows(c * HR + spot * HS, HS)
    fin[fin_at, :] = whole.astype(BF16)
    for i in range(1, NP):
        _, to = in_plane(i)
        push(fin.at[fin_at], fin.at[fin_at], ga_s.at[i], ga_r.at[i], to)

    dk[...] = dk[...] * scale
    for s, o in enumerate(offsets):
        back_valid = jnp.logical_and(spot_in_row - o >= 0, spot_in_row - o < z.per_row)

        @pl.when(back_valid)
        def _(s=s, o=o):
            halo_copy(s, o).wait_recv()
            at = off if (not inside or o > 0) else off + T - LONGEST
            at = rows(at, PC, 128)
            dk[at, :] = dk[at, :] + halo_in[s, 0].astype(F32)
            dv[at, :] = dv[at, :] + halo_in[s, 1].astype(F32)

    key_grad = dk[own, :]
    value_grad = dv[own, :]
    key_low, value_low = key_grad.astype(BF16), value_grad.astype(BF16)
    gkv[0] = dot_tn(key_low, rw[own, :]).astype(BF16)
    gkv[1] = dot_tn(value_low, rw[own, :]).astype(BF16)
    push(gkv.at[1 - c], ckv, qc_s.at[1], qc_r.at[1], mate)
    sp[15:16, :] = jnp.zeros((1, D), F32)
    sp[15:16, 0:HEAD] = jnp.sum(value_grad, axis=0, keepdims=True)
    acc[...] = acc[...] + dot(key_low, wk[...]) + dot(value_low, wv[...])

    def norm_one_back(i, carry):
        at = rows(i * 128, 128, 128)
        unit, inverse = norm_stats(xw[rows(off + i * 128, 128, 128), :])
        grad = acc[at, :]
        scaled = grad * gain_one
        back = inverse * (
            scaled
            - jnp.mean(scaled, axis=1, keepdims=True)
            - unit * jnp.mean(scaled * unit, axis=1, keepdims=True)
        )
        ig_ref[at, :] = hgrad[at, :] + back
        parts = (grad * unit, grad)
        return tuple(a + jnp.sum(b, axis=0, keepdims=True) for a, b in zip(carry, parts))

    sums = lax.fori_loop(0, T // 128, norm_one_back, (zero_row,) * 2)
    sp[0:1, :] = sums[0]
    sp[1:2, :] = sums[1]
    for j in range(8 + N, 15):
        sp[j : j + 1, :] = zero_row
    push(sp, csp, qc_s.at[2], qc_r.at[2], mate)

    YW = D // NY
    ER = N * R
    landed(cqo, qc_s.at[0], qc_r.at[0])
    pqo[...] = (gqo[c].astype(F32) + cqo[...].astype(F32)).astype(BF16)
    for i in range(1, NP):
        there, to = in_plane(i)
        src = pqo.at[rows(rem(there, NE) * ER, ER), rows(lax.div(there, NE) * YW, YW, 128)]
        push(src, rqo.at[i], qp_s.at[0, i], qp_r.at[0, i], to)
    landed(ckv, qc_s.at[1], qc_r.at[1])
    pkv[...] = (gkv[c].astype(F32) + ckv[...].astype(F32)).astype(BF16)
    for i in range(1, NP):
        _, to = in_plane(i)
        push(pkv, rkv.at[i], qp_s.at[1, i], qp_r.at[1, i], to)
    landed(csp, qc_s.at[2], qc_r.at[2])
    psp[...] = sp[...] + csp[...]
    for i in range(1, NP):
        _, to = in_plane(i)
        push(psp, rsp.at[i], qp_s.at[2, i], qp_r.at[2, i], to)

    for i in range(1, NP):
        near, _ = in_plane(-i)
        landed(fin.at[rows(c * HR + near * HS, HS)], ga_s.at[i], ga_r.at[i])
    at = fin.at[rows(c * HR, HR)]
    push(at, at, ga_s.at[0], ga_r.at[0], mate)

    whole = pqo[rows(e * ER, ER), rows(y * YW, YW, 128)].astype(F32)
    for i in range(1, NP):
        landed(rqo.at[i], qp_s.at[0, i], qp_r.at[0, i])
        whole = whole + rqo[i].astype(F32)
    zqo[...] = whole.astype(BF16)
    for j in range(1, N):
        there, to = in_line(j)
        push(zqo.at[rows(there * R, R)], yqo.at[j], qz_s.at[0, j], qz_r.at[0, j], to)
    whole = pkv[...].astype(F32)
    for i in range(1, NP):
        landed(rkv.at[i], qp_s.at[1, i], qp_r.at[1, i])
        whole = whole + rkv[i].astype(F32)
    zkv[...] = whole.astype(BF16)
    for j in range(1, N):
        there, to = in_line(j)
        push(zkv.at[rows(there * HP, HP)], ykv.at[j], qz_s.at[1, j], qz_r.at[1, j], to)
    whole = psp[...]
    for i in range(1, NP):
        landed(rsp.at[i], qp_s.at[2, i], qp_r.at[2, i])
        whole = whole + rsp[i]
    zsp[...] = whole
    for j in range(1, N):
        _, to = in_line(j)
        push(zsp, ysp.at[j], qz_s.at[2, j], qz_r.at[2, j], to)

    for j in range(1, N):
        there, _ = in_line(-j)
        landed(outd.at[there], od_s.at[j], od_r.at[j])
    cols_copy.wait()
    for j in range(N):
        out_ref[j * T : (j + 1) * T, :] = xcols[j * T : (j + 1) * T, :] + outd[j].astype(F32)

    landed(fin.at[rows((1 - c) * HR, HR)], ga_s.at[0], ga_r.at[0])
    gup_ref[...] = fin[0:D, :].astype(F32)
    gdown_ref[...] = fin[D : D + FL, :].astype(F32)

    whole = zqo[rows(n * R, R), :].astype(F32)
    for j in range(1, N):
        landed(yqo.at[j], qz_s.at[0, j], qz_r.at[0, j])
        whole = whole + yqo[j].astype(F32)
    my_cols = rows(y * YW, YW, 128)
    fqo[c, :, my_cols] = whole.astype(BF16)
    for i in range(1, NY):
        _, to = in_rows(i)
        at = fqo.at[c, :, my_cols]
        push(at, at, qa_s.at[0, i], qa_r.at[0, i], to)
    whole = zkv[rows(n * HP, HP), :].astype(F32)
    for j in range(1, N):
        landed(ykv.at[j], qz_s.at[1, j], qz_r.at[1, j])
        whole = whole + ykv[j].astype(F32)
    fkv[c] = whole.astype(BF16)
    push(fkv.at[c], fkv.at[c], qa_s.at[1, 0], qa_r.at[1, 0], mate)
    whole = zsp[...]
    for j in range(1, N):
        landed(ysp.at[j], qz_s.at[2, j], qz_r.at[2, j])
        whole = whole + ysp[j]
    small_ref[...] = whole
    for i in range(1, NY):
        near, _ = in_rows(-i)
        landed(fqo.at[c, :, rows(near * YW, YW, 128)], qa_s.at[0, i], qa_r.at[0, i])
    push(fqo.at[c], fqo.at[c], qa_s.at[0, 0], qa_r.at[0, 0], mate)
    landed(fkv.at[1 - c], qa_s.at[1, 0], qa_r.at[1, 0])
    gk_ref[...] = fkv[0].astype(F32)
    gv_ref[...] = fkv[1].astype(F32)
    landed(fqo.at[1 - c], qa_s.at[0, 0], qa_r.at[0, 0])
    gq_ref[...] = fqo[0].astype(F32)
    go_ref[...] = fqo[1].astype(F32)

    for copy in started:
        copy.wait_send()
    for s, o in enumerate(offsets):
        valid = jnp.logical_and(spot_in_row + o >= 0, spot_in_row + o < z.per_row)

        @pl.when(valid)
        def _(s=s, o=o):
            halo_copy(s, o).wait_send()


def run(z, x, seg, chosen, vec, q, k, v, o, r, up, down, cot):
    N, G, NP, NY = z.narrow, z.group, z.plane, z.rows_y
    T, W, D, R, HP = z.block, z.window, z.width, z.shard, z.head_part
    FL = z.ff_local
    FR = D + FL
    HR = FR // 2
    HS = HR // NP
    YW = D // NY
    ER = N * R
    QR = G * R
    S = 2 * z.reach
    SMALL = z.small_rows
    vmem = pl.BlockSpec(memory_space=pltpu.VMEM)
    anywhere = pl.BlockSpec(memory_space=pl.ANY)
    scratch = [
        ((W, D), F32),
        ((N * T, D // N), F32),
        ((W, D), BF16),
        ((QR, D), BF16),
        ((QR, D), BF16),
        ((HEAD, D), BF16),
        ((HEAD, D), BF16),
        ((G, 8, D), F32),
        ((N, FR, D), BF16),
        ((T, D), BF16),
        ((8, z.row_len), F32),
        ((W, 8), F32),
        ((W, HEAD), BF16),
        ((W, HEAD), BF16),
        ((HEAD, W), BF16),
        ((HEAD, W), BF16),
        ((QR, T), F32),
        ((2, HEAD, T), BF16),
        ((2, W, T), BF16),
        ((2, HEAD, T), F32),
        ((QR, T), BF16),
        ((T, D), F32),
        ((T, D), F32),
        ((T, D), BF16),
        ((T, FL), BF16),
        ((T, FL), BF16),
        ((T, D), F32),
        ((T, D), F32),
        ((T, D), BF16),
        ((2, HEAD, T), BF16),
        ((W, HEAD), F32),
        ((W, HEAD), F32),
        ((2, HEAD, T), BF16),
        ((QR, T), BF16),
        ((max(S, 1), 2, z.piece, HEAD), BF16),
        ((max(S, 1), 2, z.piece, HEAD), BF16),
        ((T, D), BF16),
        ((N, T, D // N), BF16),
        ((N, FR, D), BF16),
        ((N, HR, D), BF16),
        ((N, HR, D), BF16),
        ((N, NP, HS, D), BF16),
        ((N, HS, D), BF16),
        ((N, HS, D), BF16),
        ((FR, D), BF16),
        ((2, QR, D), BF16),
        ((QR, D), BF16),
        ((QR, D), BF16),
        ((NP, ER, YW), BF16),
        ((ER, YW), BF16),
        ((N, R, YW), BF16),
        ((2, R, D), BF16),
        ((2, HEAD, D), BF16),
        ((HEAD, D), BF16),
        ((HEAD, D), BF16),
        ((NP, HEAD, D), BF16),
        ((HEAD, D), BF16),
        ((N, HP, D), BF16),
        ((2, HP, D), BF16),
        ((SMALL, D), F32),
        ((SMALL, D), F32),
        ((SMALL, D), F32),
        ((NP, SMALL, D), F32),
        ((SMALL, D), F32),
        ((N, SMALL, D), F32),
    ]
    pairs = [
        (G,),
        (G,),
        (2, N),
        (G,),
        (2, G),
        (N,),
        (N, NP),
        (N,),
        (N,),
        (N,),
        (max(S, 1),),
        (N,),
        (N, NP),
        (N,),
        (NP,),
        (3,),
        (3, NP),
        (3, N),
        (2, NY),
    ]
    sems = [pltpu.SemaphoreType.DMA((4,))]
    for shape in pairs:
        sems += [pltpu.SemaphoreType.DMA(shape)] * 2
    outs = [
        ((N * T, D // N), F32),
        ((T, D), F32),
        ((R, D), F32),
        ((R, D), F32),
        ((HP, D), F32),
        ((HP, D), F32),
        ((D, FL), F32),
        ((FL, D), F32),
        ((SMALL, D), F32),
    ]
    return pl.pallas_call(
        functools.partial(kernel, z),
        out_shape=[jax.ShapeDtypeStruct(s, t) for s, t in outs],
        in_specs=[anywhere] + [vmem] * 8 + [anywhere] * 2 + [vmem],
        out_specs=[vmem] * len(outs),
        scratch_shapes=[pltpu.VMEM(s, t) for s, t in scratch] + sems,
        compiler_params=pltpu.CompilerParams(
            collective_id=0, has_side_effects=True, vmem_limit_bytes=60 * 2**20
        ),
        name="layer",
    )(x, seg, chosen, vec, q, k, v, o, r, up, down, cot)


def per_device(
    inputs,
    seg_ids,
    chosen,
    gain_one,
    shift_one,
    query_w,
    query_b,
    key_w,
    value_w,
    value_b,
    out_w,
    out_b,
    router_w,
    router_b,
    gain_two,
    shift_two,
    up_w,
    up_b,
    down_w,
    down_b,
    cotangent,
):
    narrow = lax.axis_size("narrow")
    e, n = lax.axis_index("expert"), lax.axis_index("narrow")
    z = Sizes(
        lax.axis_size("dp"),
        lax.axis_size("expert"),
        narrow,
        inputs.shape[0],
        inputs.shape[1],
        seg_ids.shape[1],
        query_w.shape[0],
        up_w.shape[1],
    )
    D, R, HP = z.width, z.shard, z.head_part
    zero = jnp.zeros((D,), F32)
    spread = jnp.where(
        jnp.arange(HEAD) // HP == n, jnp.tile(value_b, narrow), 0.0
    )
    vec = jnp.stack(
        [
            gain_one,
            shift_one,
            out_b,
            gain_two,
            shift_two,
            down_b,
            zero,
            zero,
            up_b,
            jnp.pad(query_b.reshape(-1), (0, D - R)),
            jnp.pad(spread, (0, D - HEAD)),
            zero,
            zero,
            zero,
            zero,
            zero,
        ]
    )
    vec = jnp.concatenate([vec, jnp.broadcast_to(router_b[:, None], (z.experts, D))])
    out, ig, gq, go, gk, gv, gup, gdown, small = run(
        z,
        inputs,
        seg_ids,
        jnp.transpose(chosen),
        vec,
        jnp.transpose(query_w, (0, 2, 1)).reshape(R, D),
        jnp.transpose(key_w),
        jnp.transpose(value_w),
        out_w.reshape(R, D),
        jnp.transpose(router_w),
        up_w,
        down_w,
        cotangent,
    )
    up_b_grad = lax.dynamic_index_in_dim(small[8 : 8 + narrow], n, 0, keepdims=False)
    query_b_grad = lax.dynamic_slice_in_dim(small[6], (e * narrow + n) * R, R).reshape(query_b.shape)
    value_b_grad = lax.dynamic_slice_in_dim(small[15], n * HP, HP)
    return (
        out,
        ig,
        small[0],
        small[1],
        jnp.transpose(gq.reshape(z.local_experts, HP, D), (0, 2, 1)),
        query_b_grad,
        jnp.transpose(gk),
        jnp.transpose(gv),
        value_b_grad,
        go.reshape(z.local_experts, HP, D),
        small[2],
        jnp.transpose(small[16 : 16 + z.experts]),
        small[7, : z.experts],
        small[3],
        small[4],
        gup,
        up_b_grad,
        gdown,
        small[5],
    )


def solution(mesh):
    return jax.shard_map(
        per_device,
        mesh=mesh,
        in_specs=(
            P("dp", None),
            P("dp", None),
            P("dp", None),
            P(),
            P(),
            P("expert", None, "narrow"),
            P("expert", "narrow"),
            P(None, "narrow"),
            P(None, "narrow"),
            P("narrow"),
            P("expert", "narrow", None),
            P(),
            P(),
            P(),
            P(),
            P(),
            P(None, "narrow"),
            P("narrow"),
            P("narrow", None),
            P(),
            P(("dp", "expert"), "narrow"),
        ),
        out_specs=(
            P(("dp", "expert"), "narrow"),
            P(("dp", "expert", "narrow"), None),
            P(),
            P(),
            P("expert", None, "narrow"),
            P("expert", "narrow"),
            P(None, "narrow"),
            P(None, "narrow"),
            P("narrow"),
            P("expert", "narrow", None),
            P(),
            P(),
            P(),
            P(),
            P(),
            P(None, "narrow"),
            P("narrow"),
            P("narrow", None),
            P(),
        ),
        check_vma=False,
    )
```

time: 1020 us -> 147 us (0.14)
  waiting for transfers between devices: 486 us -> 0 us
  matrix products: 232 us -> 0 us
  other arithmetic: 132 us -> 0.01 us
  Pallas kernels: 0 us -> 119 us
  blocking collectives: 96.1 us -> 0 us
  local copies, waits for them, and re-layouts: 47.6 us -> 27.2 us
  between operations: 15.8 us -> 0.7 us
    psum x6 -> x0, waiting for transfers between devices: 316 us -> none  [the longest x1 154 us: per_device(): lax.psum(gated.astype(jnp.bfloat16), ('expert', 'narrow'))]
    dot_general x44 -> x0, matrix products: 231 us -> none  [the longest x4 45.1 us: per_device(): jnp.einsum('esh,kh->esk', grad_full[:, row_lower:row_lower + row_len], va...]
    pallas_call x0 -> x1, Pallas kernels: none -> 119 us  [run(): pl.pallas_call(functools.partial(kernel, z), out_shape=[jax.ShapeDtypeStr...]
    all_gather x4 -> x0, waiting for transfers between devices: 109 us -> none  [the longest x1 55.4 us: per_device(): lax.all_gather(hidden_rows_grad.astype(jnp.bfloat16), 'expert', axis=0, t...]
    convert_element_type x13 -> x0, other arithmetic: 60.7 us -> none  [the longest x4 47.3 us: per_device(): score_grad = (probability * (prob_grad - row_delta)).astype(jnp.bfloat16)]
    reduce_scatter x1 -> x0, waiting for transfers between devices: 60.5 us -> none  [per_device(): lax.psum_scatter(normed_part.astype(jnp.bfloat16), ('expert', 'narrow'),...]
    reduce_sum x20 -> x0, other arithmetic: 54.5 us -> none  [the longest x1 14.9 us: per_device(): gate_local = jnp.transpose(jnp.sum(hidden_grad[None] * projected, axis=2))]
    psum x2 -> x0, blocking collectives: 51.3 us -> none  [the longest x1 40.4 us: per_device(): lax.psum((gain_one_part, shift_one_part), ('dp', 'expert', 'narrow'))]
  transfers between devices with their start and end apart: 12 -> 0, of which waited for: 8 -> 0; matrix products, arithmetic and copies ran while one was open for 26% -> 0% of each run, Pallas kernels for 0% -> 0%
where the time goes in v1:
time: 147 us; the launch traced here: 146 us
  Pallas kernels  119 us (81%)
  local copies, waits for them, and re-layouts  27.2 us (19%)
    pallas_call x1, Pallas kernels, run(): pl.pallas_call(functools.partial(kernel, z), out_shape=[jax.ShapeDtypeStr...  119 us
    unnamed x8, local copies, waits for them, and re-layouts  14.9 us
    concatenate x3, local copies, waits for them, and re-layouts, per_device(): jnp.concatenate([vec, jnp.broadcast_to(router_b[:, None], (z.experts, D))])  3.31 us

profile of v1, /device:TPU:0, one launch (start us, length us, event | category | flops | bytes accessed | tf_op | source)
XLA Modules:
  0.0 146.4 jit_solution(2649838357995232182)
XLA Ops:
  0.7 0.7 tile.4
  1.3 0.1 tile.10
  1.4 0.7 broadcast_in_dim.11
  2.1 0.8 reshape.61
  2.9 3.3 %concatenate.11.vec_ref = f32[24,512]{1,0:T(8,128)} concatenate(f32[1,512]{1,0:T(1,128)} %bitcast.48, f32[1,512]{1,0:T(1,128)} %bitcast.49, f32[1,512]{1,0:T(1,128)} %bitcast.50, f32[1,512]{1,0:T(1,128)} %bitcast.51, f32[1,512]{1,0:T(1,128)} %bitcast.52, f32[1,512]{1,0:T(1,128)} %bitcast.53, f32[2,512]{1,0:T(2,128)S(1)} %concatenate.9, f32[1,512]{1,0:T(1,128)} %bitcast.54, ...), dimensions={0} | concatenate | bytes 98304 | tf_op jit(solution)/shard_map/concatenate | solution.py:994
  6.2 118.5 %layer.1 = (f32[2048,128]{1,0:T(8,128)}, f32[512,512]{1,0:T(8,128)}, f32[64,512]{1,0:T(8,128)}, f32[64,512]{1,0:T(8,128)}, f32[16,512]{1,0:T(8,128)}, /*index=5*...) custom-call(f32[4096,512]{1,0:T(8,128)} %x_any.1, s32[4,1024]{1,0:T(4,128)} %seg_ref.1, ...), custom_call_target="tpu_custom_call" | custom-call | tf_op jit(solution)/shard_map/layer/pallas_call | solution.py:921
  124.8 1.6 %fusion.2 = (f32[1,512]{1,0:T(1,128)}, f32[1,512]{1,0:T(1,128)}, f32[1,512]{1,0:T(1,128)}, f32[1,512]{1,0:T(1,128)}, f32[1,512]{1,0:T(1,128)S(1)}, /*index=5*/f3...) fusion(f32[24,512]{1,0:T(8,128)} %get-tuple-element.30), kind=kLoop, calls=%fused_computation.12 | loop fusion | bytes 32768 | tf_op jit(solution)/shard_map/slice | solution.py:1032
  126.4 0.1 fusion
  126.4 0.7 reshape.65
  127.1 0.6 fusion.1
  127.7 0.7 slice.42
  128.4 0.6 constant_dynamic-slice_fusion
  129.0 1.3 slice_bitcast_fusion
  130.3 1.2 slice_bitcast_fusion.1
  131.5 2.3 %copy.48 = f32[2048,128]{1,0:T(8,128)} copy(f32[2048,128]{1,0:T(8,128)} %get-tuple-element.64) | data formatting | bytes 2097152
  133.8 2.3 %copy.49 = f32[512,512]{1,0:T(8,128)} copy(f32[512,512]{1,0:T(8,128)} %get-tuple-element.65) | data formatting | bytes 2097152
  136.0 1.6 %copy.50 = f32[4,512,16]{1,2,0:T(8,128)} copy(f32[4,512,16]{1,2,0:T(8,128)} %bitcast.37) | data formatting | bytes 262144
  137.6 1.4 copy.51
  139.0 1.4 copy.52
  140.3 1.6 %copy.53 = f32[4,16,512]{2,1,0:T(8,128)} copy(f32[4,16,512]{2,1,0:T(8,128)} %bitcast.36) | data formatting | bytes 262144
  141.9 2.3 %copy.54 = f32[512,512]{1,0:T(8,128)} copy(f32[512,512]{1,0:T(8,128)} %get-tuple-element.79) | data formatting | bytes 2097152
  144.2 2.3 %copy.55 = f32[512,512]{1,0:T(8,128)} copy(f32[512,512]{1,0:T(8,128)} %get-tuple-element.81) | data formatting | bytes 2097152
  (6 shorter events, 0.0 us)

commit v2 on v1

v2 whole, which is shorter than its diff:
```python
import functools
import math

import jax
import jax.numpy as jnp
from jax import lax
from jax.experimental import pallas as pl
from jax.experimental.pallas import tpu as pltpu
from jax.sharding import PartitionSpec as P

HEAD = 64
LONGEST = 256
EPSILON = 1e-05
MASKED = -1000000000.0
GELU_A = math.sqrt(2.0 / math.pi)
GELU_B = 0.044715
F32 = jnp.float32
BF16 = jnp.bfloat16
MESH = pl.DeviceIdType.MESH


def dot(a, b):
    return lax.dot_general(a, b, (((1,), (0,)), ((), ())), preferred_element_type=F32)


def dot_nt(a, b):
    return lax.dot_general(a, b, (((1,), (1,)), ((), ())), preferred_element_type=F32)


def dot_tn(a, b):
    return lax.dot_general(a, b, (((0,), (0,)), ((), ())), preferred_element_type=F32)


def norm_stats(x):
    centred = x - jnp.mean(x, axis=1, keepdims=True)
    inverse = lax.rsqrt(jnp.mean(centred * centred, axis=1, keepdims=True) + EPSILON)
    return centred * inverse, inverse


def rem(a, b):
    return lax.rem(a, b)


class Sizes:
    def __init__(self, dp, expert, narrow, tokens, width, row_len, local_experts, ff_local):
        self.dp, self.expert, self.narrow = dp, expert, narrow
        self.tokens, self.width, self.row_len = tokens, width, row_len
        self.local_experts = local_experts
        self.experts = local_experts * expert
        self.group = expert * narrow
        self.block = tokens // self.group
        self.rows_y = dp // 2
        self.plane = self.rows_y * expert
        self.ff_local = ff_local
        self.head_part = HEAD // narrow
        self.shard = local_experts * self.head_part
        self.per_row = row_len // self.block
        spans = [
            min(row_len, (j + 1) * self.block + LONGEST) - max(0, j * self.block - LONGEST)
            for j in range(self.per_row)
        ]
        self.window = max(spans)
        self.reach = max(1, LONGEST // self.block) if self.per_row > 1 else 0
        self.piece = min(self.block, LONGEST)
        self.tile = min(256, self.block)
        self.up_rows = narrow * ff_local // width
        self.small_rows = 24


def kernel(
    z,
    x_any,
    seg_ref,
    chosen_ref,
    g1_ref,
    s1_ref,
    ob_ref,
    g2_ref,
    s2_ref,
    db_ref,
    ub_ref,
    qb_ref,
    vb_ref,
    rb_ref,
    q_ref,
    k_ref,
    v_ref,
    o_ref,
    r_ref,
    up_any,
    down_any,
    cot_ref,
    out_ref,
    ig_ref,
    fin_ref,
    fqo_ref,
    small_ref,
    xw,
    rw,
    wq,
    wo,
    wkv,
    bias,
    corner,
    vcol,
    ffw,
    cot,
    segs,
    segc,
    kn,
    vn,
    kt,
    vt,
    qt,
    qk,
    prob,
    mix,
    mixg,
    hid,
    acc,
    second,
    active,
    slope,
    ugrad,
    sgrad,
    hgrad,
    hgb,
    mgk,
    dk,
    dv,
    dq,
    dqt,
    halo_out,
    halo_in,
    delta,
    outd,
    gsend,
    crecv,
    psend,
    pea,
    pya,
    mea,
    mya,
    pyb,
    peb,
    zsend,
    zrecv,
    fin,
    gqo,
    cqo,
    pqo,
    rqo,
    zqo,
    yqo,
    fqo,
    sp,
    csp,
    psp,
    rsp,
    zsp,
    ysp,
    fsp,
    loc_sem,
    w_s,
    w_r,
    wm_s,
    wm_r,
    b_s,
    b_r,
    q_s,
    q_r,
    qm_s,
    qm_r,
    o_s,
    o_r,
    om_s,
    om_r,
    fz_s,
    fz_r,
    fp_s,
    fp_r,
    fm_s,
    fm_r,
    ct_s,
    ct_r,
    od_s,
    od_r,
    hl_s,
    hl_r,
    gc_s,
    gc_r,
    gp_s,
    gp_r,
    gz_s,
    gz_r,
    ga_s,
    ga_r,
    qc_s,
    qc_r,
    qp_s,
    qp_r,
    qz_s,
    qz_r,
    qa_s,
    qa_r,
):
    d, e, n = lax.axis_index("dp"), lax.axis_index("expert"), lax.axis_index("narrow")
    c, y = rem(d, 2), lax.div(d, 2)
    N, G, NP, NE, NY = z.narrow, z.group, z.plane, z.expert, z.rows_y
    T, W, D, R, HP, LE = z.block, z.window, z.width, z.shard, z.head_part, z.local_experts
    FL = z.ff_local
    half = D // 2
    here = e * N + n
    spot = y * NE + e
    mate = (d + 1 - 2 * c, e, n)

    def in_group(j):
        at = rem(here + j + G, G)
        return at, (d, lax.div(at, N), rem(at, N))

    def in_plane(j):
        at = rem(spot + j + NP, NP)
        return at, (2 * lax.div(at, NE) + c, rem(at, NE), n)

    def in_line(j):
        at = rem(n + j + N, N)
        return at, (d, e, at)

    def in_rows(j):
        at = rem(y + j + NY, NY)
        return at, (2 * at + c, e, n)

    started = []

    def push(src, dst, send, recv, device):
        copy = pltpu.make_async_remote_copy(
            src_ref=src,
            dst_ref=dst,
            send_sem=send,
            recv_sem=recv,
            device_id=device,
            device_id_type=MESH,
        )
        copy.start()
        started.append(copy)

    def landed(dst, send, recv):
        pltpu.make_async_remote_copy(
            src_ref=dst,
            dst_ref=dst,
            send_sem=send,
            recv_sem=recv,
            device_id=mate,
            device_id_type=MESH,
        ).wait_recv()

    def rows(start, size, step=16):
        return pl.ds(pl.multiple_of(start, step), size)

    start = here * T
    row = lax.div(start, z.row_len)
    spot_in_row = rem(here, z.per_row)
    base = row * z.row_len
    ws = jnp.minimum(jnp.maximum(spot_in_row * T - LONGEST, 0), z.row_len - W)
    off = spot_in_row * T - ws
    own = rows(off, T, 128)

    x_copy = pltpu.make_async_copy(x_any.at[rows(base + ws, W, 128)], xw, loc_sem.at[0])
    x_copy.start()
    up_copy = pltpu.make_async_copy(up_any, ffw.at[n, pl.ds(0, D)], loc_sem.at[1])
    up_copy.start()
    down_copy = pltpu.make_async_copy(down_any, ffw.at[n, pl.ds(D, FL)], loc_sem.at[2])
    down_copy.start()
    cols_copy = pltpu.make_async_copy(
        x_any.at[rows(e * N * T, N * T, 128), rows(n * (D // N), D // N, 128)], out_ref, loc_sem.at[3]
    )
    cols_copy.start()
    wq[rows(here * R, R)] = q_ref[...]
    wo[rows(here * R, R)] = o_ref[...]
    wkv[0, rows(n * HP, HP)] = k_ref[...]
    wkv[1, rows(n * HP, HP)] = v_ref[...]
    bias[here] = jnp.zeros((16, 128), F32)
    for i in range(FL // 128):
        bias[here, i : i + 1, :] = ub_ref[0:1, i * 128 : (i + 1) * 128]
    bias[here, 8 : 8 + LE, 0:HP] = qb_ref[...]
    bias[here, 7:8, 0:HP] = vb_ref[...]

    barrier = pltpu.get_barrier_semaphore()
    pl.semaphore_signal(barrier, inc=1, device_id=mate, device_id_type=MESH)
    for j in range(1, NP):
        pl.semaphore_signal(barrier, inc=1, device_id=in_plane(j)[1], device_id_type=MESH)
    for j in range(1, G):
        pl.semaphore_signal(barrier, inc=1, device_id=in_group(j)[1], device_id_type=MESH)
    pl.semaphore_wait(barrier, NP + G - 1)

    mine_cols = rows(c * half, half, 128)
    other_cols = rows((1 - c) * half, half, 128)

    def in_expert(i):
        at = rem(e + i + NE, NE)
        return at, (d, at, n)

    def shard_at(i, j):
        return rem(e - i + NE, NE) * N + rem(n - j + N, N)

    def spread_start(part, send, recv):
        for j in range(1, N):
            at = part(here)
            push(at, at, send.at[0, j], recv.at[0, j], in_line(j)[1])
        for i in range(1, NE):
            at = part(here)
            push(at, at, send.at[i, 0], recv.at[i, 0], in_expert(i)[1])

    def spread_on(part, send, recv, to_mate):
        for j in range(1, N):
            at = part(shard_at(0, j))
            landed(at, send.at[0, j], recv.at[0, j])
            for i in range(1, NE):
                push(at, at, send.at[i, j], recv.at[i, j], in_expert(i)[1])
            if to_mate is not None:
                push(at, at, to_mate[0].at[0, j], to_mate[1].at[0, j], mate)

    def spread_end(part, send, recv, to_mate):
        for i in range(1, NE):
            for j in range(N):
                at = part(shard_at(i, j))
                landed(at, send.at[i, j], recv.at[i, j])
                if to_mate is not None:
                    push(at, at, to_mate[0].at[i, j], to_mate[1].at[i, j], mate)

    def spread_wait(part, to_mate):
        for i in range(NE):
            for j in range(N):
                if i or j:
                    landed(part(shard_at(i, j)), to_mate[0].at[i, j], to_mate[1].at[i, j])

    def bias_part(g):
        return bias.at[g]

    def q_part(g):
        return wq.at[rows(g * R, R), mine_cols]

    def q_other(g):
        return wq.at[rows(g * R, R), other_cols]

    def o_part(g):
        return wo.at[rows(g * R, R), mine_cols]

    def o_other(g):
        return wo.at[rows(g * R, R), other_cols]

    for j in range(1, N):
        at = wkv.at[c, rows(n * HP, HP)]
        push(at, at, w_s.at[j], w_r.at[j], in_line(j)[1])
    spread_start(q_part, q_s, q_r)
    spread_start(bias_part, b_s, b_r)
    up_copy.wait()
    down_copy.wait()
    FR = D + FL

    left, right = pl.ds(0, half), pl.ds(half, half)
    HR = FR // 2
    HS = HR // NP
    HA, HB = HR // NE, HR // NY
    near_first = sorted(range(1, N), key=lambda j: (min(j, N - j), j))
    first, last = near_first[: N // 2], near_first[N // 2 :]

    def left_slice(of, ys, es):
        return ffw.at[of, rows(c * HR + (es * NY + ys) * HS, HS), left]

    def right_slice(of, ys, es):
        return ffw.at[of, rows(c * HR + (ys * NE + es) * HS, HS), right]

    def left_half(of, es):
        return ffw.at[of, rows(c * HR + es * HA, HA), left]

    def right_half(of, ys):
        return ffw.at[of, rows(c * HR + ys * HB, HB), right]

    def shard_start(j):
        to = in_line(j)[1]
        at = left_slice(n, y, e)
        push(at, at, fz_s.at[0, j], fz_r.at[0, j], to)
        at = right_slice(n, y, e)
        push(at, at, fz_s.at[1, j], fz_r.at[1, j], to)

    def plane_on(j):
        there, _ = in_line(-j)
        at = left_slice(there, y, e)
        landed(at, fz_s.at[0, j], fz_r.at[0, j])
        for i in range(1, NY):
            push(at, at, fp_s.at[0, j, i], fp_r.at[0, j, i], in_rows(i)[1])
        at = right_slice(there, y, e)
        landed(at, fz_s.at[1, j], fz_r.at[1, j])
        for i in range(1, NE):
            push(at, at, fp_s.at[1, j, i], fp_r.at[1, j, i], in_expert(i)[1])

    def plane_turn(j):
        there, _ = in_line(-j)
        for i in range(1, NY):
            near, _ = in_rows(-i)
            landed(left_slice(there, near, e), fp_s.at[0, j, i], fp_r.at[0, j, i])
        at = left_half(there, e)
        for i in range(1, NE):
            push(at, at, fp_s.at[2, j, i], fp_r.at[2, j, i], in_expert(i)[1])
        for i in range(1, NE):
            near, _ = in_expert(-i)
            landed(right_slice(there, y, near), fp_s.at[1, j, i], fp_r.at[1, j, i])
        at = right_half(there, y)
        for i in range(1, NY):
            push(at, at, fp_s.at[3, j, i], fp_r.at[3, j, i], in_rows(i)[1])

    def mate_on(j):
        there, _ = in_line(-j)
        for i in range(1, NE):
            near, _ = in_expert(-i)
            landed(left_half(there, near), fp_s.at[2, j, i], fp_r.at[2, j, i])
        for i in range(1, NY):
            near, _ = in_rows(-i)
            landed(right_half(there, near), fp_s.at[3, j, i], fp_r.at[3, j, i])
        at = ffw.at[there, rows(c * HR, HR)]
        push(at, at, fm_s.at[j], fm_r.at[j], mate)

    x_copy.wait()
    gain_one, shift_one = g1_ref[...], s1_ref[...]

    def norm_one(i, carry):
        at = rows(i * 128, 128, 128)
        unit, _ = norm_stats(xw[at, :])
        rw[at, :] = (unit * gain_one + shift_one).astype(BF16)
        return carry

    lax.fori_loop(0, W // 128, norm_one, 0)

    seg_all = seg_ref[...].astype(F32)
    row_id = lax.broadcasted_iota(jnp.int32, seg_all.shape, 0)
    seg_here = jnp.sum(jnp.where(row_id == row, seg_all, 0.0), axis=0, keepdims=True)
    segs[...] = jnp.broadcast_to(seg_here, segs.shape)
    segc[...] = jnp.transpose(segs[:, rows(ws, W, 128)])
    seg_own = segs[0:1, rows(spot_in_row * T, T, 128)]
    corner[...] = jnp.zeros_like(corner)
    corner[:, 0 : z.experts] = jnp.broadcast_to(rb_ref[...], (8, z.experts))
    router_col = jnp.transpose(corner[...])[0 : z.experts, 0:1]
    logits = dot_nt(r_ref[...], rw[own, :]) + router_col
    expert_id = lax.broadcasted_iota(jnp.int32, (z.experts, T), 0)
    hot, picked = [], []
    for k in range(2):
        chosen = chosen_ref[k : k + 1, rows(start, T, 128)]
        hot.append((expert_id == chosen).astype(F32))
        picked.append(jnp.sum(logits * hot[k], axis=0, keepdims=True))
    top = jnp.maximum(picked[0], picked[1])
    raised = [jnp.exp(p - top) for p in picked]
    total = raised[0] + raised[1]
    gate = [r / total for r in raised]

    for j in range(1, N):
        there, _ = in_line(-j)
        at = wkv.at[c, rows(there * HP, HP)]
        landed(at, w_s.at[j], w_r.at[j])
        push(at, at, wm_s.at[j], wm_r.at[j], mate)
    spread_on(q_part, q_s, q_r, (qm_s, qm_r))
    spread_on(bias_part, b_s, b_r, None)
    for j in first:
        shard_start(j)
    spread_start(o_part, o_s, o_r)

    for j in range(1, N):
        there, _ = in_line(-j)
        landed(wkv.at[1 - c, rows(there * HP, HP)], wm_s.at[j], wm_r.at[j])
    kn[...] = dot_nt(rw[...], wkv[0]).astype(BF16)
    kt[...] = dot_nt(wkv[0], rw[...]).astype(BF16)
    spread_end(q_part, q_s, q_r, (qm_s, qm_r))
    spread_end(bias_part, b_s, b_r, None)
    columns = [jnp.transpose(bias[g, 0:16, :]) for g in range(G)]
    for part in range(N):
        vcol[part * HP : (part + 1) * HP, :] = jnp.broadcast_to(columns[part][0:HP, 7:8], (HP, 128))
    value_row = jnp.transpose(vcol[...])[0:1, :]
    vn[...] = (dot_nt(rw[...], wkv[1]) + value_row).astype(BF16)
    vt[...] = (dot_nt(wkv[1], rw[...]) + vcol[:, 0:1]).astype(BF16)

    spread_wait(q_other, (qm_s, qm_r))
    qt[...] = dot_nt(wq[...], rw[own, :])

    def expert_rows(at, i, part):
        return ((at * N + part) * LE + i) * HP

    for part in range(N):
        chosen_rows = [jnp.zeros((HP, T), F32), jnp.zeros((HP, T), F32)]
        for at in range(NE):
            g = at * N + part
            for i in range(LE):
                lo = expert_rows(at, i, part)
                one = qt[lo : lo + HP, :] + columns[g][0:HP, 8 + i : 9 + i]
                for k in range(2):
                    chosen_rows[k] = chosen_rows[k] + one * hot[k][at * LE + i : at * LE + i + 1, :]
        for k in range(2):
            qk[k, part * HP : (part + 1) * HP, :] = chosen_rows[k].astype(BF16)

    scale = 1.0 / math.sqrt(HEAD)
    TL = z.tile
    tiles = T // TL
    seg_tiles = [seg_own[:, i * TL : (i + 1) * TL] for i in range(tiles)]

    def attend(k):
        for i in range(tiles):
            at = pl.ds(i * TL, TL)
            scores = dot(kn[...], qk[k, :, at]) * scale
            scores = jnp.where(segc[:, 0:1] == seg_tiles[i], scores, MASKED)
            high = jnp.max(scores, axis=0, keepdims=True)
            raised_scores = jnp.exp(scores - high)
            low = (raised_scores * (1.0 / jnp.sum(raised_scores, axis=0, keepdims=True))).astype(BF16)
            prob[k, :, at] = low
            mix[k, :, at] = dot(vt[...], low)

    for j in last:
        shard_start(j)
    attend(0)
    attend(1)
    plane_on(first[0])
    for j in first[1:]:
        plane_on(j)
    spread_on(o_part, o_s, o_r, (om_s, om_r))
    for j in first:
        plane_turn(j)
    CW = D // N
    cot[:, rows(n * CW, CW, 128)] = cot_ref[rows(n * T, T, 128), :]
    for j in range(1, N):
        there, to = in_line(j)
        push(
            cot_ref.at[rows(there * T, T, 128)],
            cot.at[:, rows(n * CW, CW, 128)],
            ct_s.at[j],
            ct_r.at[j],
            to,
        )
    for j in last:
        plane_on(j)
    spread_end(o_part, o_s, o_r, (om_s, om_r))

    for part in range(N):
        for at in range(NE):
            for i in range(LE):
                lo = expert_rows(at, i, part)
                x = at * LE + i
                gated = jnp.zeros((HP, T), F32)
                for k in range(2):
                    rounded_mix = mix[k, part * HP : (part + 1) * HP, :].astype(BF16).astype(F32)
                    gated = gated + rounded_mix * (hot[k][x : x + 1, :] * gate[k])
                mixg[lo : lo + HP, :] = gated.astype(BF16)
    spread_wait(o_other, (om_s, om_r))
    out_b, down_b = ob_ref[...], db_ref[...]
    gain_two, shift_two = g2_ref[...], s2_ref[...]
    attention = dot_tn(mixg[...], wo[...]) + out_b
    acc[...] = attention + down_b
    hid[...] = xw[own, :] + attention

    def norm_two(i, carry):
        at = rows(i * 128, 128, 128)
        unit, _ = norm_stats(hid[at, :])
        second[at, :] = (unit * gain_two + shift_two).astype(BF16)
        return carry

    lax.fori_loop(0, T // 128, norm_two, 0)
    sgrad[...] = jnp.zeros_like(sgrad)

    def core_start(j):
        push(
            gsend.at[j, rows((1 - c) * HR, HR)], crecv.at[j], gc_s.at[j], gc_r.at[j], mate
        )

    def plane_start(j):
        landed(crecv.at[j], gc_s.at[j], gc_r.at[j])
        psend[j] = (
            gsend[j, rows(c * HR, HR), :].astype(F32) + crecv[j].astype(F32)
        ).astype(BF16)
        for i in range(1, NE):
            there, to = in_expert(i)
            src = psend.at[j, rows(there * HA, HA), left]
            push(src, pea.at[j, i], gp_s.at[0, j, i], gp_r.at[0, j, i], to)
        for i in range(1, NY):
            there, to = in_rows(i)
            src = psend.at[j, rows(there * HB, HB), right]
            push(src, pya.at[j, i], gp_s.at[1, j, i], gp_r.at[1, j, i], to)

    def plane_middle(j):
        whole = psend[j, rows(e * HA, HA), left].astype(F32)
        for i in range(1, NE):
            landed(pea.at[j, i], gp_s.at[0, j, i], gp_r.at[0, j, i])
            whole = whole + pea[j, i].astype(F32)
        mea[j] = whole.astype(BF16)
        for i in range(1, NY):
            there, to = in_rows(i)
            src = mea.at[j, rows(there * HS, HS)]
            push(src, pyb.at[j, i], gp_s.at[2, j, i], gp_r.at[2, j, i], to)
        whole = psend[j, rows(y * HB, HB), right].astype(F32)
        for i in range(1, NY):
            landed(pya.at[j, i], gp_s.at[1, j, i], gp_r.at[1, j, i])
            whole = whole + pya[j, i].astype(F32)
        mya[j] = whole.astype(BF16)
        for i in range(1, NE):
            there, to = in_expert(i)
            src = mya.at[j, rows(there * HS, HS)]
            push(src, peb.at[j, i], gp_s.at[3, j, i], gp_r.at[3, j, i], to)

    def line_start(j):
        whole = mea[j, rows(y * HS, HS), :].astype(F32)
        for i in range(1, NY):
            landed(pyb.at[j, i], gp_s.at[2, j, i], gp_r.at[2, j, i])
            whole = whole + pyb[j, i].astype(F32)
        zsend[j, :, left] = whole.astype(BF16)
        whole = mya[j, rows(e * HS, HS), :].astype(F32)
        for i in range(1, NE):
            landed(peb.at[j, i], gp_s.at[3, j, i], gp_r.at[3, j, i])
            whole = whole + peb[j, i].astype(F32)
        zsend[j, :, right] = whole.astype(BF16)
        if j:
            _, to = in_line(-j)
            push(zsend.at[j], zrecv.at[j], gz_s.at[j], gz_r.at[j], to)

    for step, j in enumerate([0] + near_first):
        there, _ = in_line(-j)
        if j:
            if step == 1:
                mate_on(j)
            if step + 1 < N:
                mate_on(near_first[step])
            landed(ffw.at[there, rows((1 - c) * HR, HR)], fm_s.at[j], fm_r.at[j])
        up_b = jnp.concatenate(
            [bias[e * N + there, i : i + 1, :] for i in range(FL // 128)], axis=1
        )

        def feed(i, carry):
            at = rows(i * TL, TL, 128)
            upper = dot(second[at, :], ffw[there, 0:D, :]) + up_b
            square = upper * upper
            t = jnp.tanh(upper * (GELU_A + (GELU_A * GELU_B) * square))
            one = 0.5 + 0.5 * t
            low = (upper * one).astype(BF16)
            active[j, at, :] = low
            slope[j, at, :] = (
                one + (0.5 * upper) * (1.0 - t * t) * (GELU_A + (3.0 * GELU_A * GELU_B) * square)
            ).astype(BF16)
            acc[at, :] = acc[at, :] + dot(low, ffw[there, D : D + FL, :])
            return carry

        lax.fori_loop(0, T // TL, feed, 0)
        if step == 0:
            for j in last:
                plane_turn(j)
    delta[...] = acc[...].astype(BF16)

    for j in range(1, N):
        there, _ = in_line(-j)
        landed(cot.at[:, rows(there * CW, CW, 128)], ct_s.at[j], ct_r.at[j])


    outd[n] = delta[:, rows(n * CW, CW, 128)]
    for j in range(1, N):
        there, to = in_line(j)
        push(delta.at[:, rows(there * CW, CW, 128)], outd.at[n], od_s.at[j], od_r.at[j], to)

    order = list(range(1, N)) + [0]
    for step, j in enumerate(order):
        there, _ = in_line(-j)

        def feed_back(i, carry):
            at = rows(i * TL, TL, 128)
            back = dot_nt(cot[at, :], ffw[there, D : D + FL, :]) * slope[j, at, :].astype(F32)
            back = back.astype(BF16)
            ugrad[at, :] = back
            sgrad[at, :] = sgrad[at, :] + dot_nt(back, ffw[there, 0:D, :])
            return carry

        lax.fori_loop(0, T // TL, feed_back, 0)
        sp[pl.ds(8 + there, 1), :] = jnp.sum(ugrad[...].astype(F32), axis=0, keepdims=True)
        gsend[j, 0:D, :] = dot_tn(second[...], ugrad[...]).astype(BF16)
        gsend[j, D : D + FL, :] = dot_tn(active[j], cot[...]).astype(BF16)
        core_start(j)
        if step:
            plane_start(order[step - 1])

    zero_row = jnp.zeros((1, D), F32)

    def norm_two_back(i, carry):
        at = rows(i * 128, 128, 128)
        unit, inverse = norm_stats(hid[at, :])
        grad = sgrad[at, :]
        scaled = grad * gain_two
        back = inverse * (
            scaled
            - jnp.mean(scaled, axis=1, keepdims=True)
            - unit * jnp.mean(scaled * unit, axis=1, keepdims=True)
        )
        top_grad = cot[at, :].astype(F32)
        whole = top_grad + back
        hgrad[at, :] = whole
        hgb[at, :] = whole.astype(BF16)
        parts = (grad * unit, grad, whole, top_grad)
        return tuple(a + jnp.sum(b, axis=0, keepdims=True) for a, b in zip(carry, parts))

    sums = lax.fori_loop(0, T // 128, norm_two_back, (zero_row,) * 4)
    sp[3:4, :] = sums[0]
    sp[4:5, :] = sums[1]
    sp[2:3, :] = sums[2]
    sp[5:6, :] = sums[3]

    plane_start(order[N - 1])
    plane_middle(order[0])

    SH = R + HP
    out_grad = dot(mixg[...], hgb[...]).astype(BF16)
    for g in range(G):
        gqo[1, g * SH : g * SH + R, :] = out_grad[g * R : (g + 1) * R, :]
    qt[...] = dot_nt(wo[...], hgb[...])
    gate_grad = [jnp.zeros((1, T), F32), jnp.zeros((1, T), F32)]
    for part in range(N):
        picked_rows = [jnp.zeros((HP, T), F32), jnp.zeros((HP, T), F32)]
        for at in range(NE):
            for i in range(LE):
                lo = expert_rows(at, i, part)
                one = qt[lo : lo + HP, :]
                x = at * LE + i
                for k in range(2):
                    picked_rows[k] = picked_rows[k] + one * hot[k][x : x + 1, :]
        for k in range(2):
            span = slice(part * HP, (part + 1) * HP)
            rounded_mix = mix[k, span, :].astype(BF16).astype(F32)
            gate_grad[k] = gate_grad[k] + jnp.sum(picked_rows[k] * rounded_mix, axis=0, keepdims=True)
            mgk[k, span, :] = (picked_rows[k] * gate[k]).astype(BF16)
    middle = gate[0] * gate_grad[0] + gate[1] * gate_grad[1]
    logit_grad = sum(hot[k] * (gate[k] * (gate_grad[k] - middle)) for k in range(2))
    logit_low = logit_grad.astype(BF16)

    def attend_back(k):
        for i in range(tiles):
            at = pl.ds(i * TL, TL)
            low = prob[k, :, at]
            p = low.astype(F32)
            prob_grad = dot(vn[...], mgk[k, :, at])
            inner = jnp.sum(p * prob_grad, axis=0, keepdims=True)
            score = (p * (prob_grad - inner)).astype(BF16)
            dq[k, :, at] = (dot(kt[...], score) * scale).astype(BF16)
            key_part = dot_nt(score, qk[k, :, at])
            value_part = dot_nt(low, mgk[k, :, at])
            if k == 0 and i == 0:
                dk[...] = key_part
                dv[...] = value_part
            else:
                dk[...] = dk[...] + key_part
                dv[...] = dv[...] + value_part

    attend_back(0)
    attend_back(1)
    plane_middle(order[1])

    H, PC = z.reach, z.piece
    offsets = [o for o in range(-H, H + 1) if o]
    inside = T >= LONGEST

    def halo_source(o):
        if inside:
            return (spot_in_row + 1) * T - ws if o > 0 else spot_in_row * T - LONGEST - ws
        return (spot_in_row + o) * T - ws

    def halo_copy(s, o):
        to = rem(here + o + G, G)
        return pltpu.make_async_remote_copy(
            src_ref=halo_out.at[s],
            dst_ref=halo_in.at[s],
            send_sem=hl_s.at[s],
            recv_sem=hl_r.at[s],
            device_id=(d, lax.div(to, N), rem(to, N)),
            device_id_type=MESH,
        )

    for s, o in enumerate(offsets):
        valid = jnp.logical_and(spot_in_row + o >= 0, spot_in_row + o < z.per_row)

        @pl.when(valid)
        def _(s=s, o=o):
            at = rows(halo_source(o), PC, 128)
            halo_out[s, 0] = (dk[at, :] * scale).astype(BF16)
            halo_out[s, 1] = dv[at, :].astype(BF16)
            halo_copy(s, o).start()

    for part in range(N):
        for at in range(NE):
            for i in range(LE):
                lo = expert_rows(at, i, part)
                x = at * LE + i
                span = slice(part * HP, (part + 1) * HP)
                one = dq[0, span, :].astype(F32) * hot[0][x : x + 1, :]
                one = one + dq[1, span, :].astype(F32) * hot[1][x : x + 1, :]
                dqt[lo : lo + HP, :] = one.astype(BF16)
    query_w_grad = dot(dqt[...], rw[own, :]).astype(BF16)
    key_w_grad = dot_tn((dk[...] * scale).astype(BF16), rw[...]).astype(BF16)
    value_w_grad = dot_tn(dv[...].astype(BF16), rw[...]).astype(BF16)
    for g in range(G):
        shared = slice((g % N) * HP, (g % N + 1) * HP)
        gqo[0, g * SH : g * SH + R, :] = query_w_grad[g * R : (g + 1) * R, :]
        gqo[0, g * SH + R : (g + 1) * SH, :] = key_w_grad[shared, :]
        gqo[1, g * SH + R : (g + 1) * SH, :] = value_w_grad[shared, :]
    push(gqo.at[1 - c], cqo, qc_s.at[0], qc_r.at[0], mate)
    plane_middle(order[2])
    line_start(order[0])
    ones = jnp.ones((8, T), BF16)
    sp[6:7, :] = dot_nt(ones, dqt[...])[0:1, :]
    sp[7:8, :] = jnp.zeros((1, D), F32)
    sp[7:8, 0 : z.experts] = jnp.transpose(
        jnp.broadcast_to(jnp.sum(logit_grad, axis=1, keepdims=True), (z.experts, 128))
    )[0:1, :]
    acc[...] = dot_tn(dqt[...], wq[...]) + dot_tn(logit_low, r_ref[...])
    sp[16:24, :] = dot(logit_low, rw[own, :])
    sp[15:16, :] = jnp.zeros((1, D), F32)
    sp[15:16, 0:HEAD] = jnp.sum(dv[...], axis=0, keepdims=True)
    for j in order[3:]:
        plane_middle(j)
    YW = D // NY
    ER = N * SH
    landed(cqo, qc_s.at[0], qc_r.at[0])
    pqo[...] = (gqo[c].astype(F32) + cqo[...].astype(F32)).astype(BF16)
    for i in range(1, NP):
        there, to = in_plane(i)
        src = pqo.at[rows(rem(there, NE) * ER, ER), rows(lax.div(there, NE) * YW, YW, 128)]
        push(src, rqo.at[i], qp_s.at[0, i], qp_r.at[0, i], to)
    line_start(order[1])

    dk[...] = dk[...] * scale
    for s, o in enumerate(offsets):
        back_valid = jnp.logical_and(spot_in_row - o >= 0, spot_in_row - o < z.per_row)

        @pl.when(back_valid)
        def _(s=s, o=o):
            halo_copy(s, o).wait_recv()
            at = off if (not inside or o > 0) else off + T - LONGEST
            at = rows(at, PC, 128)
            dk[at, :] = dk[at, :] + halo_in[s, 0].astype(F32)
            dv[at, :] = dv[at, :] + halo_in[s, 1].astype(F32)

    key_grad = dk[own, :]
    value_grad = dv[own, :]
    key_low, value_low = key_grad.astype(BF16), value_grad.astype(BF16)
    acc[...] = acc[...] + dot(key_low, wkv[0]) + dot(value_low, wkv[1])

    def norm_one_back(i, carry):
        at = rows(i * 128, 128, 128)
        unit, inverse = norm_stats(xw[rows(off + i * 128, 128, 128), :])
        grad = acc[at, :]
        scaled = grad * gain_one
        back = inverse * (
            scaled
            - jnp.mean(scaled, axis=1, keepdims=True)
            - unit * jnp.mean(scaled * unit, axis=1, keepdims=True)
        )
        ig_ref[at, :] = hgrad[at, :] + back
        parts = (grad * unit, grad)
        return tuple(a + jnp.sum(b, axis=0, keepdims=True) for a, b in zip(carry, parts))

    sums = lax.fori_loop(0, T // 128, norm_one_back, (zero_row,) * 2)
    sp[0:1, :] = sums[0]
    sp[1:2, :] = sums[1]
    for j in range(8 + N, 15):
        sp[j : j + 1, :] = zero_row
    push(sp.at[:, other_cols], csp, qc_s.at[2], qc_r.at[2], mate)
    for j in order[2:]:
        line_start(j)

    landed(csp, qc_s.at[2], qc_r.at[2])
    psp[...] = sp[:, mine_cols] + csp[...]
    for i in range(1, NP):
        _, to = in_plane(i)
        push(psp, rsp.at[i], qp_s.at[2, i], qp_r.at[2, i], to)

    whole = pqo[rows(e * ER, ER), rows(y * YW, YW, 128)].astype(F32)
    for i in range(1, NP):
        landed(rqo.at[i], qp_s.at[0, i], qp_r.at[0, i])
        whole = whole + rqo[i].astype(F32)
    zqo[...] = whole.astype(BF16)
    for j in range(1, N):
        there, to = in_line(j)
        push(zqo.at[rows(there * SH, SH)], yqo.at[j], qz_s.at[0, j], qz_r.at[0, j], to)
    whole = psp[...]
    for i in range(1, NP):
        landed(rsp.at[i], qp_s.at[2, i], qp_r.at[2, i])
        whole = whole + rsp[i]
    zsp[...] = whole
    for j in range(1, N):
        _, to = in_line(j)
        push(zsp, ysp.at[j], qz_s.at[2, j], qz_r.at[2, j], to)

    whole = zsend[0].astype(F32)
    for j in range(1, N):
        landed(zrecv.at[j], gz_s.at[j], gz_r.at[j])
        whole = whole + zrecv[j].astype(F32)

    def fin_left(ys, es):
        return fin.at[rows(c * HR + (es * NY + ys) * HS, HS), left]

    def fin_right(ys, es):
        return fin.at[rows(c * HR + (ys * NE + es) * HS, HS), right]

    fin[rows(c * HR + (e * NY + y) * HS, HS), left] = whole[:, 0:half].astype(BF16)
    fin[rows(c * HR + (y * NE + e) * HS, HS), right] = whole[:, half:].astype(BF16)
    for i in range(1, NP):
        _, to = in_plane(i)
        push(fin_left(y, e), fin_left(y, e), ga_s.at[0, i], ga_r.at[0, i], to)
        push(fin_right(y, e), fin_right(y, e), ga_s.at[1, i], ga_r.at[1, i], to)

    cols_copy.wait()
    for j in range(1, N):
        there, _ = in_line(-j)
        landed(outd.at[there], od_s.at[j], od_r.at[j])
    for j in range(N):
        at = pl.ds(j * T, T)
        out_ref[at, :] = out_ref[at, :] + outd[j].astype(F32)

    whole = zqo[rows(n * SH, SH), :].astype(F32)
    for j in range(1, N):
        landed(yqo.at[j], qz_s.at[0, j], qz_r.at[0, j])
        whole = whole + yqo[j].astype(F32)
    my_cols = rows(y * YW, YW, 128)
    fqo[c, :, my_cols] = whole.astype(BF16)
    for i in range(1, NY):
        _, to = in_rows(i)
        at = fqo.at[c, :, my_cols]
        push(at, at, qa_s.at[0, i], qa_r.at[0, i], to)
    whole = zsp[...]
    for j in range(1, N):
        landed(ysp.at[j], qz_s.at[2, j], qz_r.at[2, j])
        whole = whole + ysp[j]
    fsp[:, mine_cols] = whole
    at = fsp.at[:, mine_cols]
    push(at, at, qa_s.at[2, 0], qa_r.at[2, 0], mate)
    for i in range(1, NY):
        near, _ = in_rows(-i)
        landed(fqo.at[c, :, rows(near * YW, YW, 128)], qa_s.at[0, i], qa_r.at[0, i])
    push(fqo.at[c], fqo.at[c], qa_s.at[0, 0], qa_r.at[0, 0], mate)

    for i in range(1, NP):
        near, _ = in_plane(-i)
        ys, es = lax.div(near, NE), rem(near, NE)
        landed(fin_left(ys, es), ga_s.at[0, i], ga_r.at[0, i])
        landed(fin_right(ys, es), ga_s.at[1, i], ga_r.at[1, i])
    at = fin.at[rows(c * HR, HR)]
    push(at, at, ga_s.at[0, 0], ga_r.at[0, 0], mate)
    landed(fsp.at[:, other_cols], qa_s.at[2, 0], qa_r.at[2, 0])
    small_ref[...] = fsp[...]
    landed(fqo.at[1 - c], qa_s.at[0, 0], qa_r.at[0, 0])
    fqo_ref[...] = fqo[...]
    landed(fin.at[rows((1 - c) * HR, HR)], ga_s.at[0, 0], ga_r.at[0, 0])
    fin_ref[...] = fin[...]

    for copy in started:
        copy.wait_send()
    for s, o in enumerate(offsets):
        valid = jnp.logical_and(spot_in_row + o >= 0, spot_in_row + o < z.per_row)

        @pl.when(valid)
        def _(s=s, o=o):
            halo_copy(s, o).wait_send()


def run(z, x, seg, chosen, vectors, q, k, v, o, r, up, down, cot):
    N, G, NP, NY, NE = z.narrow, z.group, z.plane, z.rows_y, z.expert
    T, W, D, R, HP = z.block, z.window, z.width, z.shard, z.head_part
    FL = z.ff_local
    FR = D + FL
    HR = FR // 2
    HS = HR // NP
    YW = D // NY
    SH = R + HP
    ER = N * SH
    QR = G * R
    GR = G * SH
    S = 2 * z.reach
    SMALL = z.small_rows
    vmem = pl.BlockSpec(memory_space=pltpu.VMEM)
    anywhere = pl.BlockSpec(memory_space=pltpu.HBM)
    scratch = [
        ((W, D), F32),
        ((W, D), BF16),
        ((QR, D), BF16),
        ((QR, D), BF16),
        ((2, HEAD, D), BF16),
        ((G, 16, 128), F32),
        ((8, 128), F32),
        ((HEAD, 128), F32),
        ((N, FR, D), BF16),
        ((T, D), BF16),
        ((8, z.row_len), F32),
        ((W, 8), F32),
        ((W, HEAD), BF16),
        ((W, HEAD), BF16),
        ((HEAD, W), BF16),
        ((HEAD, W), BF16),
        ((QR, T), F32),
        ((2, HEAD, T), BF16),
        ((2, W, T), BF16),
        ((2, HEAD, T), F32),
        ((QR, T), BF16),
        ((T, D), F32),
        ((T, D), F32),
        ((T, D), BF16),
        ((N, T, FL), BF16),
        ((N, T, FL), BF16),
        ((T, FL), BF16),
        ((T, D), F32),
        ((T, D), F32),
        ((T, D), BF16),
        ((2, HEAD, T), BF16),
        ((W, HEAD), F32),
        ((W, HEAD), F32),
        ((2, HEAD, T), BF16),
        ((QR, T), BF16),
        ((max(S, 1), 2, z.piece, HEAD), BF16),
        ((max(S, 1), 2, z.piece, HEAD), BF16),
        ((T, D), BF16),
        ((N, T, D // N), BF16),
        ((N, FR, D), BF16),
        ((N, HR, D), BF16),
        ((N, HR, D), BF16),
        ((N, NE, HR // NE, D // 2), BF16),
        ((N, NY, HR // NY, D // 2), BF16),
        ((N, HR // NE, D // 2), BF16),
        ((N, HR // NY, D // 2), BF16),
        ((N, NY, HS, D // 2), BF16),
        ((N, NE, HS, D // 2), BF16),
        ((N, HS, D), BF16),
        ((N, HS, D), BF16),
        ((FR, D), BF16),
        ((2, GR, D), BF16),
        ((GR, D), BF16),
        ((GR, D), BF16),
        ((NP, ER, YW), BF16),
        ((ER, YW), BF16),
        ((N, SH, YW), BF16),
        ((2, SH, D), BF16),
        ((SMALL, D), F32),
        ((SMALL, D // 2), F32),
        ((SMALL, D // 2), F32),
        ((NP, SMALL, D // 2), F32),
        ((SMALL, D // 2), F32),
        ((N, SMALL, D // 2), F32),
        ((SMALL, D), F32),
    ]
    pairs = [
        (N,),
        (N,),
        (NE, N),
        (NE, N),
        (NE, N),
        (NE, N),
        (NE, N),
        (2, N),
        (4, N, max(NE, NY)),
        (N,),
        (N,),
        (N,),
        (max(S, 1),),
        (N,),
        (4, N, max(NE, NY)),
        (N,),
        (2, NP),
        (3,),
        (3, NP),
        (3, N),
        (3, NY),
    ]
    sems = [pltpu.SemaphoreType.DMA((4,))]
    for shape in pairs:
        sems += [pltpu.SemaphoreType.DMA(shape)] * 2
    outs = [
        ((N * T, D // N), F32),
        ((T, D), F32),
        ((FR, D), BF16),
        ((2, SH, D), BF16),
        ((SMALL, D), F32),
    ]
    return pl.pallas_call(
        functools.partial(kernel, z),
        out_shape=[pltpu.VMEM(s, t) for s, t in outs],
        in_specs=[anywhere] + [vmem] * (7 + len(vectors)) + [anywhere] * 2 + [vmem],
        out_specs=[vmem] * len(outs),
        scratch_shapes=[pltpu.VMEM(s, t) for s, t in scratch] + sems,
        compiler_params=pltpu.CompilerParams(
            collective_id=0, has_side_effects=True, vmem_limit_bytes=58 * 2**20
        ),
        name="layer",
    )(x, seg, chosen, *vectors, q, k, v, o, r, up, down, cot)


def finish_kernel(
    z,
    out_in,
    ig_in,
    fin_ref,
    fqo_ref,
    small_ref,
    out_any,
    ig_out,
    g1_ref,
    s1_ref,
    gq_ref,
    qb_ref,
    gk_ref,
    gv_ref,
    vb_ref,
    go_ref,
    ob_ref,
    rw_ref,
    rb_ref,
    g2_ref,
    s2_ref,
    gup_any,
    ub_ref,
    gdown_any,
    db_ref,
    gup,
    gdown,
    sems,
):
    e, n = lax.axis_index("expert"), lax.axis_index("narrow")
    N, T, D, R, HP, LE = z.narrow, z.block, z.width, z.shard, z.head_part, z.local_experts
    copies = []

    def put(src, dst):
        copies.append(pltpu.make_async_copy(src, dst, sems.at[len(copies)]))
        copies[-1].start()

    put(out_in, out_any)
    put(ig_in, ig_out)
    gup[...] = fin_ref[0:D, :].astype(F32)
    put(gup, gup_any)
    gdown[...] = fin_ref[D : D + z.ff_local, :].astype(F32)
    put(gdown, gdown_any)
    gq_ref[...] = fqo_ref[0, 0:R, :].astype(F32)
    go_ref[...] = fqo_ref[1, 0:R, :].astype(F32)
    gk_ref[...] = fqo_ref[0, R : R + HP, :].astype(F32)
    gv_ref[...] = fqo_ref[1, R : R + HP, :].astype(F32)
    g1_ref[...] = small_ref[0:1, :]
    s1_ref[...] = small_ref[1:2, :]
    ob_ref[...] = small_ref[2:3, :]
    g2_ref[...] = small_ref[3:4, :]
    s2_ref[...] = small_ref[4:5, :]
    db_ref[...] = small_ref[5:6, :]
    rb_ref[...] = small_ref[7:8, 0 : z.experts]
    rw_ref[...] = small_ref[16 : 16 + z.experts, :]
    upper = jnp.zeros((1, D), F32)
    for j in range(N):
        upper = jnp.where(n == j, small_ref[8 + j : 9 + j, :], upper)
    ub_ref[...] = upper
    here = e * N + n
    query = pltpu.roll(small_ref[0:8, :], lax.rem(D - here * R, D), 1)
    for i in range(LE):
        qb_ref[i : i + 1, :] = query[6:7, i * HP : (i + 1) * HP]
    value = pltpu.roll(small_ref[8:16, :], lax.rem(D - n * HP, D), 1)
    vb_ref[...] = value[7:8, 0:HP]
    for copy in copies:
        copy.wait()


def finish(z, out, ig, fin, fqo, small):
    N, T, D, R, HP = z.narrow, z.block, z.width, z.shard, z.head_part
    FL = z.ff_local
    vmem = pl.BlockSpec(memory_space=pltpu.VMEM)
    anywhere = pl.BlockSpec(memory_space=pltpu.HBM)
    shapes = [
        (N * T, D // N),
        (T, D),
        (1, D),
        (1, D),
        (R, D),
        (z.local_experts, HP),
        (HP, D),
        (HP, D),
        (1, HP),
        (R, D),
        (1, D),
        (z.experts, D),
        (1, z.experts),
        (1, D),
        (1, D),
        (D, FL),
        (1, FL),
        (FL, D),
        (1, D),
    ]
    return pl.pallas_call(
        functools.partial(finish_kernel, z),
        out_shape=[jax.ShapeDtypeStruct(s, F32) for s in shapes],
        in_specs=[vmem] * 5,
        out_specs=[anywhere] * 2 + [vmem] * 13 + [anywhere, vmem, anywhere, vmem],
        scratch_shapes=[
            pltpu.VMEM((D, FL), F32),
            pltpu.VMEM((FL, D), F32),
            pltpu.SemaphoreType.DMA((4,)),
        ],
        compiler_params=pltpu.CompilerParams(vmem_limit_bytes=16 * 2**20),
        name="finish",
    )(out, ig, fin, fqo, small)


def per_device(
    inputs,
    seg_ids,
    chosen,
    gain_one,
    shift_one,
    query_w,
    query_b,
    key_w,
    value_w,
    value_b,
    out_w,
    out_b,
    router_w,
    router_b,
    gain_two,
    shift_two,
    up_w,
    up_b,
    down_w,
    down_b,
    cotangent,
):
    narrow = lax.axis_size("narrow")
    e, n = lax.axis_index("expert"), lax.axis_index("narrow")
    z = Sizes(
        lax.axis_size("dp"),
        lax.axis_size("expert"),
        narrow,
        inputs.shape[0],
        inputs.shape[1],
        seg_ids.shape[1],
        query_w.shape[0],
        up_w.shape[1],
    )
    D, R, HP = z.width, z.shard, z.head_part
    vectors = [gain_one, shift_one, out_b, gain_two, shift_two, down_b, up_b]
    vectors = [v.reshape(1, -1) for v in vectors]
    vectors += [query_b, value_b.reshape(1, -1), router_b.reshape(1, -1)]
    parts = run(
        z,
        inputs,
        seg_ids,
        jnp.transpose(chosen),
        vectors,
        jnp.transpose(query_w, (0, 2, 1)).reshape(R, D),
        jnp.transpose(key_w),
        jnp.transpose(value_w),
        out_w.reshape(R, D),
        jnp.transpose(router_w),
        up_w,
        down_w,
        cotangent,
    )
    out, ig, g1, s1, gq, qb, gk, gv, vb, go, ob, rw, rb, g2, s2, gup, ub, gdown, db = finish(
        z, *parts
    )
    return (
        out,
        ig,
        g1.reshape(-1),
        s1.reshape(-1),
        jnp.transpose(gq.reshape(z.local_experts, HP, D), (0, 2, 1)),
        qb,
        jnp.transpose(gk),
        jnp.transpose(gv),
        vb.reshape(-1),
        go.reshape(z.local_experts, HP, D),
        ob.reshape(-1),
        jnp.transpose(rw),
        rb.reshape(-1),
        g2.reshape(-1),
        s2.reshape(-1),
        gup,
        ub.reshape(-1),
        gdown,
        db.reshape(-1),
    )


def solution(mesh):
    return jax.shard_map(
        per_device,
        mesh=mesh,
        in_specs=(
            P("dp", None),
            P("dp", None),
            P("dp", None),
            P(),
            P(),
            P("expert", None, "narrow"),
            P("expert", "narrow"),
            P(None, "narrow"),
            P(None, "narrow"),
            P("narrow"),
            P("expert", "narrow", None),
            P(),
            P(),
            P(),
            P(),
            P(),
            P(None, "narrow"),
            P("narrow"),
            P("narrow", None),
            P(),
            P(("dp", "expert"), "narrow"),
        ),
        out_specs=(
            P(("dp", "expert"), "narrow"),
            P(("dp", "expert", "narrow"), None),
            P(),
            P(),
            P("expert", None, "narrow"),
            P("expert", "narrow"),
            P(None, "narrow"),
            P(None, "narrow"),
            P("narrow"),
            P("expert", "narrow", None),
            P(),
            P(),
            P(),
            P(),
            P(),
            P(None, "narrow"),
            P("narrow"),
            P("narrow", None),
            P(),
        ),
        check_vma=False,
    )
```

time: 147 us -> 93 us (0.63)
  Pallas kernels: 119 us -> 91.8 us
  local copies, waits for them, and re-layouts: 27.2 us -> 0 us
    pallas_call x1 -> x2, Pallas kernels: 119 us -> 91.8 us  [the longest x1 89 us: run(): pl.pallas_call(functools.partial(kernel, z), out_shape=[pltpu.VMEM(s, t)...]
    unnamed x8 -> x0, local copies, waits for them, and re-layouts: 14.9 us -> none
    concatenate x3 -> x0, local copies, waits for them, and re-layouts: 3.31 us -> none  [per_device(): jnp.concatenate([vec, jnp.broadcast_to(router_b[:, None], (z.experts, D))])]
    slice x2 -> x0, local copies, waits for them, and re-layouts: 2.3 us -> none  [the longest x1 1.58 us: per_device(): small[5]]
where the time goes in v2:
time: 93 us; the launch traced here: 92.6 us
  Pallas kernels  91.8 us (99%)
    pallas_call x1, Pallas kernels, run(): pl.pallas_call(functools.partial(kernel, z), out_shape=[pltpu.VMEM(s, t)...  89 us
    pallas_call x1, Pallas kernels, finish(): pl.pallas_call(functools.partial(finish_kernel, z), out_shape=[jax.ShapeD...  2.82 us

profile of v2, /device:TPU:0, one launch (start us, length us, event | category | flops | bytes accessed | tf_op | source)
XLA Modules:
  0.0 92.6 jit_solution(2841037209502998002)
XLA Ops:
  0.7 89.0 %layer.1 = (f32[2048,128]{1,0:T(8,128)S(1)}, f32[512,512]{1,0:T(8,128)S(1)}, bf16[1024,512]{1,0:T(8,128)(2,1)S(1)}, bf16[2,80,512]{2,1,0:T(8,128)(2,1)S(1)}, f32[24,512]{1,0:T(8,128)S(1)}) custom-call(f32[4096,512]{1,0:T(8,128)} %x_any.1, s32[4,1024]{1,0:T(4,128)} %seg_ref.1, s32[2,4096]{1,0:T(2,128)} %bitcast.35, f32[1,512]{1,0:T(1,128)} %bitcast.39, ...), custom_call_target="tpu_custom_call" | custom-call | tf_op jit(solution)/shard_map/layer/pallas_call | solution.py:1079
  89.7 2.8 %finish.1 = (f32[2048,128]{1,0:T(8,128)}, f32[512,512]{1,0:T(8,128)}, f32[1,512]{1,0:T(1,128)}, f32[1,512]{1,0:T(1,128)}, f32[64,512]{1,0:T(8,128)}, /*index=5*/...) custom-call(f32[2048,128]{1,0:T(8,128)S(1)} %get-tuple-element.43.ou, ...), custom_call_target="tpu_custom_call" | custom-call | tf_op jit(solution)/shard_map/finish/pallas_call | solution.py:1188

commit v3 on v2

--- a/solution.py
+++ b/solution.py
@@ -90,11 +90,13 @@
     up_any,
     down_any,
     cot_ref,
+    out_any,
+    ig_any,
+    fin_any,
+    fqo_ref,
+    small_ref,
     out_ref,
     ig_ref,
-    fin_ref,
-    fqo_ref,
-    small_ref,
     xw,
     rw,
     wq,
@@ -175,8 +177,6 @@
     o_r,
     om_s,
     om_r,
-    fz_s,
-    fz_r,
     fp_s,
     fp_r,
     fm_s,
@@ -203,6 +203,8 @@
     qz_r,
     qa_s,
     qa_r,
+    fz_s,
+    fz_r,
 ):
     d, e, n = lax.axis_index("dp"), lax.axis_index("expert"), lax.axis_index("narrow")
     c, y = rem(d, 2), lax.div(d, 2)
@@ -306,33 +308,33 @@
     def spread_start(part, send, recv):
         for j in range(1, N):
             at = part(here)
-            push(at, at, send.at[0, j], recv.at[0, j], in_line(j)[1])
+            push(at, at, send.at[j - 1], recv.at[j - 1], in_line(j)[1])
         for i in range(1, NE):
             at = part(here)
-            push(at, at, send.at[i, 0], recv.at[i, 0], in_expert(i)[1])
+            push(at, at, send.at[i * N - 1], recv.at[i * N - 1], in_expert(i)[1])
 
     def spread_on(part, send, recv, to_mate):
         for j in range(1, N):
             at = part(shard_at(0, j))
-            landed(at, send.at[0, j], recv.at[0, j])
+            landed(at, send.at[j - 1], recv.at[j - 1])
             for i in range(1, NE):
-                push(at, at, send.at[i, j], recv.at[i, j], in_expert(i)[1])
+                push(at, at, send.at[i * N + j - 1], recv.at[i * N + j - 1], in_expert(i)[1])
             if to_mate is not None:
-                push(at, at, to_mate[0].at[0, j], to_mate[1].at[0, j], mate)
+                push(at, at, to_mate[0].at[j - 1], to_mate[1].at[j - 1], mate)
 
     def spread_end(part, send, recv, to_mate):
         for i in range(1, NE):
             for j in range(N):
                 at = part(shard_at(i, j))
-                landed(at, send.at[i, j], recv.at[i, j])
+                landed(at, send.at[i * N + j - 1], recv.at[i * N + j - 1])
                 if to_mate is not None:
-                    push(at, at, to_mate[0].at[i, j], to_mate[1].at[i, j], mate)
+                    push(at, at, to_mate[0].at[i * N + j - 1], to_mate[1].at[i * N + j - 1], mate)
 
     def spread_wait(part, to_mate):
         for i in range(NE):
             for j in range(N):
                 if i or j:
-                    landed(part(shard_at(i, j)), to_mate[0].at[i, j], to_mate[1].at[i, j])
+                    landed(part(shard_at(i, j)), to_mate[0].at[i * N + j - 1], to_mate[1].at[i * N + j - 1])
 
     def bias_part(g):
         return bias.at[g]
@@ -351,7 +353,7 @@
 
     for j in range(1, N):
         at = wkv.at[c, rows(n * HP, HP)]
-        push(at, at, w_s.at[j], w_r.at[j], in_line(j)[1])
+        push(at, at, w_s.at[j - 1], w_r.at[j - 1], in_line(j)[1])
     spread_start(q_part, q_s, q_r)
     spread_start(bias_part, b_s, b_r)
     up_copy.wait()
@@ -362,9 +364,6 @@
     HR = FR // 2
     HS = HR // NP
     HA, HB = HR // NE, HR // NY
-    near_first = sorted(range(1, N), key=lambda j: (min(j, N - j), j))
-    first, last = near_first[: N // 2], near_first[N // 2 :]
-
     def left_slice(of, ys, es):
         return ffw.at[of, rows(c * HR + (es * NY + ys) * HS, HS), left]
 
@@ -377,49 +376,93 @@
     def right_half(of, ys):
         return ffw.at[of, rows(c * HR + ys * HB, HB), right]
 
-    def shard_start(j):
-        to = in_line(j)[1]
-        at = left_slice(n, y, e)
-        push(at, at, fz_s.at[0, j], fz_r.at[0, j], to)
-        at = right_slice(n, y, e)
-        push(at, at, fz_s.at[1, j], fz_r.at[1, j], to)
+    def by_distance(at):
+        return sorted((o for o in range(N) if o != at), key=lambda o: (abs(o - at), o))
+
+    def pick(choices):
+        value = choices[0]
+        for at in range(1, N):
+            value = jnp.where(n == at, choices[at], value)
+        return value
+
+    shard_of = [n] + [pick([by_distance(at)[k] for at in range(N)]) for k in range(N - 1)]
+    maybe_started = []
+
+    def line_push(of, step, valid):
+        of = jnp.clip(of, 0, N - 1)
+        to = (d, e, jnp.clip(n + step, 0, N - 1))
+        way = (step + 1) // 2
+        copies = [
+            pltpu.make_async_remote_copy(
+                src_ref=at,
+                dst_ref=at,
+                send_sem=fz_s.at[part, way, of],
+                recv_sem=fz_r.at[part, of],
+                device_id=to,
+                device_id_type=MESH,
+            )
+            for part, at in enumerate((left_slice(of, y, e), right_slice(of, y, e)))
+        ]
+
+        @pl.when(valid)
+        def _():
+            for copy in copies:
+                copy.start()
+
+        maybe_started.append((valid, copies))
+
+    def line_landed(of, valid):
+        of = jnp.clip(of, 0, N - 1)
+
+        @pl.when(valid)
+        def _():
+            landed(left_slice(of, y, e), fz_s.at[0, 0, of], fz_r.at[0, of])
+            landed(right_slice(of, y, e), fz_s.at[1, 0, of], fz_r.at[1, of])
+
+    def shards_start():
+        line_push(n, 1, n + 1 < N)
+        line_push(n, -1, n > 0)
+
+    def shards_on(hop):
+        line_landed(n - hop, n >= hop)
+        line_push(n - hop, 1, jnp.logical_and(n >= hop, n + 1 < N))
+        line_landed(n + hop, n + hop < N)
+        line_push(n + hop, -1, jnp.logical_and(n + hop < N, n > 0))
 
     def plane_on(j):
-        there, _ = in_line(-j)
+        there = shard_of[j]
         at = left_slice(there, y, e)
-        landed(at, fz_s.at[0, j], fz_r.at[0, j])
         for i in range(1, NY):
-            push(at, at, fp_s.at[0, j, i], fp_r.at[0, j, i], in_rows(i)[1])
+            push(at, at, fp_s.at[0, j - 1, i - 1], fp_r.at[0, j - 1, i - 1], in_rows(i)[1])
         at = right_slice(there, y, e)
-        landed(at, fz_s.at[1, j], fz_r.at[1, j])
         for i in range(1, NE):
-            push(at, at, fp_s.at[1, j, i], fp_r.at[1, j, i], in_expert(i)[1])
+            push(at, at, fp_s.at[1, j - 1, i - 1], fp_r.at[1, j - 1, i - 1], in_expert(i)[1])
 
     def plane_turn(j):
-        there, _ = in_line(-j)
+        there = shard_of[j]
         for i in range(1, NY):
             near, _ = in_rows(-i)
-            landed(left_slice(there, near, e), fp_s.at[0, j, i], fp_r.at[0, j, i])
+            landed(left_slice(there, near, e), fp_s.at[0, j - 1, i - 1], fp_r.at[0, j - 1, i - 1])
         at = left_half(there, e)
         for i in range(1, NE):
-            push(at, at, fp_s.at[2, j, i], fp_r.at[2, j, i], in_expert(i)[1])
+            push(at, at, fp_s.at[2, j - 1, i - 1], fp_r.at[2, j - 1, i - 1], in_expert(i)[1])
         for i in range(1, NE):
             near, _ = in_expert(-i)
-            landed(right_slice(there, y, near), fp_s.at[1, j, i], fp_r.at[1, j, i])
+            landed(right_slice(there, y, near), fp_s.at[1, j - 1, i - 1], fp_r.at[1, j - 1, i - 1])
         at = right_half(there, y)
         for i in range(1, NY):
-            push(at, at, fp_s.at[3, j, i], fp_r.at[3, j, i], in_rows(i)[1])
+            push(at, at, fp_s.at[3, j - 1, i - 1], fp_r.at[3, j - 1, i - 1], in_rows(i)[1])
 
     def mate_on(j):
-        there, _ = in_line(-j)
+        there = shard_of[j]
         for i in range(1, NE):
             near, _ = in_expert(-i)
-            landed(left_half(there, near), fp_s.at[2, j, i], fp_r.at[2, j, i])
+            landed(left_half(there, near), fp_s.at[2, j - 1, i - 1], fp_r.at[2, j - 1, i - 1])
         for i in range(1, NY):
             near, _ = in_rows(-i)
-            landed(right_half(there, near), fp_s.at[3, j, i], fp_r.at[3, j, i])
+            landed(right_half(there, near), fp_s.at[3, j - 1, i - 1], fp_r.at[3, j - 1, i - 1])
         at = ffw.at[there, rows(c * HR, HR)]
-        push(at, at, fm_s.at[j], fm_r.at[j], mate)
+        push(at, at, fm_s.at[j - 1], fm_r.at[j - 1], mate)
 
     x_copy.wait()
     gain_one, shift_one = g1_ref[...], s1_ref[...]
@@ -456,17 +499,16 @@
     for j in range(1, N):
         there, _ = in_line(-j)
         at = wkv.at[c, rows(there * HP, HP)]
-        landed(at, w_s.at[j], w_r.at[j])
-        push(at, at, wm_s.at[j], wm_r.at[j], mate)
+        landed(at, w_s.at[j - 1], w_r.at[j - 1])
+        push(at, at, wm_s.at[j - 1], wm_r.at[j - 1], mate)
     spread_on(q_part, q_s, q_r, (qm_s, qm_r))
     spread_on(bias_part, b_s, b_r, None)
-    for j in first:
-        shard_start(j)
+    shards_start()
     spread_start(o_part, o_s, o_r)
 
     for j in range(1, N):
         there, _ = in_line(-j)
-        landed(wkv.at[1 - c, rows(there * HP, HP)], wm_s.at[j], wm_r.at[j])
+        landed(wkv.at[1 - c, rows(there * HP, HP)], wm_s.at[j - 1], wm_r.at[j - 1])
     kn[...] = dot_nt(rw[...], wkv[0]).astype(BF16)
     kt[...] = dot_nt(wkv[0], rw[...]).astype(BF16)
     spread_end(q_part, q_s, q_r, (qm_s, qm_r))
@@ -512,16 +554,14 @@
             prob[k, :, at] = low
             mix[k, :, at] = dot(vt[...], low)
 
-    for j in last:
-        shard_start(j)
     attend(0)
     attend(1)
-    plane_on(first[0])
-    for j in first[1:]:
-        plane_on(j)
+    shards_on(1)
+    plane_on(1)
     spread_on(o_part, o_s, o_r, (om_s, om_r))
-    for j in first:
-        plane_turn(j)
+    plane_turn(1)
+    shards_on(2)
+    plane_on(2)
     CW = D // N
     cot[:, rows(n * CW, CW, 128)] = cot_ref[rows(n * T, T, 128), :]
     for j in range(1, N):
@@ -529,12 +569,10 @@
         push(
             cot_ref.at[rows(there * T, T, 128)],
             cot.at[:, rows(n * CW, CW, 128)],
-            ct_s.at[j],
-            ct_r.at[j],
+            ct_s.at[j - 1],
+            ct_r.at[j - 1],
             to,
         )
-    for j in last:
-        plane_on(j)
     spread_end(o_part, o_s, o_r, (om_s, om_r))
 
     for part in range(N):
@@ -576,55 +614,50 @@
         for i in range(1, NE):
             there, to = in_expert(i)
             src = psend.at[j, rows(there * HA, HA), left]
-            push(src, pea.at[j, i], gp_s.at[0, j, i], gp_r.at[0, j, i], to)
+            push(src, pea.at[j, i], gp_s.at[0, j, i - 1], gp_r.at[0, j, i - 1], to)
         for i in range(1, NY):
             there, to = in_rows(i)
             src = psend.at[j, rows(there * HB, HB), right]
-            push(src, pya.at[j, i], gp_s.at[1, j, i], gp_r.at[1, j, i], to)
+            push(src, pya.at[j, i], gp_s.at[1, j, i - 1], gp_r.at[1, j, i - 1], to)
 
     def plane_middle(j):
         whole = psend[j, rows(e * HA, HA), left].astype(F32)
         for i in range(1, NE):
-            landed(pea.at[j, i], gp_s.at[0, j, i], gp_r.at[0, j, i])
+            landed(pea.at[j, i], gp_s.at[0, j, i - 1], gp_r.at[0, j, i - 1])
             whole = whole + pea[j, i].astype(F32)
         mea[j] = whole.astype(BF16)
         for i in range(1, NY):
             there, to = in_rows(i)
             src = mea.at[j, rows(there * HS, HS)]
-            push(src, pyb.at[j, i], gp_s.at[2, j, i], gp_r.at[2, j, i], to)
+            push(src, pyb.at[j, i], gp_s.at[2, j, i - 1], gp_r.at[2, j, i - 1], to)
         whole = psend[j, rows(y * HB, HB), right].astype(F32)
         for i in range(1, NY):
-            landed(pya.at[j, i], gp_s.at[1, j, i], gp_r.at[1, j, i])
+            landed(pya.at[j, i], gp_s.at[1, j, i - 1], gp_r.at[1, j, i - 1])
             whole = whole + pya[j, i].astype(F32)
         mya[j] = whole.astype(BF16)
         for i in range(1, NE):
             there, to = in_expert(i)
             src = mya.at[j, rows(there * HS, HS)]
-            push(src, peb.at[j, i], gp_s.at[3, j, i], gp_r.at[3, j, i], to)
+            push(src, peb.at[j, i], gp_s.at[3, j, i - 1], gp_r.at[3, j, i - 1], to)
 
     def line_start(j):
         whole = mea[j, rows(y * HS, HS), :].astype(F32)
         for i in range(1, NY):
-            landed(pyb.at[j, i], gp_s.at[2, j, i], gp_r.at[2, j, i])
+            landed(pyb.at[j, i], gp_s.at[2, j, i - 1], gp_r.at[2, j, i - 1])
             whole = whole + pyb[j, i].astype(F32)
         zsend[j, :, left] = whole.astype(BF16)
         whole = mya[j, rows(e * HS, HS), :].astype(F32)
         for i in range(1, NE):
-            landed(peb.at[j, i], gp_s.at[3, j, i], gp_r.at[3, j, i])
+            landed(peb.at[j, i], gp_s.at[3, j, i - 1], gp_r.at[3, j, i - 1])
             whole = whole + peb[j, i].astype(F32)
         zsend[j, :, right] = whole.astype(BF16)
         if j:
-            _, to = in_line(-j)
-            push(zsend.at[j], zrecv.at[j], gz_s.at[j], gz_r.at[j], to)
-
-    for step, j in enumerate([0] + near_first):
-        there, _ = in_line(-j)
+            push(zsend.at[j], zrecv.at[n], gz_s.at[j], gz_r.at[n], (d, e, shard_of[j]))
+
+    def forward(j):
+        there = shard_of[j]
         if j:
-            if step == 1:
-                mate_on(j)
-            if step + 1 < N:
-                mate_on(near_first[step])
-            landed(ffw.at[there, rows((1 - c) * HR, HR)], fm_s.at[j], fm_r.at[j])
+            landed(ffw.at[there, rows((1 - c) * HR, HR)], fm_s.at[j - 1], fm_r.at[j - 1])
         up_b = jnp.concatenate(
             [bias[e * N + there, i : i + 1, :] for i in range(FL // 128)], axis=1
         )
@@ -644,24 +677,9 @@
             return carry
 
         lax.fori_loop(0, T // TL, feed, 0)
-        if step == 0:
-            for j in last:
-                plane_turn(j)
-    delta[...] = acc[...].astype(BF16)
-
-    for j in range(1, N):
-        there, _ = in_line(-j)
-        landed(cot.at[:, rows(there * CW, CW, 128)], ct_s.at[j], ct_r.at[j])
-
-
-    outd[n] = delta[:, rows(n * CW, CW, 128)]
-    for j in range(1, N):
-        there, to = in_line(j)
-        push(delta.at[:, rows(there * CW, CW, 128)], outd.at[n], od_s.at[j], od_r.at[j], to)
-
-    order = list(range(1, N)) + [0]
-    for step, j in enumerate(order):
-        there, _ = in_line(-j)
+
+    def backward(j):
+        there = shard_of[j]
 
         def feed_back(i, carry):
             at = rows(i * TL, TL, 128)
@@ -676,8 +694,38 @@
         gsend[j, 0:D, :] = dot_tn(second[...], ugrad[...]).astype(BF16)
         gsend[j, D : D + FL, :] = dot_tn(active[j], cot[...]).astype(BF16)
         core_start(j)
-        if step:
-            plane_start(order[step - 1])
+
+    def cotangent_wait():
+        for j in range(1, N):
+            there, _ = in_line(-j)
+            landed(cot.at[:, rows(there * CW, CW, 128)], ct_s.at[j - 1], ct_r.at[j - 1])
+
+    forward(0)
+    plane_turn(2)
+    mate_on(1)
+    shards_on(3)
+    plane_on(3)
+    forward(1)
+    mate_on(2)
+    plane_turn(3)
+    forward(2)
+    cotangent_wait()
+    backward(1)
+    backward(2)
+    plane_start(1)
+    mate_on(3)
+    forward(3)
+    delta[...] = acc[...].astype(BF16)
+    outd[n] = delta[:, rows(n * CW, CW, 128)]
+    for j in range(1, N):
+        there, to = in_line(j)
+        push(delta.at[:, rows(there * CW, CW, 128)], outd.at[n], od_s.at[j - 1], od_r.at[j - 1], to)
+
+    backward(3)
+    plane_start(2)
+    backward(0)
+    plane_start(3)
+    plane_middle(1)
 
     zero_row = jnp.zeros((1, D), F32)
 
@@ -704,8 +752,7 @@
     sp[2:3, :] = sums[2]
     sp[5:6, :] = sums[3]
 
-    plane_start(order[N - 1])
-    plane_middle(order[0])
+    plane_start(0)
 
     SH = R + HP
     out_grad = dot(mixg[...], hgb[...]).astype(BF16)
@@ -751,7 +798,7 @@
 
     attend_back(0)
     attend_back(1)
-    plane_middle(order[1])
+    plane_middle(2)
 
     H, PC = z.reach, z.piece
     offsets = [o for o in range(-H, H + 1) if o]
@@ -801,8 +848,8 @@
         gqo[0, g * SH + R : (g + 1) * SH, :] = key_w_grad[shared, :]
         gqo[1, g * SH + R : (g + 1) * SH, :] = value_w_grad[shared, :]
     push(gqo.at[1 - c], cqo, qc_s.at[0], qc_r.at[0], mate)
-    plane_middle(order[2])
-    line_start(order[0])
+    plane_middle(3)
+    line_start(1)
     ones = jnp.ones((8, T), BF16)
     sp[6:7, :] = dot_nt(ones, dqt[...])[0:1, :]
     sp[7:8, :] = jnp.zeros((1, D), F32)
@@ -813,8 +860,6 @@
     sp[16:24, :] = dot(logit_low, rw[own, :])
     sp[15:16, :] = jnp.zeros((1, D), F32)
     sp[15:16, 0:HEAD] = jnp.sum(dv[...], axis=0, keepdims=True)
-    for j in order[3:]:
-        plane_middle(j)
     YW = D // NY
     ER = N * SH
     landed(cqo, qc_s.at[0], qc_r.at[0])
@@ -822,8 +867,10 @@
     for i in range(1, NP):
         there, to = in_plane(i)
         src = pqo.at[rows(rem(there, NE) * ER, ER), rows(lax.div(there, NE) * YW, YW, 128)]
-        push(src, rqo.at[i], qp_s.at[0, i], qp_r.at[0, i], to)
-    line_start(order[1])
+        push(src, rqo.at[i], qp_s.at[0, i - 1], qp_r.at[0, i - 1], to)
+    plane_middle(0)
+    line_start(2)
+    line_start(3)
 
     dk[...] = dk[...] * scale
     for s, o in enumerate(offsets):
@@ -857,101 +904,117 @@
         return tuple(a + jnp.sum(b, axis=0, keepdims=True) for a, b in zip(carry, parts))
 
     sums = lax.fori_loop(0, T // 128, norm_one_back, (zero_row,) * 2)
+    ig_copy = pltpu.make_async_copy(ig_ref, ig_any, loc_sem.at[4])
+    ig_copy.start()
     sp[0:1, :] = sums[0]
     sp[1:2, :] = sums[1]
     for j in range(8 + N, 15):
         sp[j : j + 1, :] = zero_row
-    push(sp.at[:, other_cols], csp, qc_s.at[2], qc_r.at[2], mate)
-    for j in order[2:]:
-        line_start(j)
-
-    landed(csp, qc_s.at[2], qc_r.at[2])
+    push(sp.at[:, other_cols], csp, qc_s.at[1], qc_r.at[1], mate)
+
+    landed(csp, qc_s.at[1], qc_r.at[1])
     psp[...] = sp[:, mine_cols] + csp[...]
     for i in range(1, NP):
         _, to = in_plane(i)
-        push(psp, rsp.at[i], qp_s.at[2, i], qp_r.at[2, i], to)
+        push(psp, rsp.at[i], qp_s.at[1, i - 1], qp_r.at[1, i - 1], to)
+
+    line_start(0)
+
+    whole = zsend[0].astype(F32)
+    for j in range(1, N):
+        there, _ = in_line(-j)
+        landed(zrecv.at[there], gz_s.at[j], gz_r.at[there])
+        whole = whole + zrecv[there].astype(F32)
+
+    def fin_left(ys, es):
+        return fin.at[rows(c * HR + (es * NY + ys) * HS, HS), left]
+
+    def fin_right(ys, es):
+        return fin.at[rows(c * HR + (ys * NE + es) * HS, HS), right]
+
+    fin[rows(c * HR + (e * NY + y) * HS, HS), left] = whole[:, 0:half].astype(BF16)
+    fin[rows(c * HR + (y * NE + e) * HS, HS), right] = whole[:, half:].astype(BF16)
+    for i in range(1, NP):
+        _, to = in_plane(i)
+        push(fin_left(y, e), fin_left(y, e), ga_s.at[i], ga_r.at[i], to)
+        push(fin_right(y, e), fin_right(y, e), ga_s.at[NP - 1 + i], ga_r.at[NP - 1 + i], to)
 
     whole = pqo[rows(e * ER, ER), rows(y * YW, YW, 128)].astype(F32)
     for i in range(1, NP):
-        landed(rqo.at[i], qp_s.at[0, i], qp_r.at[0, i])
+        landed(rqo.at[i], qp_s.at[0, i - 1], qp_r.at[0, i - 1])
         whole = whole + rqo[i].astype(F32)
     zqo[...] = whole.astype(BF16)
     for j in range(1, N):
         there, to = in_line(j)
-        push(zqo.at[rows(there * SH, SH)], yqo.at[j], qz_s.at[0, j], qz_r.at[0, j], to)
+        push(zqo.at[rows(there * SH, SH)], yqo.at[j], qz_s.at[0, j - 1], qz_r.at[0, j - 1], to)
     whole = psp[...]
     for i in range(1, NP):
-        landed(rsp.at[i], qp_s.at[2, i], qp_r.at[2, i])
+        landed(rsp.at[i], qp_s.at[1, i - 1], qp_r.at[1, i - 1])
         whole = whole + rsp[i]
     zsp[...] = whole
     for j in range(1, N):
         _, to = in_line(j)
-        push(zsp, ysp.at[j], qz_s.at[2, j], qz_r.at[2, j], to)
-
-    whole = zsend[0].astype(F32)
-    for j in range(1, N):
-        landed(zrecv.at[j], gz_s.at[j], gz_r.at[j])
-        whole = whole + zrecv[j].astype(F32)
-
-    def fin_left(ys, es):
-        return fin.at[rows(c * HR + (es * NY + ys) * HS, HS), left]
-
-    def fin_right(ys, es):
-        return fin.at[rows(c * HR + (ys * NE + es) * HS, HS), right]
-
-    fin[rows(c * HR + (e * NY + y) * HS, HS), left] = whole[:, 0:half].astype(BF16)
-    fin[rows(c * HR + (y * NE + e) * HS, HS), right] = whole[:, half:].astype(BF16)
-    for i in range(1, NP):
-        _, to = in_plane(i)
-        push(fin_left(y, e), fin_left(y, e), ga_s.at[0, i], ga_r.at[0, i], to)
-        push(fin_right(y, e), fin_right(y, e), ga_s.at[1, i], ga_r.at[1, i], to)
+        push(zsp, ysp.at[j], qz_s.at[1, j - 1], qz_r.at[1, j - 1], to)
 
     cols_copy.wait()
     for j in range(1, N):
         there, _ = in_line(-j)
-        landed(outd.at[there], od_s.at[j], od_r.at[j])
+        landed(outd.at[there], od_s.at[j - 1], od_r.at[j - 1])
     for j in range(N):
         at = pl.ds(j * T, T)
         out_ref[at, :] = out_ref[at, :] + outd[j].astype(F32)
+    out_copy = pltpu.make_async_copy(out_ref, out_any, loc_sem.at[5])
+    out_copy.start()
 
     whole = zqo[rows(n * SH, SH), :].astype(F32)
     for j in range(1, N):
-        landed(yqo.at[j], qz_s.at[0, j], qz_r.at[0, j])
+        landed(yqo.at[j], qz_s.at[0, j - 1], qz_r.at[0, j - 1])
         whole = whole + yqo[j].astype(F32)
     my_cols = rows(y * YW, YW, 128)
     fqo[c, :, my_cols] = whole.astype(BF16)
     for i in range(1, NY):
         _, to = in_rows(i)
         at = fqo.at[c, :, my_cols]
-        push(at, at, qa_s.at[0, i], qa_r.at[0, i], to)
+        push(at, at, qa_s.at[1 + i], qa_r.at[1 + i], to)
     whole = zsp[...]
     for j in range(1, N):
-        landed(ysp.at[j], qz_s.at[2, j], qz_r.at[2, j])
+        landed(ysp.at[j], qz_s.at[1, j - 1], qz_r.at[1, j - 1])
         whole = whole + ysp[j]
     fsp[:, mine_cols] = whole
     at = fsp.at[:, mine_cols]
-    push(at, at, qa_s.at[2, 0], qa_r.at[2, 0], mate)
+    push(at, at, qa_s.at[1], qa_r.at[1], mate)
     for i in range(1, NY):
         near, _ = in_rows(-i)
-        landed(fqo.at[c, :, rows(near * YW, YW, 128)], qa_s.at[0, i], qa_r.at[0, i])
-    push(fqo.at[c], fqo.at[c], qa_s.at[0, 0], qa_r.at[0, 0], mate)
+        landed(fqo.at[c, :, rows(near * YW, YW, 128)], qa_s.at[1 + i], qa_r.at[1 + i])
+    push(fqo.at[c], fqo.at[c], qa_s.at[0], qa_r.at[0], mate)
 
     for i in range(1, NP):
         near, _ = in_plane(-i)
         ys, es = lax.div(near, NE), rem(near, NE)
-        landed(fin_left(ys, es), ga_s.at[0, i], ga_r.at[0, i])
-        landed(fin_right(ys, es), ga_s.at[1, i], ga_r.at[1, i])
-    at = fin.at[rows(c * HR, HR)]
-    push(at, at, ga_s.at[0, 0], ga_r.at[0, 0], mate)
-    landed(fsp.at[:, other_cols], qa_s.at[2, 0], qa_r.at[2, 0])
+        landed(fin_left(ys, es), ga_s.at[i], ga_r.at[i])
+        landed(fin_right(ys, es), ga_s.at[NP - 1 + i], ga_r.at[NP - 1 + i])
+    at = rows(c * HR, HR)
+    push(fin.at[at], fin_any.at[at], ga_s.at[0], ga_r.at[0], mate)
+    fin_copy = pltpu.make_async_copy(fin.at[at], fin_any.at[at], loc_sem.at[6])
+    fin_copy.start()
+    landed(fsp.at[:, other_cols], qa_s.at[1], qa_r.at[1])
     small_ref[...] = fsp[...]
-    landed(fqo.at[1 - c], qa_s.at[0, 0], qa_r.at[0, 0])
+    landed(fqo.at[1 - c], qa_s.at[0], qa_r.at[0])
     fqo_ref[...] = fqo[...]
-    landed(fin.at[rows((1 - c) * HR, HR)], ga_s.at[0, 0], ga_r.at[0, 0])
-    fin_ref[...] = fin[...]
+    ig_copy.wait()
+    out_copy.wait()
+    fin_copy.wait()
+    landed(fin_any.at[rows((1 - c) * HR, HR)], ga_s.at[0], ga_r.at[0])
 
     for copy in started:
         copy.wait_send()
+    for valid, copies in maybe_started:
+
+        @pl.when(valid)
+        def _(copies=copies):
+            for copy in copies:
+                copy.wait_send()
+
     for s, o in enumerate(offsets):
         valid = jnp.logical_and(spot_in_row + o >= 0, spot_in_row + o < z.per_row)
 
@@ -977,6 +1040,8 @@
     vmem = pl.BlockSpec(memory_space=pltpu.VMEM)
     anywhere = pl.BlockSpec(memory_space=pltpu.HBM)
     scratch = [
+        ((N * T, D // N), F32),
+        ((T, D), F32),
         ((W, D), F32),
         ((W, D), BF16),
         ((QR, D), BF16),
@@ -1044,31 +1109,31 @@
         ((SMALL, D), F32),
     ]
     pairs = [
-        (N,),
-        (N,),
-        (NE, N),
-        (NE, N),
-        (NE, N),
-        (NE, N),
-        (NE, N),
-        (2, N),
-        (4, N, max(NE, NY)),
-        (N,),
-        (N,),
-        (N,),
+        (N - 1,),
+        (N - 1,),
+        (G - 1,),
+        (G - 1,),
+        (G - 1,),
+        (G - 1,),
+        (G - 1,),
+        (4, N - 1, max(NE, NY) - 1),
+        (N - 1,),
+        (N - 1,),
+        (N - 1,),
         (max(S, 1),),
         (N,),
-        (4, N, max(NE, NY)),
+        (4, N, max(NE, NY) - 1),
         (N,),
-        (2, NP),
-        (3,),
-        (3, NP),
-        (3, N),
-        (3, NY),
+        (2 * NP - 1,),
+        (2,),
+        (2, NP - 1),
+        (2, N - 1),
+        (NY + 1,),
     ]
-    sems = [pltpu.SemaphoreType.DMA((4,))]
+    sems = [pltpu.SemaphoreType.DMA((7,))]
     for shape in pairs:
         sems += [pltpu.SemaphoreType.DMA(shape)] * 2
+    sems += [pltpu.SemaphoreType.DMA((2, 2, N)), pltpu.SemaphoreType.DMA((2, N))]
     outs = [
         ((N * T, D // N), F32),
         ((T, D), F32),
@@ -1080,7 +1145,7 @@
         functools.partial(kernel, z),
         out_shape=[pltpu.VMEM(s, t) for s, t in outs],
         in_specs=[anywhere] + [vmem] * (7 + len(vectors)) + [anywhere] * 2 + [vmem],
-        out_specs=[vmem] * len(outs),
+        out_specs=[pl.BlockSpec(memory_space=pl.ANY)] * 3 + [vmem] * 2,
         scratch_shapes=[pltpu.VMEM(s, t) for s, t in scratch] + sems,
         compiler_params=pltpu.CompilerParams(
             collective_id=0, has_side_effects=True, vmem_limit_bytes=58 * 2**20
@@ -1188,7 +1253,7 @@
     return pl.pallas_call(
         functools.partial(finish_kernel, z),
         out_shape=[jax.ShapeDtypeStruct(s, F32) for s in shapes],
-        in_specs=[vmem] * 5,
+        in_specs=[pl.BlockSpec(memory_space=pl.ANY)] * 2 + [vmem] * 3,
         out_specs=[anywhere] * 2 + [vmem] * 13 + [anywhere, vmem, anywhere, vmem],
         scratch_shapes=[
             pltpu.VMEM((D, FL), F32),

time: 93 us -> 90.8 us (0.976)
  Pallas kernels: 91.8 us -> 89.8 us
    pallas_call x1, Pallas kernels: 89 us -> 86.9 us  [run(): pl.pallas_call(functools.partial(kernel, z), out_shape=[pltpu.VMEM(s, t)...]
where the time goes in v3:
time: 90.8 us; the launch traced here: 90.6 us
  Pallas kernels  89.8 us (99%)
    pallas_call x1, Pallas kernels, run(): pl.pallas_call(functools.partial(kernel, z), out_shape=[pltpu.VMEM(s, t)...  86.9 us
    pallas_call x1, Pallas kernels, finish(): pl.pallas_call(functools.partial(finish_kernel, z), out_shape=[jax.ShapeD...  2.82 us

profile of v3, /device:TPU:0, one launch (start us, length us, event | category | flops | bytes accessed | tf_op | source)
XLA Modules:
  0.0 90.6 jit_solution(2802253721453397701)
XLA Ops:
  0.7 86.9 %layer.1 = (f32[2048,128]{1,0:T(8,128)S(1)}, f32[512,512]{1,0:T(8,128)S(1)}, bf16[1024,512]{1,0:T(8,128)(2,1)S(1)}, bf16[2,80,512]{2,1,0:T(8,128)(2,1)S(1)}, f32[24,512]{1,0:T(8,128)S(1)}) custom-call(f32[4096,512]{1,0:T(8,128)} %x_any.1, s32[4,1024]{1,0:T(4,128)} %seg_ref.1, s32[2,4096]{1,0:T(2,128)} %bitcast.35, f32[1,512]{1,0:T(1,128)} %bitcast.39, ...), custom_call_target="tpu_custom_call" | custom-call | tf_op jit(solution)/shard_map/layer/pallas_call | solution.py:1144
  87.6 2.8 %finish.1 = (f32[2048,128]{1,0:T(8,128)}, f32[512,512]{1,0:T(8,128)}, f32[1,512]{1,0:T(1,128)}, f32[1,512]{1,0:T(1,128)}, f32[64,512]{1,0:T(8,128)}, /*index=5*/...) custom-call(f32[2048,128]{1,0:T(8,128)S(1)} %get-tuple-element.43.ou, ...), custom_call_target="tpu_custom_call" | custom-call | tf_op jit(solution)/shard_map/finish/pallas_call | solution.py:1253

commit v4 on v3

--- a/solution.py
+++ b/solution.py
@@ -293,7 +293,10 @@
         pl.semaphore_signal(barrier, inc=1, device_id=in_plane(j)[1], device_id_type=MESH)
     for j in range(1, G):
         pl.semaphore_signal(barrier, inc=1, device_id=in_group(j)[1], device_id_type=MESH)
-    pl.semaphore_wait(barrier, NP + G - 1)
+    for j in range(1, NY):
+        to = (2 * in_rows(j)[0] + 1 - c, e, n)
+        pl.semaphore_signal(barrier, inc=1, device_id=to, device_id_type=MESH)
+    pl.semaphore_wait(barrier, NP + G + NY - 2)
 
     mine_cols = rows(c * half, half, 128)
     other_cols = rows((1 - c) * half, half, 128)
@@ -377,7 +380,7 @@
         return ffw.at[of, rows(c * HR + ys * HB, HB), right]
 
     def by_distance(at):
-        return sorted((o for o in range(N) if o != at), key=lambda o: (abs(o - at), o))
+        return sorted((o for o in range(N) if o != at), key=lambda o: (abs(o - at), o if 2 * at >= N else -o))
 
     def pick(choices):
         value = choices[0]
@@ -926,18 +929,32 @@
         landed(zrecv.at[there], gz_s.at[j], gz_r.at[there])
         whole = whole + zrecv[there].astype(F32)
 
-    def fin_left(ys, es):
-        return fin.at[rows(c * HR + (es * NY + ys) * HS, HS), left]
-
-    def fin_right(ys, es):
-        return fin.at[rows(c * HR + (ys * NE + es) * HS, HS), right]
+    def fin_left(buffer, core, ys, es):
+        return buffer.at[rows(core * HR + (es * NY + ys) * HS, HS), left]
+
+    def fin_right(buffer, core, ys, es):
+        return buffer.at[rows(core * HR + (ys * NE + es) * HS, HS), right]
+
+    def fin_to_mate(i, ys, es):
+        for part, piece in enumerate((fin_left, fin_right)):
+            sem = 2 * NP - 2 + 2 * i + part
+            src, dst = piece(fin, c, ys, es), piece(fin_any, c, ys, es)
+            push(src, dst, ga_s.at[sem], ga_r.at[sem], mate)
+
+    def fin_from_mate(i, ys, es):
+        for part, piece in enumerate((fin_left, fin_right)):
+            sem = 2 * NP - 2 + 2 * i + part
+            landed(piece(fin_any, 1 - c, ys, es), ga_s.at[sem], ga_r.at[sem])
 
     fin[rows(c * HR + (e * NY + y) * HS, HS), left] = whole[:, 0:half].astype(BF16)
     fin[rows(c * HR + (y * NE + e) * HS, HS), right] = whole[:, half:].astype(BF16)
     for i in range(1, NP):
         _, to = in_plane(i)
-        push(fin_left(y, e), fin_left(y, e), ga_s.at[i], ga_r.at[i], to)
-        push(fin_right(y, e), fin_right(y, e), ga_s.at[NP - 1 + i], ga_r.at[NP - 1 + i], to)
+        at = fin_left(fin, c, y, e)
+        push(at, at, ga_s.at[i - 1], ga_r.at[i - 1], to)
+        at = fin_right(fin, c, y, e)
+        push(at, at, ga_s.at[NP - 2 + i], ga_r.at[NP - 2 + i], to)
+    fin_to_mate(0, y, e)
 
     whole = pqo[rows(e * ER, ER), rows(y * YW, YW, 128)].astype(F32)
     for i in range(1, NP):
@@ -972,39 +989,40 @@
         whole = whole + yqo[j].astype(F32)
     my_cols = rows(y * YW, YW, 128)
     fqo[c, :, my_cols] = whole.astype(BF16)
-    for i in range(1, NY):
-        _, to = in_rows(i)
-        at = fqo.at[c, :, my_cols]
-        push(at, at, qa_s.at[1 + i], qa_r.at[1 + i], to)
+    at = fqo.at[c, :, my_cols]
+    others = [(i, other) for i in range(NY) for other in range(2) if i or other]
+    for k, (i, other) in enumerate(others):
+        to = (2 * in_rows(i)[0] + (1 - c if other else c), e, n)
+        push(at, at, qa_s.at[k], qa_r.at[k], to)
     whole = zsp[...]
     for j in range(1, N):
         landed(ysp.at[j], qz_s.at[1, j - 1], qz_r.at[1, j - 1])
         whole = whole + ysp[j]
     fsp[:, mine_cols] = whole
     at = fsp.at[:, mine_cols]
-    push(at, at, qa_s.at[1], qa_r.at[1], mate)
-    for i in range(1, NY):
-        near, _ = in_rows(-i)
-        landed(fqo.at[c, :, rows(near * YW, YW, 128)], qa_s.at[1 + i], qa_r.at[1 + i])
-    push(fqo.at[c], fqo.at[c], qa_s.at[0], qa_r.at[0], mate)
-
+    push(at, at, qa_s.at[2 * NY - 1], qa_r.at[2 * NY - 1], mate)
     for i in range(1, NP):
         near, _ = in_plane(-i)
         ys, es = lax.div(near, NE), rem(near, NE)
-        landed(fin_left(ys, es), ga_s.at[i], ga_r.at[i])
-        landed(fin_right(ys, es), ga_s.at[NP - 1 + i], ga_r.at[NP - 1 + i])
+        landed(fin_left(fin, c, ys, es), ga_s.at[i - 1], ga_r.at[i - 1])
+        landed(fin_right(fin, c, ys, es), ga_s.at[NP - 2 + i], ga_r.at[NP - 2 + i])
+        fin_to_mate(i, ys, es)
     at = rows(c * HR, HR)
-    push(fin.at[at], fin_any.at[at], ga_s.at[0], ga_r.at[0], mate)
     fin_copy = pltpu.make_async_copy(fin.at[at], fin_any.at[at], loc_sem.at[6])
     fin_copy.start()
-    landed(fsp.at[:, other_cols], qa_s.at[1], qa_r.at[1])
+    landed(fsp.at[:, other_cols], qa_s.at[2 * NY - 1], qa_r.at[2 * NY - 1])
     small_ref[...] = fsp[...]
-    landed(fqo.at[1 - c], qa_s.at[0], qa_r.at[0])
+    for k, (i, other) in enumerate(others):
+        near, _ = in_rows(-i)
+        at = fqo.at[1 - c if other else c, :, rows(near * YW, YW, 128)]
+        landed(at, qa_s.at[k], qa_r.at[k])
     fqo_ref[...] = fqo[...]
     ig_copy.wait()
     out_copy.wait()
     fin_copy.wait()
-    landed(fin_any.at[rows((1 - c) * HR, HR)], ga_s.at[0], ga_r.at[0])
+    for i in range(NP):
+        near, _ = in_plane(-i)
+        fin_from_mate(i, lax.div(near, NE), rem(near, NE))
 
     for copy in started:
         copy.wait_send()
@@ -1124,11 +1142,11 @@
         (N,),
         (4, N, max(NE, NY) - 1),
         (N,),
-        (2 * NP - 1,),
+        (4 * NP - 2,),
         (2,),
         (2, NP - 1),
         (2, N - 1),
-        (NY + 1,),
+        (2 * NY,),
     ]
     sems = [pltpu.SemaphoreType.DMA((7,))]
     for shape in pairs:

time: 90.8 us -> 87.9 us (0.968)
  Pallas kernels: 89.8 us -> 86.9 us
    pallas_call x1, Pallas kernels: 86.9 us -> 84.1 us  [run(): pl.pallas_call(functools.partial(kernel, z), out_shape=[pltpu.VMEM(s, t)...]
where the time goes in v4:
time: 87.9 us; the launch traced here: 87.7 us
  Pallas kernels  86.9 us (99%)
    pallas_call x1, Pallas kernels, run(): pl.pallas_call(functools.partial(kernel, z), out_shape=[pltpu.VMEM(s, t)...  84.1 us
    pallas_call x1, Pallas kernels, finish(): pl.pallas_call(functools.partial(finish_kernel, z), out_shape=[jax.ShapeD...  2.82 us

profile of v4, /device:TPU:0, one launch (start us, length us, event | category | flops | bytes accessed | tf_op | source)
XLA Modules:
  0.0 87.7 jit_solution(16988248835475346881)
XLA Ops:
  0.7 84.1 %layer.1 = (f32[2048,128]{1,0:T(8,128)S(1)}, f32[512,512]{1,0:T(8,128)S(1)}, bf16[1024,512]{1,0:T(8,128)(2,1)S(1)}, bf16[2,80,512]{2,1,0:T(8,128)(2,1)S(1)}, f32[24,512]{1,0:T(8,128)S(1)}) custom-call(f32[4096,512]{1,0:T(8,128)} %x_any.1, s32[4,1024]{1,0:T(4,128)} %seg_ref.1, s32[2,4096]{1,0:T(2,128)} %bitcast.35, f32[1,512]{1,0:T(1,128)} %bitcast.39, ...), custom_call_target="tpu_custom_call" | custom-call | tf_op jit(solution)/shard_map/layer/pallas_call | solution.py:1162
  84.8 2.8 %finish.1 = (f32[2048,128]{1,0:T(8,128)}, f32[512,512]{1,0:T(8,128)}, f32[1,512]{1,0:T(1,128)}, f32[1,512]{1,0:T(1,128)}, f32[64,512]{1,0:T(8,128)}, /*index=5*/...) custom-call(f32[2048,128]{1,0:T(8,128)S(1)} %get-tuple-element.43.ou, ...), custom_call_target="tpu_custom_call" | custom-call | tf_op jit(solution)/shard_map/finish/pallas_call | solution.py:1271

commit v5 on v4

--- a/solution.py
+++ b/solution.py
@@ -17,6 +17,8 @@
 F32 = jnp.float32
 BF16 = jnp.bfloat16
 MESH = pl.DeviceIdType.MESH
+GROUP_BYTES = 2**20
+GROUPS = 16
 
 
 def dot(a, b):
@@ -92,7 +94,7 @@
     cot_ref,
     out_any,
     ig_any,
-    fin_any,
+    g_ref,
     fqo_ref,
     small_ref,
     out_ref,
@@ -137,6 +139,7 @@
     delta,
     outd,
     gsend,
+    ruler,
     crecv,
     psend,
     pea,
@@ -163,45 +166,27 @@
     ysp,
     fsp,
     loc_sem,
-    w_s,
+    send_sems,
     w_r,
-    wm_s,
     wm_r,
-    b_s,
     b_r,
-    q_s,
     q_r,
-    qm_s,
     qm_r,
-    o_s,
     o_r,
-    om_s,
     om_r,
-    fp_s,
     fp_r,
-    fm_s,
     fm_r,
-    ct_s,
     ct_r,
-    od_s,
     od_r,
     hl_s,
     hl_r,
-    gc_s,
     gc_r,
-    gp_s,
     gp_r,
-    gz_s,
     gz_r,
-    ga_s,
     ga_r,
-    qc_s,
     qc_r,
-    qp_s,
     qp_r,
-    qz_s,
     qz_r,
-    qa_s,
     qa_r,
     fz_s,
     fz_r,
@@ -232,25 +217,32 @@
         at = rem(y + j + NY, NY)
         return at, (2 * at + c, e, n)
 
-    started = []
-
-    def push(src, dst, send, recv, device):
+    sent = [0, 0]
+
+    def push(src, dst, recv, device):
+        size = math.prod(src.shape) * jnp.dtype(src.dtype).itemsize
+        if src.shape[-1] == 128 and src.dtype == F32:
+            kind = 0
+        else:
+            if sent[-1] + size > GROUP_BYTES:
+                sent.append(0)
+            kind = len(sent) - 1
+        sent[kind] += size
         copy = pltpu.make_async_remote_copy(
             src_ref=src,
             dst_ref=dst,
-            send_sem=send,
+            send_sem=send_sems.at[kind],
             recv_sem=recv,
             device_id=device,
             device_id_type=MESH,
         )
         copy.start()
-        started.append(copy)
-
-    def landed(dst, send, recv):
+
+    def landed(dst, recv):
         pltpu.make_async_remote_copy(
             src_ref=dst,
             dst_ref=dst,
-            send_sem=send,
+            send_sem=recv,
             recv_sem=recv,
             device_id=mate,
             device_id_type=MESH,
@@ -308,36 +300,36 @@
     def shard_at(i, j):
         return rem(e - i + NE, NE) * N + rem(n - j + N, N)
 
-    def spread_start(part, send, recv):
+    def spread_start(part, recv):
         for j in range(1, N):
             at = part(here)
-            push(at, at, send.at[j - 1], recv.at[j - 1], in_line(j)[1])
+            push(at, at, recv.at[j - 1], in_line(j)[1])
         for i in range(1, NE):
             at = part(here)
-            push(at, at, send.at[i * N - 1], recv.at[i * N - 1], in_expert(i)[1])
-
-    def spread_on(part, send, recv, to_mate):
+            push(at, at, recv.at[i * N - 1], in_expert(i)[1])
+
+    def spread_on(part, recv, to_mate):
         for j in range(1, N):
             at = part(shard_at(0, j))
-            landed(at, send.at[j - 1], recv.at[j - 1])
+            landed(at, recv.at[j - 1])
             for i in range(1, NE):
-                push(at, at, send.at[i * N + j - 1], recv.at[i * N + j - 1], in_expert(i)[1])
+                push(at, at, recv.at[i * N + j - 1], in_expert(i)[1])
             if to_mate is not None:
-                push(at, at, to_mate[0].at[j - 1], to_mate[1].at[j - 1], mate)
-
-    def spread_end(part, send, recv, to_mate):
+                push(at, at, to_mate.at[j - 1], mate)
+
+    def spread_end(part, recv, to_mate):
         for i in range(1, NE):
             for j in range(N):
                 at = part(shard_at(i, j))
-                landed(at, send.at[i * N + j - 1], recv.at[i * N + j - 1])
+                landed(at, recv.at[i * N + j - 1])
                 if to_mate is not None:
-                    push(at, at, to_mate[0].at[i * N + j - 1], to_mate[1].at[i * N + j - 1], mate)
+                    push(at, at, to_mate.at[i * N + j - 1], mate)
 
     def spread_wait(part, to_mate):
         for i in range(NE):
             for j in range(N):
                 if i or j:
-                    landed(part(shard_at(i, j)), to_mate[0].at[i * N + j - 1], to_mate[1].at[i * N + j - 1])
+                    landed(part(shard_at(i, j)), to_mate.at[i * N + j - 1])
 
     def bias_part(g):
         return bias.at[g]
@@ -356,9 +348,9 @@
 
     for j in range(1, N):
         at = wkv.at[c, rows(n * HP, HP)]
-        push(at, at, w_s.at[j - 1], w_r.at[j - 1], in_line(j)[1])
-    spread_start(q_part, q_s, q_r)
-    spread_start(bias_part, b_s, b_r)
+        push(at, at, w_r.at[j - 1], in_line(j)[1])
+    spread_start(q_part, q_r)
+    spread_start(bias_part, b_r)
     up_copy.wait()
     down_copy.wait()
     FR = D + FL
@@ -419,8 +411,8 @@
 
         @pl.when(valid)
         def _():
-            landed(left_slice(of, y, e), fz_s.at[0, 0, of], fz_r.at[0, of])
-            landed(right_slice(of, y, e), fz_s.at[1, 0, of], fz_r.at[1, of])
+            landed(left_slice(of, y, e), fz_r.at[0, of])
+            landed(right_slice(of, y, e), fz_r.at[1, of])
 
     def shards_start():
         line_push(n, 1, n + 1 < N)
@@ -436,36 +428,36 @@
         there = shard_of[j]
         at = left_slice(there, y, e)
         for i in range(1, NY):
-            push(at, at, fp_s.at[0, j - 1, i - 1], fp_r.at[0, j - 1, i - 1], in_rows(i)[1])
+            push(at, at, fp_r.at[0, j - 1, i - 1], in_rows(i)[1])
         at = right_slice(there, y, e)
         for i in range(1, NE):
-            push(at, at, fp_s.at[1, j - 1, i - 1], fp_r.at[1, j - 1, i - 1], in_expert(i)[1])
+            push(at, at, fp_r.at[1, j - 1, i - 1], in_expert(i)[1])
 
     def plane_turn(j):
         there = shard_of[j]
         for i in range(1, NY):
             near, _ = in_rows(-i)
-            landed(left_slice(there, near, e), fp_s.at[0, j - 1, i - 1], fp_r.at[0, j - 1, i - 1])
+            landed(left_slice(there, near, e), fp_r.at[0, j - 1, i - 1])
         at = left_half(there, e)
         for i in range(1, NE):
-            push(at, at, fp_s.at[2, j - 1, i - 1], fp_r.at[2, j - 1, i - 1], in_expert(i)[1])
+            push(at, at, fp_r.at[2, j - 1, i - 1], in_expert(i)[1])
         for i in range(1, NE):
             near, _ = in_expert(-i)
-            landed(right_slice(there, y, near), fp_s.at[1, j - 1, i - 1], fp_r.at[1, j - 1, i - 1])
+            landed(right_slice(there, y, near), fp_r.at[1, j - 1, i - 1])
         at = right_half(there, y)
         for i in range(1, NY):
-            push(at, at, fp_s.at[3, j - 1, i - 1], fp_r.at[3, j - 1, i - 1], in_rows(i)[1])
+            push(at, at, fp_r.at[3, j - 1, i - 1], in_rows(i)[1])
 
     def mate_on(j):
         there = shard_of[j]
         for i in range(1, NE):
             near, _ = in_expert(-i)
-            landed(left_half(there, near), fp_s.at[2, j - 1, i - 1], fp_r.at[2, j - 1, i - 1])
+            landed(left_half(there, near), fp_r.at[2, j - 1, i - 1])
         for i in range(1, NY):
             near, _ = in_rows(-i)
-            landed(right_half(there, near), fp_s.at[3, j - 1, i - 1], fp_r.at[3, j - 1, i - 1])
+            landed(right_half(there, near), fp_r.at[3, j - 1, i - 1])
         at = ffw.at[there, rows(c * HR, HR)]
-        push(at, at, fm_s.at[j - 1], fm_r.at[j - 1], mate)
+        push(at, at, fm_r.at[j - 1], mate)
 
     x_copy.wait()
     gain_one, shift_one = g1_ref[...], s1_ref[...]
@@ -502,20 +494,20 @@
     for j in range(1, N):
         there, _ = in_line(-j)
         at = wkv.at[c, rows(there * HP, HP)]
-        landed(at, w_s.at[j - 1], w_r.at[j - 1])
-        push(at, at, wm_s.at[j - 1], wm_r.at[j - 1], mate)
-    spread_on(q_part, q_s, q_r, (qm_s, qm_r))
-    spread_on(bias_part, b_s, b_r, None)
+        landed(at, w_r.at[j - 1])
+        push(at, at, wm_r.at[j - 1], mate)
+    spread_on(q_part, q_r, qm_r)
+    spread_on(bias_part, b_r, None)
     shards_start()
-    spread_start(o_part, o_s, o_r)
+    spread_start(o_part, o_r)
 
     for j in range(1, N):
         there, _ = in_line(-j)
-        landed(wkv.at[1 - c, rows(there * HP, HP)], wm_s.at[j - 1], wm_r.at[j - 1])
+        landed(wkv.at[1 - c, rows(there * HP, HP)], wm_r.at[j - 1])
     kn[...] = dot_nt(rw[...], wkv[0]).astype(BF16)
     kt[...] = dot_nt(wkv[0], rw[...]).astype(BF16)
-    spread_end(q_part, q_s, q_r, (qm_s, qm_r))
-    spread_end(bias_part, b_s, b_r, None)
+    spread_end(q_part, q_r, qm_r)
+    spread_end(bias_part, b_r, None)
     columns = [jnp.transpose(bias[g, 0:16, :]) for g in range(G)]
     for part in range(N):
         vcol[part * HP : (part + 1) * HP, :] = jnp.broadcast_to(columns[part][0:HP, 7:8], (HP, 128))
@@ -523,7 +515,7 @@
     vn[...] = (dot_nt(rw[...], wkv[1]) + value_row).astype(BF16)
     vt[...] = (dot_nt(wkv[1], rw[...]) + vcol[:, 0:1]).astype(BF16)
 
-    spread_wait(q_other, (qm_s, qm_r))
+    spread_wait(q_other, qm_r)
     qt[...] = dot_nt(wq[...], rw[own, :])
 
     def expert_rows(at, i, part):
@@ -561,7 +553,7 @@
     attend(1)
     shards_on(1)
     plane_on(1)
-    spread_on(o_part, o_s, o_r, (om_s, om_r))
+    spread_on(o_part, o_r, om_r)
     plane_turn(1)
     shards_on(2)
     plane_on(2)
@@ -572,11 +564,10 @@
         push(
             cot_ref.at[rows(there * T, T, 128)],
             cot.at[:, rows(n * CW, CW, 128)],
-            ct_s.at[j - 1],
             ct_r.at[j - 1],
             to,
         )
-    spread_end(o_part, o_s, o_r, (om_s, om_r))
+    spread_end(o_part, o_r, om_r)
 
     for part in range(N):
         for at in range(NE):
@@ -588,7 +579,7 @@
                     rounded_mix = mix[k, part * HP : (part + 1) * HP, :].astype(BF16).astype(F32)
                     gated = gated + rounded_mix * (hot[k][x : x + 1, :] * gate[k])
                 mixg[lo : lo + HP, :] = gated.astype(BF16)
-    spread_wait(o_other, (om_s, om_r))
+    spread_wait(o_other, om_r)
     out_b, down_b = ob_ref[...], db_ref[...]
     gain_two, shift_two = g2_ref[...], s2_ref[...]
     attention = dot_tn(mixg[...], wo[...]) + out_b
@@ -606,61 +597,61 @@
 
     def core_start(j):
         push(
-            gsend.at[j, rows((1 - c) * HR, HR)], crecv.at[j], gc_s.at[j], gc_r.at[j], mate
+            gsend.at[j, rows((1 - c) * HR, HR)], crecv.at[j], gc_r.at[j], mate
         )
 
     def plane_start(j):
-        landed(crecv.at[j], gc_s.at[j], gc_r.at[j])
+        landed(crecv.at[j], gc_r.at[j])
         psend[j] = (
             gsend[j, rows(c * HR, HR), :].astype(F32) + crecv[j].astype(F32)
         ).astype(BF16)
         for i in range(1, NE):
             there, to = in_expert(i)
             src = psend.at[j, rows(there * HA, HA), left]
-            push(src, pea.at[j, i], gp_s.at[0, j, i - 1], gp_r.at[0, j, i - 1], to)
+            push(src, pea.at[j, i], gp_r.at[0, j, i - 1], to)
         for i in range(1, NY):
             there, to = in_rows(i)
             src = psend.at[j, rows(there * HB, HB), right]
-            push(src, pya.at[j, i], gp_s.at[1, j, i - 1], gp_r.at[1, j, i - 1], to)
+            push(src, pya.at[j, i], gp_r.at[1, j, i - 1], to)
 
     def plane_middle(j):
         whole = psend[j, rows(e * HA, HA), left].astype(F32)
         for i in range(1, NE):
-            landed(pea.at[j, i], gp_s.at[0, j, i - 1], gp_r.at[0, j, i - 1])
+            landed(pea.at[j, i], gp_r.at[0, j, i - 1])
             whole = whole + pea[j, i].astype(F32)
         mea[j] = whole.astype(BF16)
         for i in range(1, NY):
             there, to = in_rows(i)
             src = mea.at[j, rows(there * HS, HS)]
-            push(src, pyb.at[j, i], gp_s.at[2, j, i - 1], gp_r.at[2, j, i - 1], to)
+            push(src, pyb.at[j, i], gp_r.at[2, j, i - 1], to)
         whole = psend[j, rows(y * HB, HB), right].astype(F32)
         for i in range(1, NY):
-            landed(pya.at[j, i], gp_s.at[1, j, i - 1], gp_r.at[1, j, i - 1])
+            landed(pya.at[j, i], gp_r.at[1, j, i - 1])
             whole = whole + pya[j, i].astype(F32)
         mya[j] = whole.astype(BF16)
         for i in range(1, NE):
             there, to = in_expert(i)
             src = mya.at[j, rows(there * HS, HS)]
-            push(src, peb.at[j, i], gp_s.at[3, j, i - 1], gp_r.at[3, j, i - 1], to)
+            push(src, peb.at[j, i], gp_r.at[3, j, i - 1], to)
 
     def line_start(j):
         whole = mea[j, rows(y * HS, HS), :].astype(F32)
         for i in range(1, NY):
-            landed(pyb.at[j, i], gp_s.at[2, j, i - 1], gp_r.at[2, j, i - 1])
+            landed(pyb.at[j, i], gp_r.at[2, j, i - 1])
             whole = whole + pyb[j, i].astype(F32)
         zsend[j, :, left] = whole.astype(BF16)
         whole = mya[j, rows(e * HS, HS), :].astype(F32)
         for i in range(1, NE):
-            landed(peb.at[j, i], gp_s.at[3, j, i - 1], gp_r.at[3, j, i - 1])
+            landed(peb.at[j, i], gp_r.at[3, j, i - 1])
             whole = whole + peb[j, i].astype(F32)
         zsend[j, :, right] = whole.astype(BF16)
         if j:
-            push(zsend.at[j], zrecv.at[n], gz_s.at[j], gz_r.at[n], (d, e, shard_of[j]))
+            push(zsend.at[j], zrecv.at[n], gz_r.at[n], (d, e, shard_of[j]))
 
     def forward(j):
         there = shard_of[j]
         if j:
-            landed(ffw.at[there, rows((1 - c) * HR, HR)], fm_s.at[j - 1], fm_r.at[j - 1])
+            landed(ffw.at[there, rows((1 - c) * HR, HR)], fm_r.at[j - 1])
         up_b = jnp.concatenate(
             [bias[e * N + there, i : i + 1, :] for i in range(FL // 128)], axis=1
         )
@@ -701,7 +692,7 @@
     def cotangent_wait():
         for j in range(1, N):
             there, _ = in_line(-j)
-            landed(cot.at[:, rows(there * CW, CW, 128)], ct_s.at[j - 1], ct_r.at[j - 1])
+            landed(cot.at[:, rows(there * CW, CW, 128)], ct_r.at[j - 1])
 
     forward(0)
     plane_turn(2)
@@ -722,7 +713,7 @@
     outd[n] = delta[:, rows(n * CW, CW, 128)]
     for j in range(1, N):
         there, to = in_line(j)
-        push(delta.at[:, rows(there * CW, CW, 128)], outd.at[n], od_s.at[j - 1], od_r.at[j - 1], to)
+        push(delta.at[:, rows(there * CW, CW, 128)], outd.at[n], od_r.at[j - 1], to)
 
     backward(3)
     plane_start(2)
@@ -850,7 +841,7 @@
         gqo[0, g * SH : g * SH + R, :] = query_w_grad[g * R : (g + 1) * R, :]
         gqo[0, g * SH + R : (g + 1) * SH, :] = key_w_grad[shared, :]
         gqo[1, g * SH + R : (g + 1) * SH, :] = value_w_grad[shared, :]
-    push(gqo.at[1 - c], cqo, qc_s.at[0], qc_r.at[0], mate)
+    push(gqo.at[1 - c], cqo, qc_r.at[0], mate)
     plane_middle(3)
     line_start(1)
     ones = jnp.ones((8, T), BF16)
@@ -865,12 +856,12 @@
     sp[15:16, 0:HEAD] = jnp.sum(dv[...], axis=0, keepdims=True)
     YW = D // NY
     ER = N * SH
-    landed(cqo, qc_s.at[0], qc_r.at[0])
+    landed(cqo, qc_r.at[0])
     pqo[...] = (gqo[c].astype(F32) + cqo[...].astype(F32)).astype(BF16)
     for i in range(1, NP):
         there, to = in_plane(i)
         src = pqo.at[rows(rem(there, NE) * ER, ER), rows(lax.div(there, NE) * YW, YW, 128)]
-        push(src, rqo.at[i], qp_s.at[0, i - 1], qp_r.at[0, i - 1], to)
+        push(src, rqo.at[i], qp_r.at[0, i - 1], to)
     plane_middle(0)
     line_start(2)
     line_start(3)
@@ -913,20 +904,20 @@
     sp[1:2, :] = sums[1]
     for j in range(8 + N, 15):
         sp[j : j + 1, :] = zero_row
-    push(sp.at[:, other_cols], csp, qc_s.at[1], qc_r.at[1], mate)
-
-    landed(csp, qc_s.at[1], qc_r.at[1])
+    push(sp.at[:, other_cols], csp, qc_r.at[1], mate)
+
+    landed(csp, qc_r.at[1])
     psp[...] = sp[:, mine_cols] + csp[...]
     for i in range(1, NP):
         _, to = in_plane(i)
-        push(psp, rsp.at[i], qp_s.at[1, i - 1], qp_r.at[1, i - 1], to)
+        push(psp, rsp.at[i], qp_r.at[1, i - 1], to)
 
     line_start(0)
 
     whole = zsend[0].astype(F32)
     for j in range(1, N):
         there, _ = in_line(-j)
-        landed(zrecv.at[there], gz_s.at[j], gz_r.at[there])
+        landed(zrecv.at[there], gz_r.at[there])
         whole = whole + zrecv[there].astype(F32)
 
     def fin_left(buffer, core, ys, es):
@@ -938,45 +929,45 @@
     def fin_to_mate(i, ys, es):
         for part, piece in enumerate((fin_left, fin_right)):
             sem = 2 * NP - 2 + 2 * i + part
-            src, dst = piece(fin, c, ys, es), piece(fin_any, c, ys, es)
-            push(src, dst, ga_s.at[sem], ga_r.at[sem], mate)
+            at = piece(fin, c, ys, es)
+            push(at, at, ga_r.at[sem], mate)
 
     def fin_from_mate(i, ys, es):
         for part, piece in enumerate((fin_left, fin_right)):
             sem = 2 * NP - 2 + 2 * i + part
-            landed(piece(fin_any, 1 - c, ys, es), ga_s.at[sem], ga_r.at[sem])
+            landed(piece(fin, 1 - c, ys, es), ga_r.at[sem])
 
     fin[rows(c * HR + (e * NY + y) * HS, HS), left] = whole[:, 0:half].astype(BF16)
     fin[rows(c * HR + (y * NE + e) * HS, HS), right] = whole[:, half:].astype(BF16)
     for i in range(1, NP):
         _, to = in_plane(i)
         at = fin_left(fin, c, y, e)
-        push(at, at, ga_s.at[i - 1], ga_r.at[i - 1], to)
+        push(at, at, ga_r.at[i - 1], to)
         at = fin_right(fin, c, y, e)
-        push(at, at, ga_s.at[NP - 2 + i], ga_r.at[NP - 2 + i], to)
+        push(at, at, ga_r.at[NP - 2 + i], to)
     fin_to_mate(0, y, e)
 
     whole = pqo[rows(e * ER, ER), rows(y * YW, YW, 128)].astype(F32)
     for i in range(1, NP):
-        landed(rqo.at[i], qp_s.at[0, i - 1], qp_r.at[0, i - 1])
+        landed(rqo.at[i], qp_r.at[0, i - 1])
         whole = whole + rqo[i].astype(F32)
     zqo[...] = whole.astype(BF16)
     for j in range(1, N):
         there, to = in_line(j)
-        push(zqo.at[rows(there * SH, SH)], yqo.at[j], qz_s.at[0, j - 1], qz_r.at[0, j - 1], to)
+        push(zqo.at[rows(there * SH, SH)], yqo.at[j], qz_r.at[0, j - 1], to)
     whole = psp[...]
     for i in range(1, NP):
-        landed(rsp.at[i], qp_s.at[1, i - 1], qp_r.at[1, i - 1])
+        landed(rsp.at[i], qp_r.at[1, i - 1])
         whole = whole + rsp[i]
     zsp[...] = whole
     for j in range(1, N):
         _, to = in_line(j)
-        push(zsp, ysp.at[j], qz_s.at[1, j - 1], qz_r.at[1, j - 1], to)
+        push(zsp, ysp.at[j], qz_r.at[1, j - 1], to)
 
     cols_copy.wait()
     for j in range(1, N):
         there, _ = in_line(-j)
-        landed(outd.at[there], od_s.at[j - 1], od_r.at[j - 1])
+        landed(outd.at[there], od_r.at[j - 1])
     for j in range(N):
         at = pl.ds(j * T, T)
         out_ref[at, :] = out_ref[at, :] + outd[j].astype(F32)
@@ -985,7 +976,7 @@
 
     whole = zqo[rows(n * SH, SH), :].astype(F32)
     for j in range(1, N):
-        landed(yqo.at[j], qz_s.at[0, j - 1], qz_r.at[0, j - 1])
+        landed(yqo.at[j], qz_r.at[0, j - 1])
         whole = whole + yqo[j].astype(F32)
     my_cols = rows(y * YW, YW, 128)
     fqo[c, :, my_cols] = whole.astype(BF16)
@@ -993,39 +984,49 @@
     others = [(i, other) for i in range(NY) for other in range(2) if i or other]
     for k, (i, other) in enumerate(others):
         to = (2 * in_rows(i)[0] + (1 - c if other else c), e, n)
-        push(at, at, qa_s.at[k], qa_r.at[k], to)
+        push(at, at, qa_r.at[k], to)
     whole = zsp[...]
     for j in range(1, N):
-        landed(ysp.at[j], qz_s.at[1, j - 1], qz_r.at[1, j - 1])
+        landed(ysp.at[j], qz_r.at[1, j - 1])
         whole = whole + ysp[j]
     fsp[:, mine_cols] = whole
     at = fsp.at[:, mine_cols]
-    push(at, at, qa_s.at[2 * NY - 1], qa_r.at[2 * NY - 1], mate)
+    push(at, at, qa_r.at[2 * NY - 1], mate)
     for i in range(1, NP):
         near, _ = in_plane(-i)
         ys, es = lax.div(near, NE), rem(near, NE)
-        landed(fin_left(fin, c, ys, es), ga_s.at[i - 1], ga_r.at[i - 1])
-        landed(fin_right(fin, c, ys, es), ga_s.at[NP - 2 + i], ga_r.at[NP - 2 + i])
+        landed(fin_left(fin, c, ys, es), ga_r.at[i - 1])
+        landed(fin_right(fin, c, ys, es), ga_r.at[NP - 2 + i])
         fin_to_mate(i, ys, es)
     at = rows(c * HR, HR)
-    fin_copy = pltpu.make_async_copy(fin.at[at], fin_any.at[at], loc_sem.at[6])
-    fin_copy.start()
-    landed(fsp.at[:, other_cols], qa_s.at[2 * NY - 1], qa_r.at[2 * NY - 1])
+    g_ref[at, :] = fin[at, :].astype(F32)
+    landed(fsp.at[:, other_cols], qa_r.at[2 * NY - 1])
     small_ref[...] = fsp[...]
     for k, (i, other) in enumerate(others):
         near, _ = in_rows(-i)
         at = fqo.at[1 - c if other else c, :, rows(near * YW, YW, 128)]
-        landed(at, qa_s.at[k], qa_r.at[k])
+        landed(at, qa_r.at[k])
     fqo_ref[...] = fqo[...]
     ig_copy.wait()
     out_copy.wait()
-    fin_copy.wait()
     for i in range(NP):
         near, _ = in_plane(-i)
         fin_from_mate(i, lax.div(near, NE), rem(near, NE))
-
-    for copy in started:
-        copy.wait_send()
+    at = rows((1 - c) * HR, HR)
+    g_ref[at, :] = fin[at, :].astype(F32)
+
+    for kind, size in enumerate(sent):
+        at = ruler.at[pl.ds(0, size // 256)]
+        if kind == 0:
+            at = bias.at[pl.ds(0, size // (16 * 128 * 4))]
+        pltpu.make_async_remote_copy(
+            src_ref=at,
+            dst_ref=at,
+            send_sem=send_sems.at[kind],
+            recv_sem=send_sems.at[kind],
+            device_id=mate,
+            device_id_type=MESH,
+        ).wait_send()
     for valid, copies in maybe_started:
 
         @pl.when(valid)
@@ -1100,6 +1101,7 @@
         ((T, D), BF16),
         ((N, T, D // N), BF16),
         ((N, FR, D), BF16),
+        ((GROUP_BYTES // 256, 128), BF16),
         ((N, HR, D), BF16),
         ((N, HR, D), BF16),
         ((N, NE, HR // NE, D // 2), BF16),
@@ -1148,14 +1150,15 @@
         (2, N - 1),
         (2 * NY,),
     ]
-    sems = [pltpu.SemaphoreType.DMA((7,))]
-    for shape in pairs:
-        sems += [pltpu.SemaphoreType.DMA(shape)] * 2
+    HALO = 11
+    sems = [pltpu.SemaphoreType.DMA((6,)), pltpu.SemaphoreType.DMA((GROUPS,))]
+    for at, shape in enumerate(pairs):
+        sems += [pltpu.SemaphoreType.DMA(shape)] * (2 if at == HALO else 1)
     sems += [pltpu.SemaphoreType.DMA((2, 2, N)), pltpu.SemaphoreType.DMA((2, N))]
     outs = [
         ((N * T, D // N), F32),
         ((T, D), F32),
-        ((FR, D), BF16),
+        ((FR, D), F32),
         ((2, SH, D), BF16),
         ((SMALL, D), F32),
     ]
@@ -1163,7 +1166,7 @@
         functools.partial(kernel, z),
         out_shape=[pltpu.VMEM(s, t) for s, t in outs],
         in_specs=[anywhere] + [vmem] * (7 + len(vectors)) + [anywhere] * 2 + [vmem],
-        out_specs=[pl.BlockSpec(memory_space=pl.ANY)] * 3 + [vmem] * 2,
+        out_specs=[pl.BlockSpec(memory_space=pl.ANY)] * 2 + [vmem] * 3,
         scratch_shapes=[pltpu.VMEM(s, t) for s, t in scratch] + sems,
         compiler_params=pltpu.CompilerParams(
             collective_id=0, has_side_effects=True, vmem_limit_bytes=58 * 2**20
@@ -1176,7 +1179,7 @@
     z,
     out_in,
     ig_in,
-    fin_ref,
+    g_in,
     fqo_ref,
     small_ref,
     out_any,
@@ -1198,8 +1201,6 @@
     ub_ref,
     gdown_any,
     db_ref,
-    gup,
-    gdown,
     sems,
 ):
     e, n = lax.axis_index("expert"), lax.axis_index("narrow")
@@ -1212,10 +1213,8 @@
 
     put(out_in, out_any)
     put(ig_in, ig_out)
-    gup[...] = fin_ref[0:D, :].astype(F32)
-    put(gup, gup_any)
-    gdown[...] = fin_ref[D : D + z.ff_local, :].astype(F32)
-    put(gdown, gdown_any)
+    put(g_in.at[pl.ds(0, D)], gup_any)
+    put(g_in.at[pl.ds(D, z.ff_local)], gdown_any)
     gq_ref[...] = fqo_ref[0, 0:R, :].astype(F32)
     go_ref[...] = fqo_ref[1, 0:R, :].astype(F32)
     gk_ref[...] = fqo_ref[0, R : R + HP, :].astype(F32)
@@ -1271,11 +1270,9 @@
     return pl.pallas_call(
         functools.partial(finish_kernel, z),
         out_shape=[jax.ShapeDtypeStruct(s, F32) for s in shapes],
-        in_specs=[pl.BlockSpec(memory_space=pl.ANY)] * 2 + [vmem] * 3,
+        in_specs=[pl.BlockSpec(memory_space=pl.ANY)] * 3 + [vmem] * 2,
         out_specs=[anywhere] * 2 + [vmem] * 13 + [anywhere, vmem, anywhere, vmem],
         scratch_shapes=[
-            pltpu.VMEM((D, FL), F32),
-            pltpu.VMEM((FL, D), F32),
             pltpu.SemaphoreType.DMA((4,)),
         ],
         compiler_params=pltpu.CompilerParams(vmem_limit_bytes=16 * 2**20),

time: 87.9 us -> 86.9 us (0.989)
  Pallas kernels: 86.9 us -> 85.9 us
    pallas_call x1, Pallas kernels: 84.1 us -> 83.1 us  [run(): pl.pallas_call(functools.partial(kernel, z), out_shape=[pltpu.VMEM(s, t)...]
where the time goes in v5:
time: 86.9 us; the launch traced here: 86.7 us
  Pallas kernels  85.9 us (99%)
    pallas_call x1, Pallas kernels, run(): pl.pallas_call(functools.partial(kernel, z), out_shape=[pltpu.VMEM(s, t)...  83.1 us
    pallas_call x1, Pallas kernels, finish(): pl.pallas_call(functools.partial(finish_kernel, z), out_shape=[jax.ShapeD...  2.82 us

profile of v5, /device:TPU:0, one launch (start us, length us, event | category | flops | bytes accessed | tf_op | source)
XLA Modules:
  0.0 86.7 jit_solution(6784990556774369741)
XLA Ops:
  0.7 83.1 %layer.1 = (f32[2048,128]{1,0:T(8,128)S(1)}, f32[512,512]{1,0:T(8,128)S(1)}, f32[1024,512]{1,0:T(8,128)S(1)}, bf16[2,80,512]{2,1,0:T(8,128)(2,1)S(1)}, f32[24,512]{1,0:T(8,128)S(1)}) custom-call(f32[4096,512]{1,0:T(8,128)} %x_any.1, s32[4,1024]{1,0:T(4,128)} %seg_ref.1, s32[2,4096]{1,0:T(2,128)} %bitcast.35, f32[1,512]{1,0:T(1,128)} %bitcast.39, ...), custom_call_target="tpu_custom_call" | custom-call | tf_op jit(solution)/shard_map/layer/pallas_call | solution.py:1165
  83.7 2.8 %finish.1 = (f32[2048,128]{1,0:T(8,128)}, f32[512,512]{1,0:T(8,128)}, f32[1,512]{1,0:T(1,128)}, f32[1,512]{1,0:T(1,128)}, f32[64,512]{1,0:T(8,128)}, /*index=5*/...) custom-call(f32[2048,128]{1,0:T(8,128)S(1)} %get-tuple-element.43.ou, ...), custom_call_target="tpu_custom_call" | custom-call | tf_op jit(solution)/shard_map/finish/pallas_call | solution.py:1270

commit v6 on v5

--- a/solution.py
+++ b/solution.py
@@ -17,8 +17,8 @@
 F32 = jnp.float32
 BF16 = jnp.bfloat16
 MESH = pl.DeviceIdType.MESH
-GROUP_BYTES = 2**20
-GROUPS = 16
+GROUP_BYTES = 2**21
+GROUPS = 8
 
 
 def dot(a, b):
@@ -218,16 +218,34 @@
         return at, (2 * at + c, e, n)
 
     sent = [0, 0]
+    noted = {}
+
+    def either(name, valid, block):
+        again = name in noted
+        kinds = noted.setdefault(name, [])
+        turn = iter(list(kinds)) if again else None
+
+        @pl.when(valid)
+        def _():
+            mode.append((kinds, turn))
+            block()
+            mode.pop()
+
+    mode = []
 
     def push(src, dst, recv, device):
         size = math.prod(src.shape) * jnp.dtype(src.dtype).itemsize
-        if src.shape[-1] == 128 and src.dtype == F32:
+        if mode and mode[-1][1] is not None:
+            kind = next(mode[-1][1])
+        else:
             kind = 0
-        else:
-            if sent[-1] + size > GROUP_BYTES:
-                sent.append(0)
-            kind = len(sent) - 1
-        sent[kind] += size
+            if not (src.shape[-1] == 128 and src.dtype == F32):
+                if sent[-1] + size > GROUP_BYTES:
+                    sent.append(0)
+                kind = len(sent) - 1
+            sent[kind] += size
+            if mode:
+                mode[-1][0].append(kind)
         copy = pltpu.make_async_remote_copy(
             src_ref=src,
             dst_ref=dst,
@@ -247,6 +265,10 @@
             device_id=mate,
             device_id_type=MESH,
         ).wait_recv()
+
+    def landed_all(count, of, recv):
+        size = count * math.prod(of.shape) * jnp.dtype(of.dtype).itemsize
+        landed(ruler.at[pl.ds(0, size // 256)], recv)
 
     def rows(start, size, step=16):
         return pl.ds(pl.multiple_of(start, step), size)
@@ -315,7 +337,7 @@
             for i in range(1, NE):
                 push(at, at, recv.at[i * N + j - 1], in_expert(i)[1])
             if to_mate is not None:
-                push(at, at, to_mate.at[j - 1], mate)
+                push(at, at, to_mate.at[0], mate)
 
     def spread_end(part, recv, to_mate):
         for i in range(1, NE):
@@ -323,13 +345,10 @@
                 at = part(shard_at(i, j))
                 landed(at, recv.at[i * N + j - 1])
                 if to_mate is not None:
-                    push(at, at, to_mate.at[i * N + j - 1], mate)
+                    push(at, at, to_mate.at[0], mate)
 
     def spread_wait(part, to_mate):
-        for i in range(NE):
-            for j in range(N):
-                if i or j:
-                    landed(part(shard_at(i, j)), to_mate.at[i * N + j - 1])
+        landed_all(G - 1, part(0), to_mate.at[0])
 
     def bias_part(g):
         return bias.at[g]
@@ -495,15 +514,13 @@
         there, _ = in_line(-j)
         at = wkv.at[c, rows(there * HP, HP)]
         landed(at, w_r.at[j - 1])
-        push(at, at, wm_r.at[j - 1], mate)
+        push(at, at, wm_r.at[0], mate)
     spread_on(q_part, q_r, qm_r)
     spread_on(bias_part, b_r, None)
     shards_start()
     spread_start(o_part, o_r)
 
-    for j in range(1, N):
-        there, _ = in_line(-j)
-        landed(wkv.at[1 - c, rows(there * HP, HP)], wm_r.at[j - 1])
+    landed_all(N - 1, wkv.at[0, pl.ds(0, HP)], wm_r.at[0])
     kn[...] = dot_nt(rw[...], wkv[0]).astype(BF16)
     kt[...] = dot_nt(wkv[0], rw[...]).astype(BF16)
     spread_end(q_part, q_r, qm_r)
@@ -564,9 +581,12 @@
         push(
             cot_ref.at[rows(there * T, T, 128)],
             cot.at[:, rows(n * CW, CW, 128)],
-            ct_r.at[j - 1],
+            ct_r.at[0],
             to,
         )
+    outer = jnp.logical_or(n >= 3, n + 3 < N)
+    inner = jnp.logical_not(outer)
+    either("on", inner, lambda: plane_on(3))
     spread_end(o_part, o_r, om_r)
 
     for part in range(N):
@@ -690,33 +710,35 @@
         core_start(j)
 
     def cotangent_wait():
+        landed_all(N - 1, cot.at[:, pl.ds(0, CW)], ct_r.at[0])
+
+    def last_forward():
+        forward(3)
+        delta[...] = acc[...].astype(BF16)
+        outd[n] = delta[:, rows(n * CW, CW, 128)]
         for j in range(1, N):
-            there, _ = in_line(-j)
-            landed(cot.at[:, rows(there * CW, CW, 128)], ct_r.at[j - 1])
+            there, to = in_line(j)
+            push(delta.at[:, rows(there * CW, CW, 128)], outd.at[n], od_r.at[0], to)
 
     forward(0)
     plane_turn(2)
     mate_on(1)
+    either("turn", inner, lambda: plane_turn(3))
+    forward(1)
     shards_on(3)
-    plane_on(3)
-    forward(1)
+    either("on", outer, lambda: plane_on(3))
     mate_on(2)
-    plane_turn(3)
-    forward(2)
+    either("turn", outer, lambda: plane_turn(3))
+    either("mate", inner, lambda: mate_on(3))
     cotangent_wait()
     backward(1)
+    either("mate", outer, lambda: mate_on(3))
+    forward(2)
+    plane_start(1)
     backward(2)
-    plane_start(1)
-    mate_on(3)
-    forward(3)
-    delta[...] = acc[...].astype(BF16)
-    outd[n] = delta[:, rows(n * CW, CW, 128)]
-    for j in range(1, N):
-        there, to = in_line(j)
-        push(delta.at[:, rows(there * CW, CW, 128)], outd.at[n], od_r.at[j - 1], to)
-
+    last_forward()
+    plane_start(2)
     backward(3)
-    plane_start(2)
     backward(0)
     plane_start(3)
     plane_middle(1)
@@ -857,12 +879,12 @@
     YW = D // NY
     ER = N * SH
     landed(cqo, qc_r.at[0])
+    plane_middle(0)
     pqo[...] = (gqo[c].astype(F32) + cqo[...].astype(F32)).astype(BF16)
     for i in range(1, NP):
         there, to = in_plane(i)
         src = pqo.at[rows(rem(there, NE) * ER, ER), rows(lax.div(there, NE) * YW, YW, 128)]
-        push(src, rqo.at[i], qp_r.at[0, i - 1], to)
-    plane_middle(0)
+        push(src, rqo.at[i], qp_r.at[0], to)
     line_start(2)
     line_start(3)
 
@@ -910,7 +932,7 @@
     psp[...] = sp[:, mine_cols] + csp[...]
     for i in range(1, NP):
         _, to = in_plane(i)
-        push(psp, rsp.at[i], qp_r.at[1, i - 1], to)
+        push(psp, rsp.at[i], qp_r.at[1], to)
 
     line_start(0)
 
@@ -926,16 +948,10 @@
     def fin_right(buffer, core, ys, es):
         return buffer.at[rows(core * HR + (ys * NE + es) * HS, HS), right]
 
-    def fin_to_mate(i, ys, es):
-        for part, piece in enumerate((fin_left, fin_right)):
-            sem = 2 * NP - 2 + 2 * i + part
+    def fin_to_mate(ys, es):
+        for piece in (fin_left, fin_right):
             at = piece(fin, c, ys, es)
-            push(at, at, ga_r.at[sem], mate)
-
-    def fin_from_mate(i, ys, es):
-        for part, piece in enumerate((fin_left, fin_right)):
-            sem = 2 * NP - 2 + 2 * i + part
-            landed(piece(fin, 1 - c, ys, es), ga_r.at[sem])
+            push(at, at, ga_r.at[2 * NP - 2], mate)
 
     fin[rows(c * HR + (e * NY + y) * HS, HS), left] = whole[:, 0:half].astype(BF16)
     fin[rows(c * HR + (y * NE + e) * HS, HS), right] = whole[:, half:].astype(BF16)
@@ -945,29 +961,27 @@
         push(at, at, ga_r.at[i - 1], to)
         at = fin_right(fin, c, y, e)
         push(at, at, ga_r.at[NP - 2 + i], to)
-    fin_to_mate(0, y, e)
+    fin_to_mate(y, e)
 
     whole = pqo[rows(e * ER, ER), rows(y * YW, YW, 128)].astype(F32)
+    landed_all(NP - 1, rqo.at[0], qp_r.at[0])
     for i in range(1, NP):
-        landed(rqo.at[i], qp_r.at[0, i - 1])
         whole = whole + rqo[i].astype(F32)
     zqo[...] = whole.astype(BF16)
     for j in range(1, N):
         there, to = in_line(j)
-        push(zqo.at[rows(there * SH, SH)], yqo.at[j], qz_r.at[0, j - 1], to)
+        push(zqo.at[rows(there * SH, SH)], yqo.at[j], qz_r.at[0], to)
     whole = psp[...]
+    landed_all(NP - 1, rsp.at[0], qp_r.at[1])
     for i in range(1, NP):
-        landed(rsp.at[i], qp_r.at[1, i - 1])
         whole = whole + rsp[i]
     zsp[...] = whole
     for j in range(1, N):
         _, to = in_line(j)
-        push(zsp, ysp.at[j], qz_r.at[1, j - 1], to)
+        push(zsp, ysp.at[j], qz_r.at[1], to)
 
     cols_copy.wait()
-    for j in range(1, N):
-        there, _ = in_line(-j)
-        landed(outd.at[there], od_r.at[j - 1])
+    landed_all(N - 1, outd.at[0], od_r.at[0])
     for j in range(N):
         at = pl.ds(j * T, T)
         out_ref[at, :] = out_ref[at, :] + outd[j].astype(F32)
@@ -975,43 +989,38 @@
     out_copy.start()
 
     whole = zqo[rows(n * SH, SH), :].astype(F32)
+    landed_all(N - 1, yqo.at[0], qz_r.at[0])
     for j in range(1, N):
-        landed(yqo.at[j], qz_r.at[0, j - 1])
         whole = whole + yqo[j].astype(F32)
     my_cols = rows(y * YW, YW, 128)
     fqo[c, :, my_cols] = whole.astype(BF16)
     at = fqo.at[c, :, my_cols]
     others = [(i, other) for i in range(NY) for other in range(2) if i or other]
-    for k, (i, other) in enumerate(others):
+    for i, other in others:
         to = (2 * in_rows(i)[0] + (1 - c if other else c), e, n)
-        push(at, at, qa_r.at[k], to)
+        push(at, at, qa_r.at[0], to)
     whole = zsp[...]
+    landed_all(N - 1, ysp.at[0], qz_r.at[1])
     for j in range(1, N):
-        landed(ysp.at[j], qz_r.at[1, j - 1])
         whole = whole + ysp[j]
     fsp[:, mine_cols] = whole
     at = fsp.at[:, mine_cols]
-    push(at, at, qa_r.at[2 * NY - 1], mate)
+    push(at, at, qa_r.at[1], mate)
     for i in range(1, NP):
         near, _ = in_plane(-i)
         ys, es = lax.div(near, NE), rem(near, NE)
         landed(fin_left(fin, c, ys, es), ga_r.at[i - 1])
         landed(fin_right(fin, c, ys, es), ga_r.at[NP - 2 + i])
-        fin_to_mate(i, ys, es)
+        fin_to_mate(ys, es)
     at = rows(c * HR, HR)
     g_ref[at, :] = fin[at, :].astype(F32)
-    landed(fsp.at[:, other_cols], qa_r.at[2 * NY - 1])
+    landed(fsp.at[:, other_cols], qa_r.at[1])
     small_ref[...] = fsp[...]
-    for k, (i, other) in enumerate(others):
-        near, _ = in_rows(-i)
-        at = fqo.at[1 - c if other else c, :, rows(near * YW, YW, 128)]
-        landed(at, qa_r.at[k])
+    landed_all(len(others), fqo.at[0, :, pl.ds(0, YW)], qa_r.at[0])
     fqo_ref[...] = fqo[...]
     ig_copy.wait()
     out_copy.wait()
-    for i in range(NP):
-        near, _ = in_plane(-i)
-        fin_from_mate(i, lax.div(near, NE), rem(near, NE))
+    landed(fin.at[rows((1 - c) * HR, HR)], ga_r.at[2 * NP - 2])
     at = rows((1 - c) * HR, HR)
     g_ref[at, :] = fin[at, :].astype(F32)
 
@@ -1130,25 +1139,25 @@
     ]
     pairs = [
         (N - 1,),
-        (N - 1,),
+        (1,),
         (G - 1,),
         (G - 1,),
+        (1,),
         (G - 1,),
-        (G - 1,),
-        (G - 1,),
+        (1,),
         (4, N - 1, max(NE, NY) - 1),
         (N - 1,),
-        (N - 1,),
-        (N - 1,),
+        (1,),
+        (1,),
         (max(S, 1),),
         (N,),
         (4, N, max(NE, NY) - 1),
         (N,),
-        (4 * NP - 2,),
+        (2 * NP - 1,),
         (2,),
-        (2, NP - 1),
-        (2, N - 1),
-        (2 * NY,),
+        (2,),
+        (2,),
+        (2,),
     ]
     HALO = 11
     sems = [pltpu.SemaphoreType.DMA((6,)), pltpu.SemaphoreType.DMA((GROUPS,))]

time: 86.9 us -> 85.5 us (0.984)
  Pallas kernels: 85.9 us -> 84.5 us
    pallas_call x1, Pallas kernels: 83.1 us -> 81.7 us  [run(): pl.pallas_call(functools.partial(kernel, z), out_shape=[pltpu.VMEM(s, t)...]
where the time goes in v6:
time: 85.5 us; the launch traced here: 85.3 us
  Pallas kernels  84.5 us (99%)
    pallas_call x1, Pallas kernels, run(): pl.pallas_call(functools.partial(kernel, z), out_shape=[pltpu.VMEM(s, t)...  81.7 us
    pallas_call x1, Pallas kernels, finish(): pl.pallas_call(functools.partial(finish_kernel, z), out_shape=[jax.ShapeD...  2.82 us

profile of v6, /device:TPU:0, one launch (start us, length us, event | category | flops | bytes accessed | tf_op | source)
XLA Modules:
  0.0 85.3 jit_solution(4293067009067624026)
XLA Ops:
  0.7 81.7 %layer.1 = (f32[2048,128]{1,0:T(8,128)S(1)}, f32[512,512]{1,0:T(8,128)S(1)}, f32[1024,512]{1,0:T(8,128)S(1)}, bf16[2,80,512]{2,1,0:T(8,128)(2,1)S(1)}, f32[24,512]{1,0:T(8,128)S(1)}) custom-call(f32[4096,512]{1,0:T(8,128)} %x_any.1, s32[4,1024]{1,0:T(4,128)} %seg_ref.1, s32[2,4096]{1,0:T(2,128)} %bitcast.35, f32[1,512]{1,0:T(1,128)} %bitcast.39, ...), custom_call_target="tpu_custom_call" | custom-call | tf_op jit(solution)/shard_map/layer/pallas_call | solution.py:1174
  82.4 2.8 %finish.1 = (f32[2048,128]{1,0:T(8,128)}, f32[512,512]{1,0:T(8,128)}, f32[1,512]{1,0:T(1,128)}, f32[1,512]{1,0:T(1,128)}, f32[64,512]{1,0:T(8,128)}, /*index=5*/...) custom-call(f32[2048,128]{1,0:T(8,128)S(1)} %get-tuple-element.43.ou, ...), custom_call_target="tpu_custom_call" | custom-call | tf_op jit(solution)/shard_map/finish/pallas_call | solution.py:1279

commit v7 on v6

--- a/solution.py
+++ b/solution.py
@@ -739,9 +739,9 @@
     last_forward()
     plane_start(2)
     backward(3)
+    plane_middle(1)
     backward(0)
     plane_start(3)
-    plane_middle(1)
 
     zero_row = jnp.zeros((1, D), F32)
 
@@ -813,8 +813,9 @@
                 dv[...] = dv[...] + value_part
 
     attend_back(0)
+    plane_middle(2)
+    line_start(1)
     attend_back(1)
-    plane_middle(2)
 
     H, PC = z.reach, z.piece
     offsets = [o for o in range(-H, H + 1) if o]
@@ -865,7 +866,6 @@
         gqo[1, g * SH + R : (g + 1) * SH, :] = value_w_grad[shared, :]
     push(gqo.at[1 - c], cqo, qc_r.at[0], mate)
     plane_middle(3)
-    line_start(1)
     ones = jnp.ones((8, T), BF16)
     sp[6:7, :] = dot_nt(ones, dqt[...])[0:1, :]
     sp[7:8, :] = jnp.zeros((1, D), F32)

time: 85.5 us -> 83.9 us (0.981)
  Pallas kernels: 84.5 us -> 82.9 us
    pallas_call x1, Pallas kernels: 81.7 us -> 80.1 us  [run(): pl.pallas_call(functools.partial(kernel, z), out_shape=[pltpu.VMEM(s, t)...]
where the time goes in v7:
time: 83.9 us; the launch traced here: 83.7 us
  Pallas kernels  82.9 us (99%)
    pallas_call x1, Pallas kernels, run(): pl.pallas_call(functools.partial(kernel, z), out_shape=[pltpu.VMEM(s, t)...  80.1 us
    pallas_call x1, Pallas kernels, finish(): pl.pallas_call(functools.partial(finish_kernel, z), out_shape=[jax.ShapeD...  2.82 us

profile of v7, /device:TPU:0, one launch (start us, length us, event | category | flops | bytes accessed | tf_op | source)
XLA Modules:
  0.0 83.7 jit_solution(12735047537921414308)
XLA Ops:
  0.7 80.1 %layer.1 = (f32[2048,128]{1,0:T(8,128)S(1)}, f32[512,512]{1,0:T(8,128)S(1)}, f32[1024,512]{1,0:T(8,128)S(1)}, bf16[2,80,512]{2,1,0:T(8,128)(2,1)S(1)}, f32[24,512]{1,0:T(8,128)S(1)}) custom-call(f32[4096,512]{1,0:T(8,128)} %x_any.1, s32[4,1024]{1,0:T(4,128)} %seg_ref.1, s32[2,4096]{1,0:T(2,128)} %bitcast.35, f32[1,512]{1,0:T(1,128)} %bitcast.39, ...), custom_call_target="tpu_custom_call" | custom-call | tf_op jit(solution)/shard_map/layer/pallas_call | solution.py:1174
  80.8 2.8 %finish.1 = (f32[2048,128]{1,0:T(8,128)}, f32[512,512]{1,0:T(8,128)}, f32[1,512]{1,0:T(1,128)}, f32[1,512]{1,0:T(1,128)}, f32[64,512]{1,0:T(8,128)}, /*index=5*/...) custom-call(f32[2048,128]{1,0:T(8,128)S(1)} %get-tuple-element.43.ou, ...), custom_call_target="tpu_custom_call" | custom-call | tf_op jit(solution)/shard_map/finish/pallas_call | solution.py:1279

commit v8 on v7

--- a/solution.py
+++ b/solution.py
@@ -816,6 +816,7 @@
     plane_middle(2)
     line_start(1)
     attend_back(1)
+    plane_middle(3)
 
     H, PC = z.reach, z.piece
     offsets = [o for o in range(-H, H + 1) if o]
@@ -865,7 +866,6 @@
         gqo[0, g * SH + R : (g + 1) * SH, :] = key_w_grad[shared, :]
         gqo[1, g * SH + R : (g + 1) * SH, :] = value_w_grad[shared, :]
     push(gqo.at[1 - c], cqo, qc_r.at[0], mate)
-    plane_middle(3)
     ones = jnp.ones((8, T), BF16)
     sp[6:7, :] = dot_nt(ones, dqt[...])[0:1, :]
     sp[7:8, :] = jnp.zeros((1, D), F32)

time: 83.9 us -> 83.9 us (level)
  no operation moved by 1% of the time
where the time goes in v8:
time: 83.9 us; the launch traced here: 83.7 us
  Pallas kernels  82.9 us (99%)
    pallas_call x1, Pallas kernels, run(): pl.pallas_call(functools.partial(kernel, z), out_shape=[pltpu.VMEM(s, t)...  80.1 us
    pallas_call x1, Pallas kernels, finish(): pl.pallas_call(functools.partial(finish_kernel, z), out_shape=[jax.ShapeD...  2.82 us

profile of v8, /device:TPU:0, one launch (start us, length us, event | category | flops | bytes accessed | tf_op | source)
XLA Modules:
  0.0 83.7 jit_solution(16698157460126671636)
XLA Ops:
  0.7 80.1 %layer.1 = (f32[2048,128]{1,0:T(8,128)S(1)}, f32[512,512]{1,0:T(8,128)S(1)}, f32[1024,512]{1,0:T(8,128)S(1)}, bf16[2,80,512]{2,1,0:T(8,128)(2,1)S(1)}, f32[24,512]{1,0:T(8,128)S(1)}) custom-call(f32[4096,512]{1,0:T(8,128)} %x_any.1, s32[4,1024]{1,0:T(4,128)} %seg_ref.1, s32[2,4096]{1,0:T(2,128)} %bitcast.35, f32[1,512]{1,0:T(1,128)} %bitcast.39, ...), custom_call_target="tpu_custom_call" | custom-call | tf_op jit(solution)/shard_map/layer/pallas_call | solution.py:1174
  80.8 2.8 %finish.1 = (f32[2048,128]{1,0:T(8,128)}, f32[512,512]{1,0:T(8,128)}, f32[1,512]{1,0:T(1,128)}, f32[1,512]{1,0:T(1,128)}, f32[64,512]{1,0:T(8,128)}, /*index=5*/...) custom-call(f32[2048,128]{1,0:T(8,128)S(1)} %get-tuple-element.43.ou, ...), custom_call_target="tpu_custom_call" | custom-call | tf_op jit(solution)/shard_map/finish/pallas_call | solution.py:1279
